TPU v7x, 32 devices: a whole 2x2x4 slice. The times are simulated.
32 devices in a mesh: day: 2 (over x), row: 16 (over z, y, core).
Axes of the slice: x: 2, y: 2, z: 4, core: 2. Of those that a mesh axis runs over, the one named last changes fastest.
Arguments:
- spectra: bfloat16 [4096, 2, 2, 4096], P(('day', 'row')), parts along dimension 0, may hold values from -110 to 110
- pair_channels: int32 [64, 128, 2], P('row'), may hold values from 0 to 2047, as said below
- pair_live: int32 [64, 128], P('row'), may hold values from 0 to 1, as said below
Outputs:
- correlations: float32 [128, 128, 512], P(('day', 'row')), parts along dimension 0
There are 2 independent parts, one for each index of `day`. A program takes and returns all parts, laid end to end along the dimension named above; an argument that names none is the same for every part. Nothing has to cross between parts.
Inputs may be any that keep to these rules, and one draw needn't show every extreme that they name: `pair_channels`: pair slots of device i of row are tiles i * 4 to (i + 1) * 4 - 1; their first channels are that device's own channels i * 128 to (i + 1) * 128 - 1, and their second channels lie within 128 channels of the first; distances of exactly 128 occur on both sides. `pair_live`: in each device's pair slots (tile by tile, pair by pair) the live slots come first and the padding after; every device has 128 live slots or more, and one device's slots are all live.
All inputs are finite; a program needn't handle non-finite values.
Results may differ from a plain program's by a relative error of at most 0.003.
Values may be sent and summed in bfloat16 or wider, within the bound.
No kernel may reach another device: no remote copies, remote signals or barrier semaphores. Data moves between devices by JAX's collectives and lax.ppermute only.
A program may use at most 192 MiB of HBM per device.

v0:
```python
import math

import jax
import jax.numpy as jnp
from jax import lax
from jax.sharding import PartitionSpec as P

WIN = 2
FREQ = 4096
BAND = 64
LAGS = 512
HALO = 128


def padded(block, sides, width):
    for axis, dim in sides:
        count = lax.axis_size(axis)
        forward = [(i, i + 1) for i in range(count - 1)]
        backward = [(target, source) for source, target in forward]
        low = lax.ppermute(
            lax.slice_in_dim(block, block.shape[dim] - width, None, axis=dim), axis, forward
        )
        high = lax.ppermute(lax.slice_in_dim(block, 0, width, axis=dim), axis, backward)
        block = jnp.concatenate([low, block, high], axis=dim)
    return block


def build_table(bin_total, lag_total):
    bin_index = jnp.arange(bin_total, dtype=jnp.int32)[:, None]
    shifts = jnp.arange(lag_total, dtype=jnp.int32)[None, :] - lag_total // 2
    phase_int = jnp.mod(bin_index * shifts, 2 * bin_total)
    angle_rad = phase_int.astype(jnp.float32) * (math.pi / bin_total)
    return jnp.concatenate([jnp.cos(angle_rad), -jnp.sin(angle_rad)], axis=0).astype(jnp.bfloat16)


def whiten(raw_rows, common):
    removed = raw_rows.astype(jnp.float32) - common[None]
    magnitude = jnp.sqrt(removed[:, :, 0] ** 2 + removed[:, :, 1] ** 2)
    row_count, window_count, bin_count = magnitude.shape
    banded = magnitude.reshape(row_count, window_count, bin_count // BAND, BAND)
    band_level = jnp.mean(banded, axis=3, keepdims=True) + 1e-06
    scaled = (
        removed.reshape(row_count, window_count, 2, bin_count // BAND, BAND)
        / band_level[:, :, None]
    )
    return scaled.reshape(raw_rows.shape).astype(jnp.bfloat16)


def cross_rows(first_rows, second_rows):
    first_f32 = first_rows.astype(jnp.float32)
    second_f32 = second_rows.astype(jnp.float32)
    real_part = jnp.sum(
        first_f32[:, :, 0] * second_f32[:, :, 0] + first_f32[:, :, 1] * second_f32[:, :, 1], axis=1
    )
    imag_part = jnp.sum(
        first_f32[:, :, 1] * second_f32[:, :, 0] - first_f32[:, :, 0] * second_f32[:, :, 1], axis=1
    )
    return jnp.concatenate([real_part, imag_part], axis=1).astype(jnp.bfloat16)


def body(spectra, pair_channels, pair_live):
    own_rows = spectra.shape[0]
    channels = own_rows * lax.axis_size("row")
    first_row = lax.axis_index("row") * own_rows - HALO
    local_sum = jnp.sum(spectra, axis=0, dtype=jnp.float32)
    common = lax.psum(local_sum, "row") / channels
    raw_band = padded(spectra, (("row", 0),), HALO)
    band_rows = whiten(raw_band, common)
    lag_matrix = build_table(FREQ, LAGS)
    norm_factor = 1.0 / math.sqrt(FREQ * WIN)
    tile_count = pair_channels.shape[0]
    tile_pairs = pair_channels.shape[1]
    group_count = tile_count // 4
    group_rows = 4 * tile_pairs
    pair_index = (pair_channels - first_row).reshape(group_count, group_rows, 2)
    weights = pair_live.astype(jnp.float32).reshape(group_count, group_rows)

    def correlate(index_rows, weight_rows):
        products = cross_rows(band_rows[index_rows[:, 0]], band_rows[index_rows[:, 1]])
        summed = jnp.dot(products, lag_matrix, preferred_element_type=jnp.float32)
        return summed * norm_factor * weight_rows[:, None]

    def one_group(operands):
        index_rows, weight_rows = operands
        outcome = correlate(index_rows, weight_rows)
        return outcome

    result = lax.map(one_group, (pair_index, weights))
    return result.reshape(tile_count, tile_pairs, LAGS)


def solution(mesh):
    placed = (P(("day", "row"), None, None, None), P("row", None, None), P("row", None))
    return jax.shard_map(
        body, mesh=mesh, in_specs=placed, out_specs=P(("day", "row"), None, None), check_vma=False
    )
```

profile of v0, /device:TPU:1, one launch (start us, length us, event | category | flops | bytes accessed | tf_op | source)
XLA Modules:
  0.0 472.7 jit_solution(6996535282205614045)
XLA Ops:
  6.5 0.0 copy-start.1
  6.5 0.0 copy-start.2
  6.5 0.0 all-reduce.2.cloned.1.call-start
  6.5 7.1 %copy.11 = bf16[128,2,2,4096]{3,0,2,1:T(8,128)(2,1)} copy(bf16[128,2,2,4096]{3,2,1,0:T(2,128)(2,1)} %param.3) | data formatting | bytes 8388608 | tf_op args[0]
  13.6 4.5 collective-permute-start
  18.2 1.9 collective-permute-start.1
  20.1 6.4 %convert_reduce_fusion = f32[2,2,4096]{2,1,0:T(2,128)} fusion(bf16[128,2,2,4096]{3,2,1,0:T(2,128)(2,1)} %param.3), kind=kLoop, calls=%fused_computation.27 | loop fusion | flops 4177920 | bytes 4259840 | tf_op jit(solution)/shard_map/reduce_sum | solution.py:65
  26.5 0.0 all-reduce.2.cloned.1.call-update
  26.5 0.0 copy-done.1
  26.6 0.0 copy-done.2
  26.6 35.2 %cosine_convert_fusion = (bf16[4096,512]{1,0:T(8,128)(2,1)}, bf16[4096,512]{1,0:T(8,128)(2,1)}) fusion(s32[512]{0:T(512)S(1)} %iota_add_fusion), kind=kLoop, calls=%fused_computation.24 | loop fusion | flops 35651584 | bytes 8390656 | tf_op jit(solution)/shard_map/convert
  61.8 61.6 %all-reduce.2.cloned.1.call-done = f32[2,2,4096]{2,1,0:T(2,128)} async-done(((f32[2,2,4096]{2,1,0:T(2,128)}), f32[2,2,4096]{2,1,0:T(2,128)}) %all-reduce.2.cloned.1.call-update) | async-done | bytes 65552 | tf_op jit(solution)/shard_map/psum | solution.py:66
  123.5 0.9 broadcast_multiply_fusion
  124.3 0.0 collective-permute-done
  124.3 0.0 collective-permute-done.1
  124.4 7.4 %convert_subtract_fusion = f32[384,2,2,4096]{3,0,2,1:T(8,128)S(1)} fusion(bf16[128,2,2,4096]{3,0,2,1:T(8,128)(2,1)} %collective-permute-done.1, bf16[128,2,2,4096]{3,0,2,1:T(8,128)(2,1)} %copy.11, bf16[128,2,2,4096]{3,0,2,1:T(8,128)(2,1)} %collective-permute-done, f32[2,2,4096]{2,1,0:T(2,128)S(1)} %broadcast_multiply_fusion), kind=kLoop, calls=%fused_computation.3 | loop fusion | flops 44040192 | bytes 37814272 | tf_op jit(solution)/shard_map/sub | solution.py:37
  131.8 6.7 %fusion.1 = f32[384,2,1,4096]{3,0,2,1:T(8,128)} fusion(f32[384,2,2,4096]{3,0,2,1:T(8,128)S(1)} %convert_subtract_fusion), kind=kLoop, calls=%fused_computation.8 | loop fusion | flops 9437184 | bytes 37748736 | tf_op jit(solution)/shard_map/sqrt | solution.py:38
  138.5 12.6 %copy.14 = f32[384,2,1,4096]{0,3,1,2:T(8,128)} copy(f32[384,2,1,4096]{3,0,2,1:T(8,128)} %fusion.1) | data formatting | bytes 25165824 | tf_op jit(solution)/shard_map/sqrt | solution.py:38
  151.1 6.4 %reduce_sum.39 = f32[384,2,64]{0,2,1:T(8,128)S(1)} reduce(f32[384,2,64,64]{0,3,2,1:T(8,128)} %bitcast.9, f32[]{:T(128)} %constant.25.clone.1), dimensions={3}, to_apply=%region_2.0 | reduce | flops 3096576 | bytes 12779524 | tf_op jit(solution)/shard_map/reduce_sum | solution.py:41
  157.6 5.3 %div.29 = f32[384,2,64,64]{0,3,2,1:T(8,128)} broadcast(f32[384,2,64]{0,2,1:T(8,128)S(1)} %multiply_add_fusion), dimensions={0,1,2} | broadcast | bytes 12779520 | tf_op jit(solution)/shard_map/div | solution.py:43
  162.8 12.6 %copy.15 = f32[384,2,4096]{2,0,1:T(8,128)} copy(f32[384,2,4096]{0,2,1:T(8,128)} %bitcast.10) | data formatting | bytes 25165824 | tf_op jit(solution)/shard_map/div | solution.py:43
  175.5 10.2 %divide_convert_fusion = bf16[384,2,2,4096]{3,0,2,1:T(8,128)(2,1)S(1)} fusion(f32[384,2,4096]{2,0,1:T(8,128)} %copy.15, f32[2,2,4096]{2,1,0:T(2,128)S(1)} %broadcast_multiply_fusion, bf16[128,2,2,4096]{3,0,2,1:T(8,128)(2,1)} %collective-permute-done.1, bf16[128,2,2,4096]{3,0,2,1:T(8,128)(2,1)} %copy.11, bf16[128,2,2,4096]{3,0,2,1:T(8,128)(2,1)} %collective-permute-done), kind=kLoop, calls=%fused_computation.2 | loop fusion | flops 56623104 | bytes 37814272 | tf_op jit(solution)/shard_map/convert_element_type | solution.py:46
  185.7 30.0 %copy.17 = bf16[384,2,2,4096]{3,2,1,0:T(2,128)(2,1)} copy(bf16[384,2,2,4096]{3,0,2,1:T(8,128)(2,1)S(1)} %divide_convert_fusion) | data formatting | bytes 25165824 | tf_op jit(solution)/shard_map/convert_element_type | solution.py:46
  215.6 47.0 %gather_fusion = bf16[512,2,2,4096]{3,2,1,0:T(2,128)(2,1)} fusion(bf16[384,2,2,4096]{3,2,1,0:T(2,128)(2,1)} %copy.17, s32[1024]{0:T(1024)S(1)} %pad_clamp_fusion.1), kind=kCustom, calls=%fused_computation | custom fusion | bytes 33556480 | tf_op jit(solution)/shard_map/while/body/eval_jaxpr/gather | solution.py:79
  262.6 17.6 %convert_element_type.33 = f32[512,2,2,4096]{3,2,1,0:T(2,128)} convert(bf16[512,2,2,4096]{3,2,1,0:T(2,128)(2,1)} %gather_fusion) | non-fusion elementwise | flops 8388608 | bytes 50331648 | tf_op jit(solution)/shard_map/while/body/eval_jaxpr/convert_element_type | solution.py:50
  280.3 46.8 %gather_fusion.1 = bf16[512,2,2,4096]{3,2,1,0:T(2,128)(2,1)} fusion(bf16[384,2,2,4096]{3,2,1,0:T(2,128)(2,1)} %copy.17, s32[1024]{0:T(1024)S(1)} %pad_clamp_fusion), kind=kCustom, calls=%fused_computation.1 | custom fusion | bytes 33556480 | tf_op jit(solution)/shard_map/while/body/eval_jaxpr/gather | solution.py:79
  327.1 17.6 %convert_element_type.34 = f32[512,2,2,4096]{3,2,1,0:T(2,128)} convert(bf16[512,2,2,4096]{3,2,1,0:T(2,128)(2,1)} %gather_fusion.1) | non-fusion elementwise | flops 8388608 | bytes 50331648 | tf_op jit(solution)/shard_map/while/body/eval_jaxpr/convert_element_type | solution.py:51
  344.6 0.0 copy-start
  344.6 113.5 %add_reduce_fusion = (bf16[512,4096]{1,0:T(8,128)(2,1)S(1)}, bf16[512,4096]{1,0:T(8,128)(2,1)S(1)}) fusion(f32[512,2,2,4096]{3,2,1,0:T(2,128)} %convert_element_type.34, f32[512,2,2,4096]{3,2,1,0:T(2,128)} %convert_element_type.33), kind=kLoop, calls=%fused_computation.5 | loop fusion | flops 29360128 | bytes 75497472 | tf_op jit(solution)/shard_map/while/body/eval_jaxpr/reduce_sum | solution.py:52
  458.2 0.0 copy-done
  458.2 7.6 %fusion.15 = f32[512,512]{1,0:T(8,128)} fusion(bf16[4096,512]{1,0:T(8,128)(2,1)} %get-tuple-element.28, bf16[4096,512]{1,0:T(8,128)(2,1)S(1)} %copy-done, bf16[512,4096]{1,0:T(8,128)(2,1)S(1)} %get-tuple-element.16, bf16[512,4096]{1,0:T(8,128)(2,1)S(1)} %get-tuple-element.15, f32[512]{0:T(512)S(1)} %multiply_bitcast_fusion), kind=kOutput, calls=%fused_computation.29 | convolution fusion | flops 4328783872 | bytes 17827840 | tf_op jit(solution)/shard_map/while/body/eval_jaxpr/dot_general | solution.py:80
  (7 shorter events, 0.1 us)
Async XLA Ops:
  6.5 20.0 %copy-start.1 = (s32[4,128,2]{1,2,0:T(2,128)S(1)}, s32[4,128,2]{1,2,0:T(2,128)}, u32[]{:S(2)}) copy-start(s32[4,128,2]{1,2,0:T(2,128)} %param.4) | copy-start | bytes 12292
  6.5 20.0 %copy-start.2 = (s32[4,128]{1,0:T(4,128)S(1)}, s32[4,128]{1,0:T(4,128)}, u32[]{:S(2)}) copy-start(s32[4,128]{1,0:T(4,128)} %param.5) | copy-start | bytes 6148
  6.5 116.9 %all-reduce.2.cloned.1.call-start = ((), (), s32[]{:S(2)}) async-start(), calls=%async_computation | async-start | bytes 131072 | tf_op jit(solution)/shard_map/psum | solution.py:66
  13.6 110.7 %collective-permute-start = (bf16[128,2,2,4096]{3,0,2,1:T(8,128)(2,1)}, bf16[128,2,2,4096]{3,0,2,1:T(8,128)(2,1)}, u32[]{:S(2)}, u32[]{:S(2)}) collective-permute-start(bf16[128,2,2,4096]{3,0,2,1:T(8,128)(2,1)} %copy.11), channel_id=1, source_target_pairs={{0,1},{1,2},{2,3},{3,4},{4,5},{5,6},{6,7},{7,8},{8,9},{9,10},{10,1... | collective-permute-start | bytes 12582920 | tf_op jit(solution)/shard_map/ppermute | solution.py:20
  18.2 106.2 %collective-permute-start.1 = (bf16[128,2,2,4096]{3,0,2,1:T(8,128)(2,1)}, bf16[128,2,2,4096]{3,0,2,1:T(8,128)(2,1)}, u32[]{:S(2)}, u32[]{:S(2)}) collective-permute-start(bf16[128,2,2,4096]{3,0,2,1:T(8,128)(2,1)} %copy.11), channel_id=1, source_target_pairs={{1,0},{2,1},{3,2},{4,3},{5,4},{6,5},{7,6},{8,7},{9,8},{10,9},{11,1... | collective-permute-start | bytes 12582920 | tf_op jit(solution)/shard_map/ppermute | solution.py:23
  344.6 113.5 %copy-start = (bf16[4096,512]{1,0:T(8,128)(2,1)S(1)}, bf16[4096,512]{1,0:T(8,128)(2,1)}, u32[]{:S(2)}) copy-start(bf16[4096,512]{1,0:T(8,128)(2,1)} %get-tuple-element.26) | copy-start | bytes 12582916
Sparse Core Ops, SparseCore 0:
  26.6 96.7 all-reduce.1
where the time goes:
time: 475 us; the launch traced here: 473 us
  other arithmetic  222 us (47%)
  local copies, waits for them, and re-layouts  161 us (34%)
  waiting for transfers between devices  61.7 us (13%)
  between operations  13.5 us (3%)
  matrix products  7.64 us (2%)
  starting transfers between devices  6.45 us (1%)
    reduce_sum x1, other arithmetic, cross_rows(): jnp.sum(first_f32[:, :, 0] * second_f32[:, :, 0] + first_f32[:, :, 1] * s...  114 us
    psum x1, waiting for transfers between devices, body(): common = lax.psum(local_sum, 'row') / channels  61.6 us
    gather x1, local copies, waits for them, and re-layouts, correlate(): band_rows[index_rows[:, 0]]  47 us
    gather x1, local copies, waits for them, and re-layouts, correlate(): band_rows[index_rows[:, 1]]  46.8 us
    another operation x1, other arithmetic  35.2 us
    convert_element_type x1, local copies, waits for them, and re-layouts, whiten(): return scaled.reshape(raw_rows.shape).astype(jnp.bfloat16)  30 us
    div x2, local copies, waits for them, and re-layouts, whiten(): removed.reshape(row_count, window_count, 2, bin_count // BAND, BAND)  17.9 us
    convert_element_type x1, other arithmetic, cross_rows(): first_f32 = first_rows.astype(jnp.float32)  17.6 us
  transfers between devices with their start and end apart: 3, of which 1 were waited for; matrix products, arithmetic and copies ran while one was open for 9% of the time, Pallas kernels for 0%

commit v1 on v0

v1 whole, which is shorter than its diff:
```python
import functools
import math

import jax
import jax.numpy as jnp
import numpy as np
from jax import lax
from jax.experimental import pallas as pl
from jax.experimental.pallas import tpu as pltpu
from jax.sharding import PartitionSpec as P

BAND = 64
LAGS = 512
STEP = 512
GROUP = 256
BLOCK1 = 256
BLOCK2 = 128
SLOW_CHUNKS = 2
VMEM_BYTES = 48 * 1024 * 1024
F32 = jnp.float32
BF16 = jnp.bfloat16


def lag_table(bins, lags):
    shifts = np.arange(lags, dtype=np.int64)[None, :] - lags // 2
    phase = np.mod(np.arange(bins, dtype=np.int64)[:, None] * shifts, 2 * bins)
    angle = (phase.astype(np.float32) * np.float32(math.pi / bins)).astype(np.float64)
    both = np.stack([np.cos(angle), -np.sin(angle)]).astype(np.float32)
    return both.astype(jnp.bfloat16)


def band_mean():
    rows = np.arange(GROUP)[:, None] // BAND
    cols = np.arange(GROUP)[None, :] // BAND
    return np.where(rows == cols, 1.0 / BAND, 0.0).astype(jnp.bfloat16)


def dot(a, b):
    return jnp.dot(a, b, preferred_element_type=F32)


def whiten_into(w_ref, row0, raws, commons, mean_ref):
    windows = len(raws)
    rows, bins = raws[0][0].shape
    for w in range(windows):
        for g in range(bins // GROUP):
            cols = pl.ds(g * GROUP, GROUP)
            re = raws[w][0][:, cols].astype(F32) - commons[w][0][:, cols]
            im = raws[w][1][:, cols].astype(F32) - commons[w][1][:, cols]
            magnitude = jnp.sqrt(re * re + im * im)
            high = magnitude.astype(BF16)
            low = (magnitude - high.astype(F32)).astype(BF16)
            level = dot(high, mean_ref[...]) + dot(low, mean_ref[...]) + 1e-06
            scale = 1.0 / level
            target = pl.ds(row0, rows)
            w_ref[target, pl.ds((2 * w) * bins + g * GROUP, GROUP)] = (re * scale).astype(BF16)
            w_ref[target, pl.ds((2 * w + 1) * bins + g * GROUP, GROUP)] = (im * scale).astype(BF16)


def one_hot(index_ref, hot_ref):
    slots, rows = hot_ref.shape
    lane = lax.broadcasted_iota(jnp.int32, (slots, rows), 1)
    hot_ref[...] = jnp.where(index_ref[...] == lane, 1.0, 0.0).astype(BF16)


def correlate_block(hot_a, hot_b, w_ref, table_ref, windows, start, size):
    bins = w_ref.shape[1] // (2 * windows)
    rows = pl.ds(start, size)
    a = dot(hot_a[rows, :], w_ref[...])
    b = dot(hot_b[rows, :], w_ref[...])
    real = imag = None
    for w in range(windows):
        ar, ai = (a[:, (2 * w + r) * bins : (2 * w + r + 1) * bins] for r in range(2))
        br, bi = (b[:, (2 * w + r) * bins : (2 * w + r + 1) * bins] for r in range(2))
        re = ar * br + ai * bi
        im = ai * br - ar * bi
        real = re if real is None else real + re
        imag = im if imag is None else imag + im
    return dot(real.astype(BF16), table_ref[0]) + dot(imag.astype(BF16), table_ref[1])


def near_kernel(windows, live_ref, *refs):
    parts = 2 * windows
    own = refs[:parts]
    other = refs[parts : 2 * parts]
    common = refs[2 * parts : 3 * parts]
    table_ref, mean_ref, ia_ref, ib_ref = refs[3 * parts : 3 * parts + 4]
    acc_ref = refs[3 * parts + 4]
    white = refs[3 * parts + 5 : 4 * parts + 5]
    w_ref, hot_a, hot_b = refs[4 * parts + 5 :]
    step = pl.program_id(0)

    @pl.when(step == 0)
    def _():
        acc_ref[...] = jnp.zeros_like(acc_ref)
        one_hot(ia_ref, hot_a)
        one_hot(ib_ref, hot_b)

    pairs = [common[2 * w : 2 * w + 2] for w in range(windows)]
    rows = own[0].shape[0]
    bins = own[0].shape[1]
    whiten_into(w_ref, 0, [own[2 * w : 2 * w + 2] for w in range(windows)], pairs, mean_ref)
    whiten_into(w_ref, rows, [other[2 * w : 2 * w + 2] for w in range(windows)], pairs, mean_ref)
    for part in range(parts):
        white[part][...] = w_ref[pl.ds(0, rows), pl.ds(part * bins, bins)]
    for block in range(hot_a.shape[0] // BLOCK1):

        @pl.when(block * BLOCK1 < live_ref[0])
        def _():
            acc_ref[pl.ds(block * BLOCK1, BLOCK1), :] += correlate_block(
                hot_a, hot_b, w_ref, table_ref, windows, block * BLOCK1, BLOCK1
            )


def far_kernel(windows, first, info_ref, *refs):
    parts = 2 * windows
    white = refs[:parts]
    other = refs[parts : 2 * parts]
    common = refs[2 * parts : 3 * parts]
    table_ref, mean_ref, ia_ref, ib_ref = refs[3 * parts : 3 * parts + 4]
    rest = refs[3 * parts + 4 :]
    if first:
        acc_ref, w_ref, hot_a, hot_b = rest
    else:
        before_ref, acc_ref, w_ref, hot_a, hot_b = rest
    step = pl.program_id(0)

    @pl.when(step == 0)
    def _():
        acc_ref[...] = jnp.zeros_like(acc_ref) if first else before_ref[...]
        one_hot(ia_ref, hot_a)
        one_hot(ib_ref, hot_b)

    pairs = [common[2 * w : 2 * w + 2] for w in range(windows)]
    rows, bins = other[0].shape
    for part in range(parts):
        w_ref[pl.ds(0, rows), pl.ds(part * bins, bins)] = white[part][...]
    whiten_into(w_ref, rows, [other[2 * w : 2 * w + 2] for w in range(windows)], pairs, mean_ref)
    slots = hot_a.shape[0]
    for block in range(slots // BLOCK2):
        inside = block * BLOCK2 % (slots // 2)

        @pl.when(inside < info_ref[1 + block * BLOCK2 // (slots // 2)])
        def _():
            acc_ref[pl.ds(block * BLOCK2, BLOCK2), :] += correlate_block(
                hot_a, hot_b, w_ref, table_ref, windows, block * BLOCK2, BLOCK2
            )


def sum_kernel(x_ref, o_ref):
    ones = jnp.ones((8, x_ref.shape[0]), BF16)
    o_ref[...] = dot(ones, x_ref[...])[0:1]


def merge_kernel(scale, near_ref, far_ref, back_ref, position_ref, live_ref, o_ref):
    slots = near_ref.shape[0]
    lane = lax.broadcasted_iota(jnp.int32, (slots, slots), 1)
    spread = jnp.where(position_ref[...] == lane, 1.0, 0.0).astype(BF16)
    far = far_ref[...]
    high = far.astype(BF16)
    low = (far - high.astype(F32)).astype(BF16)
    total = near_ref[...] + (dot(spread, high) + dot(spread, low) + dot(spread, back_ref[...]))
    o_ref[...] = total * scale * live_ref[...]


def params(cost_flops, cost_bytes):
    return dict(
        compiler_params=pltpu.CompilerParams(vmem_limit_bytes=VMEM_BYTES),
        cost_estimate=pl.CostEstimate(
            flops=cost_flops, bytes_accessed=cost_bytes, transcendentals=0
        ),
    )


def compact(crossing, row_a, row_b):
    slots = crossing.shape[0]
    order = jnp.arange(slots, dtype=jnp.int32)
    flag = crossing.astype(jnp.int32)
    ahead = jnp.sum(jnp.where(order[None, :] < order[:, None], flag[None, :], 0), axis=1)
    place = jnp.where(crossing, ahead, -1)
    match = place[None, :] == order[:, None]
    a = jnp.sum(jnp.where(match, row_a[None, :] + 1, 0), axis=1) - 1
    b = jnp.sum(jnp.where(match, row_b[None, :] + 1, 0), axis=1) - 1
    return a, b, place, jnp.sum(flag)


def body(spectra, pair_channels, pair_live):
    rows, windows, _, bins = spectra.shape
    parts = 2 * windows
    count = lax.axis_size("row")
    me = lax.axis_index("row")
    odd = me % 2
    first_row = me * rows
    half = bins // 2
    fast = [(i, i ^ 1) for i in range(count)]
    slow = [(i, i + 1) for i in range(1, count - 1, 2)]
    slow = slow + [(b, a) for a, b in slow]

    chunk = half // SLOW_CHUNKS
    send_start = (1 - odd) * half
    sent = [
        lax.dynamic_slice_in_dim(spectra, send_start + c * chunk, chunk, axis=3).reshape(
            rows, parts * chunk
        )
        for c in range(SLOW_CHUNKS)
    ]
    far_rows = [lax.ppermute(part, "row", slow) for part in sent]

    flat = spectra.reshape(rows, parts * bins)
    partner_rows = lax.ppermute(flat, "row", fast)

    wide = parts * bins // 8
    total = pl.pallas_call(
        sum_kernel,
        grid=(8,),
        in_specs=[pl.BlockSpec((rows, wide), lambda j: (0, j))],
        out_specs=pl.BlockSpec((1, wide), lambda j: (0, j)),
        out_shape=jax.ShapeDtypeStruct((1, parts * bins), F32),
        name="local_sum",
        **params(2 * rows * parts * bins, 2 * rows * parts * bins),
    )(flat)
    if count & (count - 1):
        total = lax.psum(total, "row")
    else:
        jump = 1
        while jump < count:
            total = total + lax.ppermute(total, "row", [(i, i ^ jump) for i in range(count)])
            jump *= 2
    common = total / (rows * count)

    slots = pair_channels.shape[0] * pair_channels.shape[1]
    pairs = pair_channels.reshape(slots, 2)
    live = pair_live.reshape(slots)
    listed = jnp.concatenate([pairs, live[:, None]], axis=1)
    far_listed = lax.ppermute(listed, "row", slow)
    order = jnp.arange(slots, dtype=jnp.int32)
    live_end = jnp.max(jnp.where(live != 0, order + 1, 0))
    near_shift = jnp.where(odd == 1, -rows, rows)
    far_shift = -near_shift
    row_a = pairs[:, 0] - first_row
    offset = pairs[:, 1] - first_row
    in_own = (offset >= 0) & (offset < rows)
    in_near = (offset >= near_shift) & (offset < near_shift + rows)
    in_far = (offset >= far_shift) & (offset < far_shift + rows)
    near_b = jnp.where(in_own, offset, jnp.where(in_near, offset - near_shift + rows, -1))
    own_a, own_b, place, own_count = compact(
        in_far & (live != 0), row_a, offset - far_shift + rows
    )
    far_a = far_listed[:, 0] - (first_row + far_shift) + rows
    far_b = far_listed[:, 1] - first_row
    their_a, their_b, _, their_count = compact(
        (far_b >= 0) & (far_b < rows) & (far_listed[:, 2] != 0), far_a, far_b
    )
    cross_a = jnp.concatenate([own_a, their_a])[:, None]
    cross_b = jnp.concatenate([own_b, their_b])[:, None]

    table = jnp.asarray(lag_table(bins, LAGS))
    mean = jnp.asarray(band_mean())
    steps = bins // STEP

    def whole(shape):
        return pl.BlockSpec(shape, lambda *_: (0,) * len(shape))

    near_acc, *white = pl.pallas_call(
        functools.partial(near_kernel, windows),
        grid_spec=pltpu.PrefetchScalarGridSpec(
            num_scalar_prefetch=1,
            grid=(steps,),
            in_specs=[
                pl.BlockSpec((n, STEP), functools.partial(lambda p, j, s: (0, p * steps + j), p))
                for n in (rows, rows, 1)
                for p in range(parts)
            ]
            + [
                pl.BlockSpec((2, STEP, LAGS), lambda j, s: (0, j, 0)),
                whole((GROUP, GROUP)),
                whole((slots, 1)),
                whole((slots, 1)),
            ],
            out_specs=[whole((slots, LAGS))]
            + [pl.BlockSpec((rows, STEP), lambda j, s: (0, j)) for _ in range(parts)],
            scratch_shapes=[
                pltpu.VMEM((2 * rows, parts * STEP), BF16),
                pltpu.VMEM((slots, 2 * rows), BF16),
                pltpu.VMEM((slots, 2 * rows), BF16),
            ],
        ),
        out_shape=[jax.ShapeDtypeStruct((slots, LAGS), F32)]
        + [jax.ShapeDtypeStruct((rows, bins), BF16) for _ in range(parts)],
        name="near_pairs",
        **params(20 * 10**9, 20 * 10**6),
    )(
        live_end[None],
        *[flat] * parts,
        *[partner_rows] * parts,
        *[common] * parts,
        table,
        mean,
        row_a[:, None],
        near_b[:, None],
    )

    chunk_steps = chunk // STEP
    info = jnp.stack([odd * (half // STEP), own_count, their_count])
    far_acc = None
    for c in range(SLOW_CHUNKS):
        own_map = functools.partial(lambda c, j, s: (0, s[0] + c * chunk_steps + j), c)
        specs = (
            [pl.BlockSpec((rows, STEP), own_map) for _ in range(parts)]
            + [
                pl.BlockSpec(
                    (rows, STEP), functools.partial(lambda p, j, s: (0, p * chunk_steps + j), p)
                )
                for p in range(parts)
            ]
            + [
                pl.BlockSpec(
                    (1, STEP),
                    functools.partial(
                        lambda c, p, j, s: (0, p * steps + s[0] + c * chunk_steps + j), c, p
                    ),
                )
                for p in range(parts)
            ]
            + [
                pl.BlockSpec(
                    (2, STEP, LAGS),
                    functools.partial(lambda c, j, s: (0, s[0] + c * chunk_steps + j, 0), c),
                ),
                whole((GROUP, GROUP)),
                whole((2 * slots, 1)),
                whole((2 * slots, 1)),
            ]
        )
        operands = [
            info,
            *white,
            *[far_rows[c]] * parts,
            *[common] * parts,
            table,
            mean,
            cross_a,
            cross_b,
        ]
        if c:
            specs.append(whole((2 * slots, LAGS)))
            operands.append(far_acc)
        far_acc = pl.pallas_call(
            functools.partial(far_kernel, windows, c == 0),
            grid_spec=pltpu.PrefetchScalarGridSpec(
                num_scalar_prefetch=1,
                grid=(chunk_steps,),
                in_specs=specs,
                out_specs=whole((2 * slots, LAGS)),
                scratch_shapes=[
                    pltpu.VMEM((2 * rows, parts * STEP), BF16),
                    pltpu.VMEM((2 * slots, 2 * rows), BF16),
                    pltpu.VMEM((2 * slots, 2 * rows), BF16),
                ],
            ),
            out_shape=jax.ShapeDtypeStruct((2 * slots, LAGS), F32),
            name="far_pairs",
            **params(10 * 10**9 // SLOW_CHUNKS, 10 * 10**6 // SLOW_CHUNKS),
        )(*operands)

    back = lax.ppermute(far_acc[slots:].astype(BF16), "row", slow)
    result = pl.pallas_call(
        functools.partial(merge_kernel, 1.0 / math.sqrt(bins * windows)),
        grid=(1,),
        in_specs=[
            whole((slots, LAGS)),
            whole((slots, LAGS)),
            whole((slots, LAGS)),
            whole((slots, 1)),
            whole((slots, 1)),
        ],
        out_specs=whole((slots, LAGS)),
        out_shape=jax.ShapeDtypeStruct((slots, LAGS), F32),
        name="merge",
        **params(10**9, 4 * 10**6),
    )(near_acc, far_acc, back, place[:, None], live.astype(F32)[:, None])
    return result.reshape(pair_live.shape + (LAGS,))


def solution(mesh):
    placed = (P(("day", "row"), None, None, None), P("row", None, None), P("row", None))
    return jax.shard_map(
        body, mesh=mesh, in_specs=placed, out_specs=P(("day", "row"), None, None), check_vma=False
    )
```

time: 475 us -> 152 us (0.32)
  the two profiles are of different devices: /device:TPU:1 before, /device:TPU:9 now
where the time goes in v1:
time: 152 us; the launch traced here: 149 us
  waiting for transfers between devices  53.6 us (35%)
  Pallas kernels  51.6 us (34%)
  local copies, waits for them, and re-layouts  21 us (14%)
  starting transfers between devices  15.4 us (10%)
  other arithmetic  6.87 us (5%)
    ppermute x4, waiting for transfers between devices, body(): lax.ppermute(total, 'row', [(i, i ^ jump) for i in range(count)])  39.6 us
    pallas_call x1, Pallas kernels, body(): pl.pallas_call(functools.partial(near_kernel, windows), grid_spec=pltpu.P...  30.4 us
    pallas_call x2, Pallas kernels, body(): pl.pallas_call(functools.partial(far_kernel, windows, c == 0), grid_spec=...  17.4 us
    ppermute x1, waiting for transfers between devices, body(): back = lax.ppermute(far_acc[slots:].astype(BF16), 'row', slow)  14 us
    reshape x1, local copies, waits for them, and re-layouts, body(): flat = spectra.reshape(rows, parts * bins)  7.82 us
    ppermute x2, starting transfers between devices, body(): far_rows = [lax.ppermute(part, 'row', slow) for part in sent]  5.54 us
    unnamed x15, local copies, waits for them, and re-layouts  3.95 us
    ppermute x4, starting transfers between devices, body(): lax.ppermute(total, 'row', [(i, i ^ jump) for i in range(count)])  3.77 us
  transfers between devices with their start and end apart: 9, of which 4 were waited for; matrix products, arithmetic and copies ran while one was open for 10% of the time, Pallas kernels for 27%

profile of v1, /device:TPU:9, one launch (start us, length us, event | category | flops | bytes accessed | tf_op | source)
XLA Modules:
  0.0 148.8 jit_solution(16126972016387571639)
XLA Ops:
  0.0 7.8 %reshape.144.x_ref.refs_0_.refs_1_.refs_2_.refs_3_ = bf16[128,16384]{1,0:T(8,128)(2,1)} reshape(bf16[128,2,2,4096]{3,2,1,0:T(2,128)(2,1)} %param.5) | data formatting | bytes 8388608 | tf_op jit(solution)/shard_map/reshape | solution.py:209
  7.8 0.7 collective-permute-start
  8.5 2.2 %copy-done = bf16[128,16384]{1,0:T(8,128)(2,1)S(1)} copy-done((bf16[128,16384]{1,0:T(8,128)(2,1)S(1)}, bf16[128,16384]{1,0:T(8,128)(2,1)}, u32[]{:S(2)}) %copy-start) | copy-done | bytes 4194328
  10.7 1.8 %local_sum.1 = f32[1,16384]{1,0:T(1,128)S(1)} custom-call(bf16[128,16384]{1,0:T(8,128)(2,1)S(1)} %copy-done), custom_call_target="tpu_custom_call" | custom-call | flops 4194304 | bytes 4194304 | tf_op jit(solution)/shard_map/local_sum/pallas_call | solution.py:213
  12.9 0.8 pad_add_fusion
  13.7 3.5 %collective-permute-start.5 = (s32[512,3]{1,0:T(8,128)}, s32[512,3]{1,0:T(8,128)S(1)}, u32[]{:S(2)}, u32[]{:S(2)}) collective-permute-start(s32[512,3]{1,0:T(8,128)} %pad_add_fusion), channel_id=1, source_target_pairs={{1,2},{3,4},{5,6},{7,8},{9,10},{11,12},{13,14},{2,1},{4,3},{6,5},{... | collective-permute-start | bytes 18440 | tf_op jit(solution)/shard_map/ppermute | solution.py:235
  17.3 3.0 %constant_dynamic-slice_fusion = (bf16[128,2,2,1024]{3,2,1,0:T(2,128)(2,1)S(1)}, bf16[128,2,2,1024]{3,2,1,0:T(2,128)(2,1)S(1)}) fusion(bf16[128,2,2,4096]{3,2,1,0:T(2,128)(2,1)} %param.5, s32[]{:T(128)S(6)} %select_n.81, s32[]{:T(128)S(6)} %select_n.72), kind=kLoop, calls=%fused_computation.41 | loop fusion | bytes 4194312 | tf_op jit(solution)/shard_map/dynamic_slice | solution.py:202
  20.3 1.6 %reshape.147 = bf16[128,4096]{1,0:T(8,128)(2,1)} reshape(bf16[128,2,2,1024]{3,2,1,0:T(2,128)(2,1)S(1)} %get-tuple-element.27) | data formatting | bytes 2097152 | tf_op jit(solution)/shard_map/reshape | solution.py:202
  21.9 2.0 %collective-permute-start.7 = (bf16[128,4096]{1,0:T(8,128)(2,1)}, bf16[128,4096]{1,0:T(8,128)(2,1)}, u32[]{:S(2)}, u32[]{:S(2)}) collective-permute-start(bf16[128,4096]{1,0:T(8,128)(2,1)} %reshape.147), channel_id=1, source_target_pairs={{1,2},{3,4},{5,6},{7,8},{9,10},{11,12},{13,14},{2,1},{4,3},{6,5},{... | collective-permute-start | bytes 3145736 | tf_op jit(solution)/shard_map/ppermute | solution.py:207
  24.0 1.6 %reshape.146 = bf16[128,4096]{1,0:T(8,128)(2,1)} reshape(bf16[128,2,2,1024]{3,2,1,0:T(2,128)(2,1)S(1)} %get-tuple-element.28) | data formatting | bytes 2097152 | tf_op jit(solution)/shard_map/reshape | solution.py:202
  25.6 3.5 %collective-permute-start.6 = (bf16[128,4096]{1,0:T(8,128)(2,1)}, bf16[128,4096]{1,0:T(8,128)(2,1)}, u32[]{:S(2)}, u32[]{:S(2)}) collective-permute-start(bf16[128,4096]{1,0:T(8,128)(2,1)} %reshape.146), channel_id=1, source_target_pairs={{1,2},{3,4},{5,6},{7,8},{9,10},{11,12},{13,14},{2,1},{4,3},{6,5},{... | collective-permute-start | bytes 3145736 | tf_op jit(solution)/shard_map/ppermute | solution.py:207
  29.1 0.3 add_reduce_fusion.1
  29.9 0.7 broadcast_select_fusion.1
  30.6 0.4 select_reduce_fusion.1
  30.9 0.7 select_reduce_fusion.6
  31.6 0.3 fusion.3
  32.1 0.7 broadcast_select_fusion
  33.1 0.4 select_reduce_fusion
  33.6 2.2 %collective-permute-start.2 = (f32[1,16384]{1,0:T(1,128)S(1)}, f32[1,16384]{1,0:T(1,128)S(1)}, u32[]{:S(2)}, u32[]{:S(2)}) collective-permute-start(f32[1,16384]{1,0:T(1,128)S(1)} %add.104), channel_id=1, source_target_pairs={{0,2},{1,3},{2,0},{3,1},{4,6},{5,7},{6,4},{7,5},{8,10},{9,11},{10,... | collective-permute-start | bytes 196616 | tf_op jit(solution)/shard_map/ppermute | solution.py:227
  36.0 35.0 %collective-permute-done.2 = f32[1,16384]{1,0:T(1,128)S(1)} collective-permute-done((f32[1,16384]{1,0:T(1,128)S(1)}, f32[1,16384]{1,0:T(1,128)S(1)}, u32[]{:S(2)}, u32[]{:S(2)}) %collective-permute-start.2) | collective-permute-done | bytes 65568 | tf_op jit(solution)/shard_map/ppermute | solution.py:227
  71.4 2.8 %collective-permute-done.3 = f32[1,16384]{1,0:T(1,128)S(1)} collective-permute-done((f32[1,16384]{1,0:T(1,128)S(1)}, f32[1,16384]{1,0:T(1,128)S(1)}, u32[]{:S(2)}, u32[]{:S(2)}) %collective-permute-start.3) | collective-permute-done | bytes 65568 | tf_op jit(solution)/shard_map/ppermute | solution.py:227
  74.3 1.4 collective-permute-start.4
  75.7 1.3 pad_add_fusion.3.info_ref
  77.0 1.8 %collective-permute-done.4 = f32[1,16384]{1,0:T(1,128)S(1)} collective-permute-done((f32[1,16384]{1,0:T(1,128)S(1)}, f32[1,16384]{1,0:T(1,128)S(1)}, u32[]{:S(2)}, u32[]{:S(2)}) %collective-permute-start.4) | collective-permute-done | bytes 65568 | tf_op jit(solution)/shard_map/ppermute | solution.py:227
  79.0 30.4 %near_pairs.1 = (f32[512,512]{1,0:T(8,128)S(1)}, bf16[128,4096]{1,0:T(8,128)(2,1)S(1)}, bf16[128,4096]{1,0:T(8,128)(2,1)S(1)}, bf16[128,4096]{1,0:T(8,128)(2,1)S(1)}, bf16[128,4096]{1,0:T(8,128)(2,1)S(1)}) custom-call(s32[1]{0:T(128)} %bitcast.live_ref, bf16[128,16384]{1,0:T(8,128)(2,1)} %reshape.144.x_ref.refs_0_.refs_1_.refs_2_.refs_3_, ...), custom_call_target="tpu_custom_call" | custom-call | flops 20000000000 | bytes 20000000 | tf_op jit(solution)/shard_map/near_pairs/pallas_call | solution.py:264
  109.4 8.3 %far_pairs.2.refs_16_ = f32[1024,512]{1,0:T(8,128)} custom-call(s32[3]{0:T(128)S(1)} %pad_add_fusion.3.info_ref, bf16[128,4096]{1,0:T(8,128)(2,1)S(1)} %get-tuple-element.11.refs_0_, bf16[128,4096]{1,0:T(8,128)(2,1)S(1)} %get-tuple-element.12.refs_1_, bf16[128,4096]{1,0:T(8,128)(2,1)S(1)} %get-tuple-element.13.refs_2_, ...), custom_call_target="tpu_custom_call" | custom-call | flops 5000000000 | bytes 5000000 | tf_op jit(solution)/shard_map/far_pairs/pallas_call | solution.py:348
  117.7 9.1 %far_pairs.3.far_ref = f32[1024,512]{1,0:T(8,128)} custom-call(s32[3]{0:T(128)S(1)} %pad_add_fusion.3.info_ref, bf16[128,4096]{1,0:T(8,128)(2,1)S(1)} %get-tuple-element.11.refs_0_, bf16[128,4096]{1,0:T(8,128)(2,1)S(1)} %get-tuple-element.12.refs_1_, bf16[128,4096]{1,0:T(8,128)(2,1)S(1)} %get-tuple-element.13.refs_2_, ...), custom_call_target="tpu_custom_call" | custom-call | flops 5000000000 | bytes 5000000 | tf_op jit(solution)/shard_map/far_pairs/pallas_call | solution.py:348
  126.8 2.1 %slice.55 = bf16[512,512]{1,0:T(8,128)(2,1)} slice(f32[1024,512]{1,0:T(8,128)} %far_pairs.3.far_ref), slice={[512:1024], [0:512]} | slice | bytes 1048576 | tf_op jit(solution)/shard_map/slice | solution.py:366
  128.9 1.9 %collective-permute-start.8 = (bf16[512,512]{1,0:T(8,128)(2,1)}, bf16[512,512]{1,0:T(8,128)(2,1)S(1)}, u32[]{:S(2)}, u32[]{:S(2)}) collective-permute-start(bf16[512,512]{1,0:T(8,128)(2,1)} %slice.55), channel_id=1, source_target_pairs={{1,2},{3,4},{5,6},{7,8},{9,10},{11,12},{13,14},{2,1},{4,3},{6,5},{... | collective-permute-start | bytes 1572872 | tf_op jit(solution)/shard_map/ppermute | solution.py:366
  131.2 14.0 %collective-permute-done.8.back_ref = bf16[512,512]{1,0:T(8,128)(2,1)S(1)} collective-permute-done((bf16[512,512]{1,0:T(8,128)(2,1)}, bf16[512,512]{1,0:T(8,128)(2,1)S(1)}, u32[]{:S(2)}, u32[]{:S(2)}) %collective-permute-start.8) | collective-permute-done | bytes 524320 | tf_op jit(solution)/shard_map/ppermute | solution.py:366
  145.2 1.6 %copy-done.1 = f32[1024,512]{1,0:T(8,128)S(1)} copy-done((f32[1024,512]{1,0:T(8,128)S(1)}, f32[1024,512]{1,0:T(8,128)}, u32[]{:S(2)}) %copy-start.1) | copy-done | bytes 2097176
  146.8 2.0 %merge.1 = f32[512,512]{1,0:T(8,128)} custom-call(f32[512,512]{1,0:T(8,128)S(1)} %get-tuple-element.10.near_ref, f32[1024,512]{1,0:T(8,128)S(1)} %copy-done.1, bf16[512,512]{1,0:T(8,128)(2,1)S(1)} %collective-permute-done.8.back_ref, s32[512,1]{1,0:T(8,128)S(1)} %and_select_fusion.position_ref, f32[512,1]{1,0:T(8,128)S(1)} %copy.43.live_ref), custom_call_target="tpu_custom_call" | custom-call | flops 1000000000 | bytes 4000000 | tf_op jit(solution)/shard_map/merge/pallas_call | solution.py:367
  (41 shorter events, 2.5 us)
Async XLA Ops:
  7.8 71.1 %collective-permute-start = (bf16[128,16384]{1,0:T(8,128)(2,1)}, bf16[128,16384]{1,0:T(8,128)(2,1)}, u32[]{:S(2)}, u32[]{:S(2)}) collective-permute-start(bf16[128,16384]{1,0:T(8,128)(2,1)} %reshape.144.x_ref.refs_0_.refs_1_.refs_2_.refs_3_), channel_id=1, source_target_pairs={{0,1},{1,0},{2,3},{3,2},{4,5},{5,4},{6,7},{7,6},{8,9},{9,8},{10,11... | collective-permute-start | bytes 12582920 | tf_op jit(solution)/shard_map/ppermute | solution.py:210
  8.5 2.2 %copy-start = (bf16[128,16384]{1,0:T(8,128)(2,1)S(1)}, bf16[128,16384]{1,0:T(8,128)(2,1)}, u32[]{:S(2)}) copy-start(bf16[128,16384]{1,0:T(8,128)(2,1)} %reshape.144.x_ref.refs_0_.refs_1_.refs_2_.refs_3_) | copy-start | bytes 12582916
  10.7 1.9 %copy-start.6 = (s32[4,128,2]{1,2,0:T(2,128)S(1)}, s32[4,128,2]{1,2,0:T(2,128)}, u32[]{:S(2)}) copy-start(s32[4,128,2]{1,2,0:T(2,128)} %param.6) | copy-start | bytes 12292
  10.7 2.1 %copy-start.5 = (s32[4,128]{1,0:T(4,128)S(1)}, s32[4,128]{1,0:T(4,128)}, u32[]{:S(2)}) copy-start(s32[4,128]{1,0:T(4,128)} %param.7) | copy-start | bytes 6148
  12.5 21.0 %collective-permute-start.1 = (f32[1,16384]{1,0:T(1,128)S(1)}, f32[1,16384]{1,0:T(1,128)S(1)}, u32[]{:S(2)}, u32[]{:S(2)}) collective-permute-start(f32[1,16384]{1,0:T(1,128)S(1)} %local_sum.1), channel_id=1, source_target_pairs={{0,1},{1,0},{2,3},{3,2},{4,5},{5,4},{6,7},{7,6},{8,9},{9,8},{10,11... | collective-permute-start | bytes 196616 | tf_op jit(solution)/shard_map/ppermute | solution.py:227
  12.9 12.7 %copy-start.3 = (s32[512,1]{1,0:T(8,128)}, s32[512,1]{1,0:T(8,128)S(1)}, u32[]{:S(2)}) copy-start(s32[512,1]{1,0:T(8,128)S(1)} %copy.36) | copy-start | bytes 6148
  13.7 17.9 %collective-permute-start.5 = (s32[512,3]{1,0:T(8,128)}, s32[512,3]{1,0:T(8,128)S(1)}, u32[]{:S(2)}, u32[]{:S(2)}) collective-permute-start(s32[512,3]{1,0:T(8,128)} %pad_add_fusion), channel_id=1, source_target_pairs={{1,2},{3,4},{5,6},{7,8},{9,10},{11,12},{13,14},{2,1},{4,3},{6,5},{... | collective-permute-start | bytes 18440 | tf_op jit(solution)/shard_map/ppermute | solution.py:235
  20.3 58.7 %copy-start.2 = (bf16[256,256]{1,0:T(8,128)(2,1)S(1)}, bf16[256,256]{1,0:T(8,128)(2,1)}, u32[]{:S(2)}) copy-start(bf16[256,256]{1,0:T(8,128)(2,1)} %constant.57.clone.refs_13_) | copy-start | bytes 393220
  21.9 87.5 %collective-permute-start.7 = (bf16[128,4096]{1,0:T(8,128)(2,1)}, bf16[128,4096]{1,0:T(8,128)(2,1)}, u32[]{:S(2)}, u32[]{:S(2)}) collective-permute-start(bf16[128,4096]{1,0:T(8,128)(2,1)} %reshape.147), channel_id=1, source_target_pairs={{1,2},{3,4},{5,6},{7,8},{9,10},{11,12},{13,14},{2,1},{4,3},{6,5},{... | collective-permute-start | bytes 3145736 | tf_op jit(solution)/shard_map/ppermute | solution.py:207
  25.6 92.1 %collective-permute-start.6 = (bf16[128,4096]{1,0:T(8,128)(2,1)}, bf16[128,4096]{1,0:T(8,128)(2,1)}, u32[]{:S(2)}, u32[]{:S(2)}) collective-permute-start(bf16[128,4096]{1,0:T(8,128)(2,1)} %reshape.146), channel_id=1, source_target_pairs={{1,2},{3,4},{5,6},{7,8},{9,10},{11,12},{13,14},{2,1},{4,3},{6,5},{... | collective-permute-start | bytes 3145736 | tf_op jit(solution)/shard_map/ppermute | solution.py:207
  33.6 37.4 %collective-permute-start.2 = (f32[1,16384]{1,0:T(1,128)S(1)}, f32[1,16384]{1,0:T(1,128)S(1)}, u32[]{:S(2)}, u32[]{:S(2)}) collective-permute-start(f32[1,16384]{1,0:T(1,128)S(1)} %add.104), channel_id=1, source_target_pairs={{0,2},{1,3},{2,0},{3,1},{4,6},{5,7},{6,4},{7,5},{8,10},{9,11},{10,... | collective-permute-start | bytes 196616 | tf_op jit(solution)/shard_map/ppermute | solution.py:227
  71.1 3.2 %collective-permute-start.3 = (f32[1,16384]{1,0:T(1,128)S(1)}, f32[1,16384]{1,0:T(1,128)S(1)}, u32[]{:S(2)}, u32[]{:S(2)}) collective-permute-start(f32[1,16384]{1,0:T(1,128)S(1)} %add.105), channel_id=1, source_target_pairs={{0,4},{1,5},{2,6},{3,7},{4,0},{5,1},{6,2},{7,3},{8,12},{9,13},{10,... | collective-permute-start | bytes 196616 | tf_op jit(solution)/shard_map/ppermute | solution.py:227
  74.3 4.5 %collective-permute-start.4 = (f32[1,16384]{1,0:T(1,128)S(1)}, f32[1,16384]{1,0:T(1,128)S(1)}, u32[]{:S(2)}, u32[]{:S(2)}) collective-permute-start(f32[1,16384]{1,0:T(1,128)S(1)} %add.106), channel_id=1, source_target_pairs={{0,8},{1,9},{2,10},{3,11},{4,12},{5,13},{6,14},{7,15},{8,0},{9,1},... | collective-permute-start | bytes 196616 | tf_op jit(solution)/shard_map/ppermute | solution.py:227
  117.6 13.5 %copy-start.4 = (s32[512,1]{1,0:T(8,128)S(1)}, s32[512,1]{1,0:T(8,128)}, u32[]{:S(2)}) copy-start(s32[512,1]{1,0:T(8,128)} %copy-done.3) | copy-start | bytes 6148
  128.9 16.3 %collective-permute-start.8 = (bf16[512,512]{1,0:T(8,128)(2,1)}, bf16[512,512]{1,0:T(8,128)(2,1)S(1)}, u32[]{:S(2)}, u32[]{:S(2)}) collective-permute-start(bf16[512,512]{1,0:T(8,128)(2,1)} %slice.55), channel_id=1, source_target_pairs={{1,2},{3,4},{5,6},{7,8},{9,10},{11,12},{13,14},{2,1},{4,3},{6,5},{... | collective-permute-start | bytes 1572872 | tf_op jit(solution)/shard_map/ppermute | solution.py:366
  145.2 1.6 %copy-start.1 = (f32[1024,512]{1,0:T(8,128)S(1)}, f32[1024,512]{1,0:T(8,128)}, u32[]{:S(2)}) copy-start(f32[1024,512]{1,0:T(8,128)} %far_pairs.3.far_ref) | copy-start | bytes 6291460

commit v2 on v0

v2 whole, which is shorter than its diff:
```python
import functools
import math

import jax
import jax.numpy as jnp
import numpy as np
from jax import lax
from jax.experimental import pallas as pl
from jax.experimental.pallas import tpu as pltpu
from jax.sharding import PartitionSpec as P

BAND = 64
LAGS = 512
GROUP = 256
NEAR_GROUPS = 4
FAR_BLOCK = 256
BACK_ROWS = 160
ROW_BLOCK = 16
TINY = 1e-37
VMEM_BYTES = 56 * 1024 * 1024
F32 = jnp.float32
BF16 = jnp.bfloat16


def lag_table(bins, lags):
    shifts = np.arange(lags, dtype=np.int64)[None, :] - lags // 2
    phase = np.mod(np.arange(bins, dtype=np.int64)[:, None] * shifts, 2 * bins)
    angle = (phase.astype(np.float32) * np.float32(math.pi / bins)).astype(np.float64)
    both = np.stack([np.cos(angle), -np.sin(angle)]).astype(np.float32)
    return both.astype(jnp.bfloat16)


def band_mean():
    rows = np.arange(GROUP)[:, None] // BAND
    cols = np.arange(GROUP)[None, :] // BAND
    return np.where(rows == cols, 1.0 / BAND, 0.0).astype(jnp.bfloat16)


def dot(a, b):
    return jnp.dot(a, b, preferred_element_type=F32)


def whiten_into(w_ref, row0, raws, common_ref, mean_ref, start):
    rows = raws[0].shape[0]
    target = pl.ds(row0, rows)
    cols = pl.ds(start, GROUP)
    for w in range(len(raws) // 2):
        re = raws[2 * w][:, cols].astype(F32) - common_ref[w, 0:1, cols]
        im = raws[2 * w + 1][:, cols].astype(F32) - common_ref[w, 1:2, cols]
        power = re * re + im * im
        magnitude = (power * lax.rsqrt(jnp.maximum(power, TINY))).astype(BF16)
        scale = 1.0 / (dot(magnitude, mean_ref[...]) + 1e-06)
        w_ref[target, pl.ds(2 * w * GROUP, GROUP)] = (re * scale).astype(BF16)
        w_ref[target, pl.ds((2 * w + 1) * GROUP, GROUP)] = (im * scale).astype(BF16)


def columns_of(rows_of_tiles):
    lanes = rows_of_tiles.shape[1]
    padded = rows_of_tiles.astype(F32)
    if missing := -padded.shape[0] % 8:
        padded = jnp.concatenate([padded, jnp.zeros((missing, lanes), F32)], axis=0)
    square = (lanes, lanes)
    same = lax.broadcasted_iota(jnp.int32, square, 0) == lax.broadcasted_iota(jnp.int32, square, 1)
    unit = jnp.where(same, 1.0, 0.0).astype(BF16)
    return lax.dot_general(
        unit, padded.astype(BF16), (((1,), (1,)), ((), ())), preferred_element_type=F32
    )


def hot_rows(column, width):
    lane = lax.broadcasted_iota(jnp.int32, (column.shape[0], width), 1).astype(F32)
    return jnp.where(column == lane, 1.0, 0.0).astype(BF16)


def fill_hot(values, hot_ref):
    tiles, lanes = values.shape
    columns = columns_of(values)
    for tile in range(tiles):
        hot_ref[pl.ds(tile * lanes, lanes), :] = hot_rows(
            columns[:, tile : tile + 1], hot_ref.shape[1]
        )


def correlate_rows(hot_a, hot_b, w_ref, table_ref, start):
    both = dot(jnp.concatenate([hot_a, hot_b], axis=0), w_ref[...])
    a, b = both[: hot_a.shape[0]], both[hot_a.shape[0] :]
    real = imag = None
    for w in range(w_ref.shape[1] // (2 * GROUP)):
        ar, ai, br, bi = (
            x[:, (2 * w + r) * GROUP : (2 * w + r + 1) * GROUP] for x in (a, b) for r in range(2)
        )
        re = ar * br + ai * bi
        im = ai * br - ar * bi
        real = re if real is None else real + re
        imag = im if imag is None else imag + im
    rows = pl.ds(start, GROUP)
    return dot(real.astype(BF16), table_ref[0, rows, :]) + dot(
        imag.astype(BF16), table_ref[1, rows, :]
    )


def near_kernel(parts, first, info_ref, *refs):
    refs = list(refs)

    def take(number):
        taken = refs[:number]
        del refs[:number]
        return taken

    own, other = take(parts), take(parts)
    common_ref, table_ref, mean_ref, first_ref, offset_ref, live_ref, before_ref = take(7)
    (acc_ref,) = take(1)
    white = take(parts) if first else []
    hot_a, hot_b, *held = refs
    rows = own[0].shape[0]

    @pl.when(pl.program_id(0) == 0)
    def _():
        acc_ref[...] = jnp.zeros_like(acc_ref) if first else before_ref[...]
        shift = info_ref[0]
        offset = offset_ref[...]
        live = live_ref[...] != 0
        inside = (offset >= 0) & (offset < rows)
        beside = (offset >= shift) & (offset < shift + rows)
        place = jnp.where(inside, offset, jnp.where(beside, offset - shift + rows, -1))
        fill_hot(jnp.where(live, first_ref[...], -1), hot_a)
        fill_hot(jnp.where(live, place, -1), hot_b)

    def prepare(group):
        start = group * GROUP
        w_ref = held[group]
        whiten_into(w_ref, 0, own, common_ref, mean_ref, start)
        whiten_into(w_ref, rows, other, common_ref, mean_ref, start)
        for part in range(len(white)):
            white[part][:, pl.ds(start, GROUP)] = w_ref[
                pl.ds(0, rows), pl.ds(part * GROUP, GROUP)
            ]

    def run(block):
        slots = pl.ds(0, block)
        prepare(0)
        for group in range(len(held)):
            if group + 1 < len(held):
                prepare(group + 1)
            acc_ref[slots, :] += correlate_rows(
                hot_a[slots, :], hot_b[slots, :], held[group], table_ref, group * GROUP
            )

    total = hot_a.shape[0]
    pl.when(info_ref[1] <= total // 2)(lambda: run(total // 2))
    pl.when(info_ref[1] > total // 2)(lambda: run(total))


def plan_kernel(info_ref, first_ref, offset_ref, live_ref, code_ref, _, hot_a, hot_b, spread, back, rest, count_ref):
    tiles, lanes = first_ref.shape
    rows = hot_a.shape[1] // 2
    shift = info_ref[0]
    code = code_ref[...].astype(F32).astype(jnp.int32)
    far_a = code[0:tiles]
    far_b = far_a + code[tiles : 2 * tiles] + shift
    theirs = (far_b >= 0) & (far_b < rows) & (code[2 * tiles : 3 * tiles] != 0)
    offset = offset_ref[...]
    owns = (offset >= shift) & (offset < shift + rows) & (live_ref[...] != 0)
    cross = jnp.concatenate([theirs.astype(F32), owns.astype(F32)], axis=0)
    values_a = jnp.concatenate([far_a + rows, first_ref[...]], axis=0)
    values_b = jnp.concatenate([far_b, offset - shift + rows], axis=0)
    square = (lanes, lanes)
    row = lax.broadcasted_iota(jnp.int32, square, 0)
    col = lax.broadcasted_iota(jnp.int32, square, 1)
    ahead = jnp.where(row < col, 1.0, 0.0).astype(BF16)
    within = dot(cross.astype(BF16), ahead)
    sums = jnp.sum(cross, axis=1, keepdims=True)
    slots = hot_a.shape[0]
    packed = lax.broadcasted_iota(jnp.int32, (slots, lanes), 0).astype(F32)
    lane_rows = lax.broadcasted_iota(jnp.int32, (2 * rows, lanes), 0)
    base = jnp.zeros((1, 1), F32)
    total_a = jnp.zeros(hot_a.shape, F32)
    total_b = jnp.zeros(hot_b.shape, F32)
    bases = []
    for tile in range(2 * tiles):
        bases.append(base)
        place = jnp.where(cross[tile : tile + 1] > 0, within[tile : tile + 1] + base, -1.0)
        select = jnp.where(packed == place, 1.0, 0.0).astype(BF16)
        for values, which in ((values_a, 0), (values_b, 1)):
            ones = jnp.where(lane_rows == values[tile : tile + 1], 1.0, 0.0).astype(BF16)
            part = lax.dot_general(
                select, ones, (((1,), (1,)), ((), ())), preferred_element_type=F32
            )
            if which:
                total_b = total_b + part
            else:
                total_a = total_a + part
        base = base + sums[tile : tile + 1]
    hot_a[...] = total_a.astype(BF16)
    hot_b[...] = total_b.astype(BF16)
    within_columns = columns_of(within)
    cross_columns = columns_of(cross)
    for tile in range(tiles):
        mine = tiles + tile
        live_column = cross_columns[:, mine : mine + 1] > 0
        column = within_columns[:, mine : mine + 1] + bases[mine]
        target = pl.ds(tile * lanes, lanes)
        spread[target, :] = hot_rows(jnp.where(live_column, column, -1.0), spread.shape[1])
        column = jnp.where(live_column, column - bases[tiles], -1.0)
        back[target, :] = hot_rows(column, back.shape[1])
        rest[target, :] = hot_rows(column - back.shape[1], rest.shape[1])
    count_ref[0] = jnp.sum(cross).astype(jnp.int32)


def far_kernel(parts, pieces, first, info_ref, count_ref, *refs):
    refs = list(refs)

    def take(number):
        taken = refs[:number]
        del refs[:number]
        return taken

    white = [take(parts) for _ in range(pieces)]
    other = [take(parts) for _ in range(pieces)]
    common = take(pieces)
    table = take(pieces)
    mean_ref, hot_a, hot_b = take(3)
    (before_ref,) = take(1)
    acc_ref = take(1)[0]
    sent_ref, rest_ref = (None, None) if first else take(2)
    work_ref, load_sem, store_sem = take(3)
    held = refs
    rows, piece = other[0][0].shape
    blocks = (count_ref[0] + FAR_BLOCK - 1) // FAR_BLOCK

    def span(block):
        return pl.ds(pl.multiple_of(block * FAR_BLOCK, FAR_BLOCK), FAR_BLOCK)

    def load(block):
        return pltpu.make_async_copy(
            before_ref.at[span(block), :], work_ref.at[span(block), :], load_sem.at[block]
        )

    def store(block):
        return pltpu.make_async_copy(
            work_ref.at[span(block), :], acc_ref.at[span(block), :], store_sem.at[block]
        )

    if not first:
        lax.fori_loop(0, blocks, lambda block, _: load(block).start(), None)
    each = piece // GROUP
    for number, w_ref in enumerate(held):
        at, start = number // each, number % each * GROUP
        for part in range(parts):
            w_ref[pl.ds(0, rows), pl.ds(part * GROUP, GROUP)] = white[at][part][
                :, pl.ds(start, GROUP)
            ]
        whiten_into(w_ref, rows, other[at], common[at], mean_ref, start)

    def one_block(block, _):
        target = span(block)
        gained = None
        for number, w_ref in enumerate(held):
            at, start = number // each, number % each * GROUP
            part = correlate_rows(hot_a[target, :], hot_b[target, :], w_ref, table[at], start)
            gained = part if gained is None else gained + part
        if first:
            work_ref[target, :] = gained
        else:
            load(block).wait()
            work_ref[target, :] += gained
        store(block).start()

    lax.fori_loop(0, blocks, one_block, None)
    if not first:
        sent = sent_ref.shape[0]
        used = lax.broadcasted_iota(jnp.int32, (sent + rest_ref.shape[0], 1), 0)
        used = used < blocks * FAR_BLOCK
        for ref, at in ((sent_ref, 0), (rest_ref, sent)):
            ours = slice(at, at + ref.shape[0])
            ref[...] = jnp.where(used[ours], work_ref[ours, :], 0.0).astype(BF16)
    lax.fori_loop(0, blocks, lambda block, _: store(block).wait(), None)


def prepare_kernel(width, counts, info_ref, x_ref, pairs_ref, live_ref, flat_ref, total_ref, *sent):
    bins = x_ref.shape[3]
    parts = flat_ref.shape[1] // bins
    flat_ref[...] = x_ref[...].reshape(flat_ref.shape)
    total = x_ref[0].astype(F32)
    for row in range(1, x_ref.shape[0]):
        total = total + x_ref[row].astype(F32)

    @pl.when(pl.program_id(0) == 0)
    def _():
        total_ref[:, :, pl.ds(0, bins)] = total
        second = pairs_ref[...][:, 1, :] - info_ref[1]
        crossing = (second >= 0) & (second < info_ref[2]) & (live_ref[...] != 0)
        number = jnp.sum(jnp.where(crossing, 1.0, 0.0))
        flag = jnp.where(number > BACK_ROWS, 1.0, 0.0)
        lanes = total_ref.shape[2] - bins
        total_ref[:, :, pl.ds(bins, lanes)] = jnp.full(total_ref.shape[:2] + (lanes,), flag, F32)

    @pl.when(pl.program_id(0) > 0)
    def _():
        total_ref[:, :, pl.ds(0, bins)] += total

    done = 0
    for pieces, ref in zip(counts, sent):
        for part in range(parts):
            start = part * bins + done * width + info_ref[0]
            ref[:, pl.ds(part * pieces * width, pieces * width)] = flat_ref[
                :, pl.ds(pl.multiple_of(start, width), pieces * width)
            ]
        done += pieces


def gather_kernel(scale, count_ref, near_ref, spread_ref, far_ref, o_ref, held, sem):
    blocks = (count_ref[0] + FAR_BLOCK - 1) // FAR_BLOCK

    def load(block):
        rows = pl.ds(pl.multiple_of(block * FAR_BLOCK, FAR_BLOCK), FAR_BLOCK)
        return pltpu.make_async_copy(far_ref.at[rows, :], held.at[rows, :], sem.at[block])

    lax.fori_loop(0, blocks, lambda block, _: load(block).start(), None)
    o_ref[...] = near_ref[...] * scale

    def add(block, _):
        load(block).wait()
        start = pl.multiple_of(block * FAR_BLOCK, FAR_BLOCK)
        far = held[pl.ds(start, FAR_BLOCK), :] * scale
        high = far.astype(BF16)
        low = (far - high.astype(F32)).astype(BF16)
        spread = spread_ref[:, pl.ds(start, FAR_BLOCK)]
        o_ref[...] += dot(spread, high) + dot(spread, low)

    lax.fori_loop(0, blocks, add, None)


def merge_kernel(scale, mine_ref, *refs):
    total = mine_ref[...]
    for spread_ref, back_ref in zip(refs[0:-1:2], refs[1:-1:2]):
        total = total + dot(spread_ref[...], back_ref[...]) * scale
    refs[-1][...] = total


def params():
    return dict(
        compiler_params=pltpu.CompilerParams(vmem_limit_bytes=VMEM_BYTES),
        cost_estimate=pl.CostEstimate(flops=1000, bytes_accessed=1000, transcendentals=0),
    )


def whole(shape):
    return pl.BlockSpec(shape, lambda *_: (0,) * len(shape))


def prepare(spectra, info, width, counts, pairs, live):
    rows, windows, two, bins = spectra.shape
    parts = windows * two
    lanes = [parts * bins] + [parts * pieces * width for pieces in counts]
    blocks = [pl.BlockSpec((ROW_BLOCK, n), lambda i, s: (i, 0)) for n in lanes]
    shapes = [jax.ShapeDtypeStruct((rows, n), BF16) for n in lanes]
    return pl.pallas_call(
        functools.partial(prepare_kernel, width, counts),
        grid_spec=pltpu.PrefetchScalarGridSpec(
            num_scalar_prefetch=1,
            grid=(rows // ROW_BLOCK,),
            in_specs=[
                pl.BlockSpec((ROW_BLOCK, windows, two, bins), lambda i, s: (i, 0, 0, 0)),
                whole(pairs.shape),
                whole(live.shape),
            ],
            out_specs=blocks[:1] + [whole((windows, two, bins + live.shape[1]))] + blocks[1:],
        ),
        out_shape=shapes[:1] + [jax.ShapeDtypeStruct((windows, two, bins + live.shape[1]), F32)]
        + shapes[1:],
        name="prepare",
        **params(),
    )(info, spectra, pairs, live)


def behind(array, *after):
    anywhere = pl.BlockSpec(memory_space=pl.ANY)
    return pl.pallas_call(
        lambda *refs: None,
        in_specs=[anywhere] * (1 + len(after)),
        out_specs=anywhere,
        out_shape=jax.ShapeDtypeStruct(array.shape, array.dtype),
        input_output_aliases={0: 0},
        name="behind",
        **params(),
    )(array, *after)


def body(spectra, pair_channels, pair_live):
    rows, windows, _, bins = spectra.shape
    parts = 2 * windows
    count = lax.axis_size("row")
    me = lax.axis_index("row")
    odd = me % 2
    first_row = me * rows
    half = bins // 2
    fast = [(i, i ^ 1) for i in range(count)]
    slow = [(i, i + 1) for i in range(1, count - 1, 2)]
    slow = slow + [(b, a) for a, b in slow]
    piece = half // 4
    send_start = (1 - odd) * half

    tiles, tile = pair_live.shape
    slots = tiles * tile
    first_rows = pair_channels[:, :, 0] - first_row
    offsets = pair_channels[:, :, 1] - first_row
    code = jnp.concatenate([first_rows, offsets - first_rows, pair_live], axis=0).astype(BF16)
    code_rows = -(-3 * tiles // 16) * 16
    code = jnp.pad(code, ((0, code_rows - 3 * tiles), (0, 0)))
    far_code = lax.ppermute(code, "row", slow)

    counts = (1, 1, 1, 1)
    far_low = first_row + jnp.where(odd == 1, rows, -rows)
    flat, total, *chunks = prepare(
        spectra,
        jnp.stack([send_start, far_low, jnp.int32(rows)]),
        piece,
        counts,
        jnp.swapaxes(pair_channels, 1, 2),
        pair_live,
    )
    if count & (count - 1):
        reach = lax.psum(total, "row")
        partner_rows = lax.ppermute(flat, "row", fast)
        far_rows = [lax.ppermute(behind(chunks[0], reach, far_code), "row", slow)]
    else:
        reach = total
        jump = 1
        while jump < count:
            others = [
                lax.ppermute(reach, "row", [(i, i ^ k) for i in range(count)])
                for k in (jump, 2 * jump, 3 * jump)
                if 2 * jump < count or k == jump
            ]
            reach = functools.reduce(jnp.add, others, reach)
            if jump == 1:
                flat = behind(flat, reach)
                partner_rows = lax.ppermute(flat, "row", fast)
                far_rows = [lax.ppermute(behind(chunks[0], reach, far_code), "row", slow)]
            jump *= 4
    common = reach / (rows * count)
    far_rows.append(lax.ppermute(behind(chunks[1], reach), "row", slow))
    far_rows.append(lax.ppermute(behind(chunks[2], partner_rows), "row", slow))

    wide = NEAR_GROUPS * GROUP
    near_shift = jnp.where(odd == 1, -rows, rows)
    order = jnp.arange(slots, dtype=jnp.int32).reshape(tiles, tile)
    live_end = jnp.max(jnp.where(pair_live != 0, order + 1, 0))
    near_info = jnp.stack(
        [near_shift, live_end, odd * (half // wide), (1 - odd) * (half // wide)]
    )
    lists = (first_rows, offsets, pair_live)
    list_specs = [whole((tiles, tile))] * 3
    table = jnp.asarray(lag_table(bins, LAGS))
    mean = jnp.asarray(band_mean())

    steps = bins // wide
    share = half // wide

    def near_call(first, before):
        offset = 2 if first else 3

        def bin_block(j, s):
            return s[offset] + j

        return pl.pallas_call(
            functools.partial(near_kernel, parts, first),
            grid_spec=pltpu.PrefetchScalarGridSpec(
                num_scalar_prefetch=1,
                grid=(share,),
                in_specs=[
                    pl.BlockSpec(
                        (rows, wide),
                        functools.partial(lambda p, j, s: (0, p * steps + bin_block(j, s)), p),
                    )
                    for _ in range(2)
                    for p in range(parts)
                ]
                + [
                    pl.BlockSpec((windows, 2, wide), lambda j, s: (0, 0, bin_block(j, s))),
                    pl.BlockSpec((2, wide, LAGS), lambda j, s: (0, bin_block(j, s), 0)),
                    whole((GROUP, GROUP)),
                ]
                + list_specs
                + [pl.BlockSpec(memory_space=pl.ANY) if first else whole((slots, LAGS))],
                out_specs=[whole((slots, LAGS))]
                + [pl.BlockSpec((rows, wide), lambda j, s: (0, j))] * (parts * first),
                scratch_shapes=[pltpu.VMEM((slots, 2 * rows), BF16)] * 2
                + [pltpu.VMEM((2 * rows, parts * GROUP), BF16)] * NEAR_GROUPS,
            ),
            out_shape=[jax.ShapeDtypeStruct((slots, LAGS), F32)]
            + [jax.ShapeDtypeStruct((rows, half), BF16)] * (parts * first),
            name="near_pairs",
            **params(),
        )(
            near_info,
            *[flat] * parts,
            *[partner_rows] * parts,
            common,
            table,
            mean,
            *lists,
            before,
        )

    near_acc, *white = near_call(True, far_code)
    far_rows.append(lax.ppermute(behind(chunks[3], near_acc), "row", slow))
    (near_acc,) = near_call(False, near_acc)

    hot_a, hot_b, spread, back_spread, rest_spread, cross_count = pl.pallas_call(
        plan_kernel,
        grid_spec=pltpu.PrefetchScalarGridSpec(
            num_scalar_prefetch=1,
            grid=(1,),
            in_specs=list_specs
            + [whole((code_rows, tile))]
            + [pl.BlockSpec(memory_space=pl.ANY)],
            out_specs=[
                whole((2 * slots, 2 * rows)),
                whole((2 * slots, 2 * rows)),
                whole((slots, 2 * slots)),
                whole((slots, BACK_ROWS)),
                whole((slots, slots - BACK_ROWS)),
                pl.BlockSpec(memory_space=pltpu.SMEM),
            ],
        ),
        out_shape=[
            jax.ShapeDtypeStruct((2 * slots, 2 * rows), BF16),
            jax.ShapeDtypeStruct((2 * slots, 2 * rows), BF16),
            jax.ShapeDtypeStruct((slots, 2 * slots), BF16),
            jax.ShapeDtypeStruct((slots, BACK_ROWS), BF16),
            jax.ShapeDtypeStruct((slots, slots - BACK_ROWS), BF16),
            jax.ShapeDtypeStruct((1,), jnp.int32),
        ],
        name="plan",
        **params(),
    )(-near_shift[None], *lists, far_code, near_acc)

    info = (odd * (half // piece))[None]

    owned = [(k, n, i) for k, n in enumerate(counts) for i in range(n)]

    def far_call(at, first, before):
        pieces = len(at)
        own_at = [functools.partial(lambda c, j, s, n: s[0] + c, c) for c in at]
        specs = (
            [
                pl.BlockSpec((rows, piece), functools.partial(lambda n, *i: (0, n), c))
                for c in at
                for _ in range(parts)
            ]
            + [
                pl.BlockSpec((rows, piece), functools.partial(lambda n, *i: (0, n), p * owned[c][1] + owned[c][2]))
                for c in at
                for p in range(parts)
            ]
            + [
                pl.BlockSpec((windows, 2, piece), functools.partial(lambda f, *i: (0, 0, f(*i)), f))
                for f in own_at
            ]
            + [
                pl.BlockSpec((2, piece, LAGS), functools.partial(lambda f, *i: (0, f(*i), 0), f))
                for f in own_at
            ]
            + [whole((GROUP, GROUP))]
            + [whole((2 * slots, 2 * rows))] * 2
        )
        operands = (
            list(white) * pieces
            + [far_rows[owned[c][0]] for c in at for _ in range(parts)]
            + [common] * pieces
            + [table] * pieces
            + [mean, hot_a, hot_b]
        )
        out_specs = [pl.BlockSpec(memory_space=pl.ANY)]
        out_shape = [jax.ShapeDtypeStruct((2 * slots, LAGS), F32)]
        specs.append(pl.BlockSpec(memory_space=pl.ANY))
        operands.append(before)
        if not first:
            for back_rows in (BACK_ROWS, slots - BACK_ROWS):
                out_specs.append(whole((back_rows, LAGS)))
                out_shape.append(jax.ShapeDtypeStruct((back_rows, LAGS), BF16))
        most = 2 * slots // FAR_BLOCK
        return pl.pallas_call(
            functools.partial(far_kernel, parts, pieces, first),
            grid_spec=pltpu.PrefetchScalarGridSpec(
                num_scalar_prefetch=2,
                grid=(1,),
                in_specs=specs,
                out_specs=out_specs,
                scratch_shapes=[
                    pltpu.VMEM((2 * slots, LAGS), F32),
                    pltpu.SemaphoreType.DMA((most,)),
                    pltpu.SemaphoreType.DMA((most,)),
                ]
                + [pltpu.VMEM((2 * rows, parts * GROUP), BF16)] * (pieces * piece // GROUP),
            ),
            out_shape=out_shape,
            name="far_pairs",
            **params(),
        )(info, cross_count, *operands)

    (before,) = far_call((0, 1, 2), True, near_acc)
    far_acc, theirs, their_rest = far_call((3,), False, before)

    scale = 1.0 / math.sqrt(bins * windows)
    back = lax.ppermute(theirs, "row", slow)
    gathered = pl.pallas_call(
        functools.partial(gather_kernel, scale),
        grid_spec=pltpu.PrefetchScalarGridSpec(
            num_scalar_prefetch=1,
            grid=(1,),
            in_specs=[
                whole((slots, LAGS)),
                whole((slots, 2 * slots)),
                pl.BlockSpec(memory_space=pl.ANY),
            ],
            out_specs=whole((slots, LAGS)),
            scratch_shapes=[
                pltpu.VMEM((2 * slots, LAGS), F32),
                pltpu.SemaphoreType.DMA((2 * slots // FAR_BLOCK,)),
            ],
        ),
        out_shape=jax.ShapeDtypeStruct((slots, LAGS), F32),
        name="gather",
        **params(),
    )(cross_count, near_acc, spread, far_acc)

    def merge(*spread_back):
        return pl.pallas_call(
            functools.partial(merge_kernel, scale),
            grid=(tiles,),
            in_specs=[pl.BlockSpec((tile, LAGS), lambda i: (i, 0))]
            + [
                spec
                for k in range(0, len(spread_back), 2)
                for spec in (
                    pl.BlockSpec((tile, spread_back[k].shape[1]), lambda i: (i, 0)),
                    whole(spread_back[k + 1].shape),
                )
            ],
            out_specs=pl.BlockSpec((tile, LAGS), lambda i: (i, 0)),
            out_shape=jax.ShapeDtypeStruct((slots, LAGS), F32),
            name="merge",
            **params(),
        )(gathered, *spread_back)

    result = lax.cond(
        common[0, 0, bins] > 0,
        lambda: merge(back_spread, back, rest_spread, lax.ppermute(their_rest, "row", slow)),
        lambda: merge(back_spread, back),
    )
    return result.reshape(pair_live.shape + (LAGS,))


def solution(mesh):
    placed = (P(("day", "row"), None, None, None), P("row", None, None), P("row", None))
    return jax.shard_map(
        body, mesh=mesh, in_specs=placed, out_specs=P(("day", "row"), None, None), check_vma=False
    )
```

time: 475 us -> 105 us (0.22)
  the two profiles are of different devices: /device:TPU:1 before, /device:TPU:23 now
where the time goes in v2:
time: 105 us; the launch traced here: 104 us
  Pallas kernels  59.6 us (57%)
  starting transfers between devices  28 us (27%)
  waiting for transfers between devices  5.6 us (5%)
  other arithmetic  5.27 us (5%)
  local copies, waits for them, and re-layouts  4.85 us (5%)
    pallas_call x2, Pallas kernels, near_call(): pl.pallas_call(functools.partial(near_kernel, parts, first), grid_spec=pl...  27 us
    pallas_call x2, Pallas kernels, far_call(): pl.pallas_call(functools.partial(far_kernel, parts, pieces, first), grid_...  15.1 us
    pallas_call x1, Pallas kernels, prepare(): pl.pallas_call(functools.partial(prepare_kernel, width, counts), grid_spe...  8.47 us
    ppermute x6, starting transfers between devices, body(): lax.ppermute(reach, 'row', [(i, i ^ k) for i in range(count)])  5.59 us
    pallas_call x1, Pallas kernels, body(): pl.pallas_call(plan_kernel, grid_spec=pltpu.PrefetchScalarGridSpec(num_sc...  4.5 us
    ppermute x1, starting transfers between devices, body(): back = lax.ppermute(theirs, 'row', slow)  4.46 us
    ppermute x1, starting transfers between devices, body(): far_code = lax.ppermute(code, 'row', slow)  4.45 us
    ppermute x1, starting transfers between devices, body(): far_rows.append(lax.ppermute(behind(chunks[2], partner_rows), 'row', slow))  4.45 us
  transfers between devices with their start and end apart: 13, of which 3 were waited for; matrix products, arithmetic and copies ran while one was open for 4% of the time, Pallas kernels for 43%

profile of v2, /device:TPU:23, one launch (start us, length us, event | category | flops | bytes accessed | tf_op | source)
XLA Modules:
  0.0 104.2 jit_solution(18190856810034709344)
XLA Ops:
  0.0 0.6 pad_add_fusion.info_ref
  0.6 8.5 %prepare.1 = (bf16[128,16384]{1,0:T(8,128)(2,1)}, f32[2,2,4224]{2,1,0:T(2,128)}, bf16[128,2048]{1,0:T(8,128)(2,1)}, bf16[128,2048]{1,0:T(8,128)(2,1)}, bf16[128,...) custom-call(s32[3]{0:T(128)} %pad_add_fusion.info_ref, bf16[128,2,2,4096]{3,2,1,0:T(2,128)(2,1)} %x_ref.1, ...), custom_call_target="tpu_custom_call" | custom-call | flops 1000 | bytes 1000 | tf_op jit(solution)/shard_map/prepare/pallas_call | solution.py:358
  9.1 0.9 collective-permute-start.3
  9.9 1.2 %collective-permute-start.2 = (f32[2,2,4224]{2,1,0:T(2,128)}, f32[2,2,4224]{2,1,0:T(2,128)S(1)}, u32[]{:S(2)}, u32[]{:S(2)}) collective-permute-start(f32[2,2,4224]{2,1,0:T(2,128)} %get-tuple-element.53), channel_id=1, source_target_pairs={{0,2},{1,3},{2,0},{3,1},{4,6},{5,7},{6,4},{7,5},{8,10},{9,11},{10,... | collective-permute-start | bytes 202760 | tf_op jit(solution)/shard_map/ppermute | solution.py:432
  11.3 2.8 %collective-permute-done.3 = f32[2,2,4224]{2,1,0:T(2,128)S(1)} collective-permute-done((f32[2,2,4224]{2,1,0:T(2,128)}, f32[2,2,4224]{2,1,0:T(2,128)S(1)}, u32[]{:S(2)}, u32[]{:S(2)}) %collective-permute-start.3) | collective-permute-done | bytes 67616 | tf_op jit(solution)/shard_map/ppermute | solution.py:432
  14.1 1.4 %collective-permute-done.2 = f32[2,2,4224]{2,1,0:T(2,128)S(1)} collective-permute-done((f32[2,2,4224]{2,1,0:T(2,128)}, f32[2,2,4224]{2,1,0:T(2,128)S(1)}, u32[]{:S(2)}, u32[]{:S(2)}) %collective-permute-start.2) | collective-permute-done | bytes 67616 | tf_op jit(solution)/shard_map/ppermute | solution.py:432
  15.5 1.6 %add_add_fusion.1.refs_1_ = f32[2,2,4224]{2,1,0:T(2,128)} fusion(f32[2,2,4224]{2,1,0:T(2,128)S(1)} %collective-permute-done.3, f32[2,2,4224]{2,1,0:T(2,128)S(1)} %collective-permute-done.2, f32[2,2,4224]{2,1,0:T(2,128)} %get-tuple-element.53, f32[2,2,4224]{2,1,0:T(2,128)S(1)} %collective-permute-done.1), kind=kLoop, calls=%fused_computation.1 | loop fusion | flops 50688 | bytes 337920 | tf_op jit(solution)/shard_map/add | solution.py:436
  17.8 0.6 select_reduce_fusion
  18.4 0.6 subtract_convert_fusion
  19.2 3.2 %collective-permute-start.5 = (f32[2,2,4224]{2,1,0:T(2,128)S(1)}, f32[2,2,4224]{2,1,0:T(2,128)S(1)}, u32[]{:S(2)}, u32[]{:S(2)}) collective-permute-start(f32[2,2,4224]{2,1,0:T(2,128)S(1)} %copy-done.4), channel_id=1, source_target_pairs={{0,8},{1,9},{2,10},{3,11},{4,12},{5,13},{6,14},{7,15},{8,0},{9,1},... | collective-permute-start | bytes 202760 | tf_op jit(solution)/shard_map/ppermute | solution.py:432
  22.4 4.5 %collective-permute-start.7 = (bf16[16,128]{1,0:T(8,128)(2,1)S(1)}, bf16[16,128]{1,0:T(8,128)(2,1)S(1)}, u32[]{:S(2)}, u32[]{:S(2)}) collective-permute-start(bf16[16,128]{1,0:T(8,128)(2,1)S(1)} %fusion.4), channel_id=1, source_target_pairs={{1,2},{3,4},{5,6},{7,8},{9,10},{11,12},{13,14},{2,1},{4,3},{6,5},{... | collective-permute-start | bytes 12296 | tf_op jit(solution)/shard_map/ppermute | solution.py:411
  26.9 1.4 %collective-permute-done.7.refs_14_.code_ref.refs_2_ = bf16[16,128]{1,0:T(8,128)(2,1)S(1)} collective-permute-done((bf16[16,128]{1,0:T(8,128)(2,1)S(1)}, bf16[16,128]{1,0:T(8,128)(2,1)S(1)}, u32[]{:S(2)}, u32[]{:S(2)}) %collective-permute-start.7) | collective-permute-done | bytes 4128 | tf_op jit(solution)/shard_map/ppermute | solution.py:411
  28.2 0.6 copy-done.10
  28.8 4.4 %collective-permute-start.10 = (bf16[128,2048]{1,0:T(8,128)(2,1)}, bf16[128,2048]{1,0:T(8,128)(2,1)S(1)}, u32[]{:S(2)}, u32[]{:S(2)}) collective-permute-start(bf16[128,2048]{1,0:T(8,128)(2,1)} %behind.7), channel_id=1, source_target_pairs={{1,2},{3,4},{5,6},{7,8},{9,10},{11,12},{13,14},{2,1},{4,3},{6,5},{... | collective-permute-start | bytes 1572872 | tf_op jit(solution)/shard_map/ppermute | solution.py:440
  33.3 0.7 broadcast_multiply_fusion
  34.0 2.0 %collective-permute-start.11 = (bf16[128,2048]{1,0:T(8,128)(2,1)}, bf16[128,2048]{1,0:T(8,128)(2,1)S(1)}, u32[]{:S(2)}, u32[]{:S(2)}) collective-permute-start(bf16[128,2048]{1,0:T(8,128)(2,1)} %behind.8), channel_id=1, source_target_pairs={{1,2},{3,4},{5,6},{7,8},{9,10},{11,12},{13,14},{2,1},{4,3},{6,5},{... | collective-permute-start | bytes 1572872 | tf_op jit(solution)/shard_map/ppermute | solution.py:443
  36.1 4.5 %collective-permute-start.12 = (bf16[128,2048]{1,0:T(8,128)(2,1)}, bf16[128,2048]{1,0:T(8,128)(2,1)S(1)}, u32[]{:S(2)}, u32[]{:S(2)}) collective-permute-start(bf16[128,2048]{1,0:T(8,128)(2,1)} %behind.9), channel_id=1, source_target_pairs={{1,2},{3,4},{5,6},{7,8},{9,10},{11,12},{13,14},{2,1},{4,3},{6,5},{... | collective-permute-start | bytes 1572872 | tf_op jit(solution)/shard_map/ppermute | solution.py:444
  40.5 1.1 %pad_add_fusion.1.info_ref = s32[4]{0:T(128)} fusion(s32[1]{0:T(128)} %bitcast.11, s32[1]{0:T(128)} %bitcast.10, s32[1]{0:T(128)} %bitcast.9, s32[1]{0:T(128)} %bitcast.6), kind=kLoop, calls=%fused_computation.14 | loop fusion | flops 12 | bytes 32 | tf_op jit(solution)/shard_map/stack | solution.py:450
  41.7 13.5 %near_pairs.2 = (f32[512,512]{1,0:T(8,128)}, bf16[128,2048]{1,0:T(8,128)(2,1)}, bf16[128,2048]{1,0:T(8,128)(2,1)}, bf16[128,2048]{1,0:T(8,128)(2,1)}, bf16[128,2048]{1,0:T(8,128)(2,1)}) custom-call(s32[4]{0:T(128)} %pad_add_fusion.1.info_ref, bf16[128,16384]{1,0:T(8,128)(2,1)} %behind.5.refs_0_.refs_1_.refs_2_.refs_3_, ...), custom_call_target="tpu_custom_call" | custom-call | flops 1000 | bytes 1000 | tf_op jit(solution)/shard_map/near_pairs/pallas_call | solution.py:467
  55.2 2.2 %collective-permute-start.9 = (bf16[128,2048]{1,0:T(8,128)(2,1)}, bf16[128,2048]{1,0:T(8,128)(2,1)S(1)}, u32[]{:S(2)}, u32[]{:S(2)}) collective-permute-start(bf16[128,2048]{1,0:T(8,128)(2,1)} %behind.6), channel_id=1, source_target_pairs={{1,2},{3,4},{5,6},{7,8},{9,10},{11,12},{13,14},{2,1},{4,3},{6,5},{... | collective-permute-start | bytes 1572872 | tf_op jit(solution)/shard_map/ppermute | solution.py:508
  57.4 13.5 %near_pairs.3._.refs_33_.near_ref = f32[512,512]{1,0:T(8,128)} custom-call(s32[4]{0:T(128)} %pad_add_fusion.1.info_ref, bf16[128,16384]{1,0:T(8,128)(2,1)} %behind.5.refs_0_.refs_1_.refs_2_.refs_3_, bf16[128,16384]{1,0:T(8,128)(2,1)} %behind.5.refs_0_.refs_1_.refs_2_.refs_3_, bf16[128,16384]{1,0:T(8,128)(2,1)} %behind.5.refs_0_.refs_1_.refs_2_.refs_3_, ...), custom_call_target="tpu_custom_call" | custom-call | flops 1000 | bytes 1000 | tf_op jit(solution)/shard_map/near_pairs/pallas_call | solution.py:467
  70.9 4.5 %plan.1 = (bf16[1024,256]{1,0:T(8,128)(2,1)}, bf16[1024,256]{1,0:T(8,128)(2,1)}, bf16[512,1024]{1,0:T(8,128)(2,1)}, bf16[512,160]{1,0:T(8,128)(2,1)S(1)}, bf16[512,352]{1,0:T(8,128)(2,1)S(1)}, /*index=5*/s32[1]{0:T(128)}) custom-call(s32[1]{0:T(128)S(6)} %neg.3.info_ref, s32[4,128]{1,0:T(4,128)} %copy-done.9, ...), custom_call_target="tpu_custom_call" | custom-call | flops 1000 | bytes 1000 | tf_op jit(solution)/shard_map/plan/pallas_call | solution.py:511
  75.4 0.7 copy-done
  76.6 9.3 %far_pairs.2.refs_13_ = f32[1024,512]{1,0:T(8,128)} custom-call(s32[1]{0:T(128)} %bitcast.12.info_ref, s32[1]{0:T(128)} %get-tuple-element.56.count_ref, bf16[128,2048]{1,0:T(8,128)(2,1)} %get-tuple-element.58.refs_0_.refs_4_.refs_8_, bf16[128,2048]{1,0:T(8,128)(2,1)} %get-tuple-element.59.refs_1_.refs_5_.refs_9_, ...), custom_call_target="tpu_custom_call" | custom-call | flops 1000 | bytes 1000 | tf_op jit(solution)/shard_map/far_pairs/pallas_call | solution.py:585
  85.9 0.8 copy-done.3
  86.7 5.8 %far_pairs.3 = (f32[1024,512]{1,0:T(8,128)}, bf16[160,512]{1,0:T(8,128)(2,1)}, bf16[352,512]{1,0:T(8,128)(2,1)S(1)}) custom-call(s32[1]{0:T(128)} %bitcast.12.info_ref, s32[1]{0:T(128)} %get-tuple-element.56.count_ref, bf16[128,2048]{1,0:T(8,128)(2,1)} %get-tuple-element.58.refs_0_.refs_4_.refs_8_, ...), custom_call_target="tpu_custom_call" | custom-call | flops 1000 | bytes 1000 | tf_op jit(solution)/shard_map/far_pairs/pallas_call | solution.py:585
  92.5 4.5 %collective-permute-start.13 = (bf16[160,512]{1,0:T(8,128)(2,1)}, bf16[160,512]{1,0:T(8,128)(2,1)S(1)}, u32[]{:S(2)}, u32[]{:S(2)}) collective-permute-start(bf16[160,512]{1,0:T(8,128)(2,1)} %get-tuple-element.70), channel_id=1, source_target_pairs={{1,2},{3,4},{5,6},{7,8},{9,10},{11,12},{13,14},{2,1},{4,3},{6,5},{... | collective-permute-start | bytes 491528 | tf_op jit(solution)/shard_map/ppermute | solution.py:608
  96.9 1.2 %slice.12 = f32[1,1,1]{2,1,0:T(1,128)} slice(f32[2,2,4224]{2,1,0:T(2,128)} %get-tuple-element.78.refs_8_.refs_24_.refs_25_.refs_26_), slice={[0:1], [0:1], [4096:4097]} | slice | bytes 8 | tf_op jit(solution)/shard_map/slice | solution.py:650
  98.7 3.8 %gather.1 = f32[512,512]{1,0:T(8,128)S(1)} custom-call(s32[1]{0:T(128)} %get-tuple-element.56.count_ref, f32[512,512]{1,0:T(8,128)} %near_pairs.3._.refs_33_.near_ref, bf16[512,1024]{1,0:T(8,128)(2,1)} %get-tuple-element.57.spread_ref, f32[1024,512]{1,0:T(8,128)} %get-tuple-element.68.far_ref), custom_call_target="tpu_custom_call" | custom-call | flops 1000 | bytes 1000 | tf_op jit(solution)/shard_map/gather/pallas_call | solution.py:609
  102.5 0.8 conditional.1
  102.5 0.7 merge.2
  103.3 1.0 copy-done.6
  (40 shorter events, 1.4 us)
Async XLA Ops:
  9.1 5.0 %collective-permute-start.3 = (f32[2,2,4224]{2,1,0:T(2,128)}, f32[2,2,4224]{2,1,0:T(2,128)S(1)}, u32[]{:S(2)}, u32[]{:S(2)}) collective-permute-start(f32[2,2,4224]{2,1,0:T(2,128)} %get-tuple-element.53), channel_id=1, source_target_pairs={{0,3},{1,2},{2,1},{3,0},{4,7},{5,6},{6,5},{7,4},{8,11},{9,10},{10,... | collective-permute-start | bytes 202760 | tf_op jit(solution)/shard_map/ppermute | solution.py:432
  9.9 5.6 %collective-permute-start.2 = (f32[2,2,4224]{2,1,0:T(2,128)}, f32[2,2,4224]{2,1,0:T(2,128)S(1)}, u32[]{:S(2)}, u32[]{:S(2)}) collective-permute-start(f32[2,2,4224]{2,1,0:T(2,128)} %get-tuple-element.53), channel_id=1, source_target_pairs={{0,2},{1,3},{2,0},{3,1},{4,6},{5,7},{6,4},{7,5},{8,10},{9,11},{10,... | collective-permute-start | bytes 202760 | tf_op jit(solution)/shard_map/ppermute | solution.py:432
  11.2 4.3 %collective-permute-start.1 = (f32[2,2,4224]{2,1,0:T(2,128)}, f32[2,2,4224]{2,1,0:T(2,128)S(1)}, u32[]{:S(2)}, u32[]{:S(2)}) collective-permute-start(f32[2,2,4224]{2,1,0:T(2,128)} %get-tuple-element.53), channel_id=1, source_target_pairs={{0,1},{1,0},{2,3},{3,2},{4,5},{5,4},{6,7},{7,6},{8,9},{9,8},{10,11... | collective-permute-start | bytes 202760 | tf_op jit(solution)/shard_map/ppermute | solution.py:432
  17.1 0.7 copy-start.8
  17.1 1.3 %copy-start.11 = (s32[4,128,2]{1,2,0:T(2,128)S(1)}, s32[4,128,2]{1,2,0:T(2,128)}, u32[]{:S(2)}) copy-start(s32[4,128,2]{1,2,0:T(2,128)} %param.8) | copy-start | bytes 12292
  17.1 1.9 %copy-start.4 = (f32[2,2,4224]{2,1,0:T(2,128)S(1)}, f32[2,2,4224]{2,1,0:T(2,128)}, u32[]{:S(2)}) copy-start(f32[2,2,4224]{2,1,0:T(2,128)} %add_add_fusion.1.refs_1_) | copy-start | bytes 202756
  17.1 16.2 %copy-start.5 = (f32[2,2,4224]{2,1,0:T(2,128)S(1)}, f32[2,2,4224]{2,1,0:T(2,128)}, u32[]{:S(2)}) copy-start(f32[2,2,4224]{2,1,0:T(2,128)} %add_add_fusion.1.refs_1_) | copy-start | bytes 202756
  17.1 18.9 %collective-permute-start.8 = (bf16[128,16384]{1,0:T(8,128)(2,1)}, bf16[128,16384]{1,0:T(8,128)(2,1)}, u32[]{:S(2)}, u32[]{:S(2)}) collective-permute-start(bf16[128,16384]{1,0:T(8,128)(2,1)} %behind.5.refs_0_.refs_1_.refs_2_.refs_3_), channel_id=1, source_target_pairs={{0,1},{1,0},{2,3},{3,2},{4,5},{5,4},{6,7},{7,6},{8,9},{9,8},{10,11... | collective-permute-start | bytes 12582920 | tf_op jit(solution)/shard_map/ppermute | solution.py:439
  18.4 23.3 %copy-start.9 = (s32[4,128]{1,0:T(4,128)}, s32[4,128]{1,0:T(4,128)S(1)}, u32[]{:S(2)}) copy-start(s32[4,128]{1,0:T(4,128)S(1)} %get-tuple-element.75.refs_11_.first_ref) | copy-start | bytes 6148
  19.0 14.3 %collective-permute-start.6 = (f32[2,2,4224]{2,1,0:T(2,128)S(1)}, f32[2,2,4224]{2,1,0:T(2,128)S(1)}, u32[]{:S(2)}, u32[]{:S(2)}) collective-permute-start(f32[2,2,4224]{2,1,0:T(2,128)S(1)} %copy-done.4), channel_id=1, source_target_pairs={{0,12},{1,13},{2,14},{3,15},{4,8},{5,9},{6,10},{7,11},{8,4},{9,5},... | collective-permute-start | bytes 202760 | tf_op jit(solution)/shard_map/ppermute | solution.py:432
  19.2 14.1 %collective-permute-start.5 = (f32[2,2,4224]{2,1,0:T(2,128)S(1)}, f32[2,2,4224]{2,1,0:T(2,128)S(1)}, u32[]{:S(2)}, u32[]{:S(2)}) collective-permute-start(f32[2,2,4224]{2,1,0:T(2,128)S(1)} %copy-done.4), channel_id=1, source_target_pairs={{0,8},{1,9},{2,10},{3,11},{4,12},{5,13},{6,14},{7,15},{8,0},{9,1},... | collective-permute-start | bytes 202760 | tf_op jit(solution)/shard_map/ppermute | solution.py:432
  22.4 10.9 %collective-permute-start.4 = (f32[2,2,4224]{2,1,0:T(2,128)S(1)}, f32[2,2,4224]{2,1,0:T(2,128)S(1)}, u32[]{:S(2)}, u32[]{:S(2)}) collective-permute-start(f32[2,2,4224]{2,1,0:T(2,128)S(1)} %copy-done.4), channel_id=1, source_target_pairs={{0,4},{1,5},{2,6},{3,7},{4,0},{5,1},{6,2},{7,3},{8,12},{9,13},{10,... | collective-permute-start | bytes 202760 | tf_op jit(solution)/shard_map/ppermute | solution.py:432
  22.4 5.8 %collective-permute-start.7 = (bf16[16,128]{1,0:T(8,128)(2,1)S(1)}, bf16[16,128]{1,0:T(8,128)(2,1)S(1)}, u32[]{:S(2)}, u32[]{:S(2)}) collective-permute-start(bf16[16,128]{1,0:T(8,128)(2,1)S(1)} %fusion.4), channel_id=1, source_target_pairs={{1,2},{3,4},{5,6},{7,8},{9,10},{11,12},{13,14},{2,1},{4,3},{6,5},{... | collective-permute-start | bytes 12296 | tf_op jit(solution)/shard_map/ppermute | solution.py:411
  28.2 0.6 copy-start.10
  28.8 46.6 %collective-permute-start.10 = (bf16[128,2048]{1,0:T(8,128)(2,1)}, bf16[128,2048]{1,0:T(8,128)(2,1)S(1)}, u32[]{:S(2)}, u32[]{:S(2)}) collective-permute-start(bf16[128,2048]{1,0:T(8,128)(2,1)} %behind.7), channel_id=1, source_target_pairs={{1,2},{3,4},{5,6},{7,8},{9,10},{11,12},{13,14},{2,1},{4,3},{6,5},{... | collective-permute-start | bytes 1572872 | tf_op jit(solution)/shard_map/ppermute | solution.py:440
  34.0 41.4 %collective-permute-start.11 = (bf16[128,2048]{1,0:T(8,128)(2,1)}, bf16[128,2048]{1,0:T(8,128)(2,1)S(1)}, u32[]{:S(2)}, u32[]{:S(2)}) collective-permute-start(bf16[128,2048]{1,0:T(8,128)(2,1)} %behind.8), channel_id=1, source_target_pairs={{1,2},{3,4},{5,6},{7,8},{9,10},{11,12},{13,14},{2,1},{4,3},{6,5},{... | collective-permute-start | bytes 1572872 | tf_op jit(solution)/shard_map/ppermute | solution.py:443
  36.1 39.4 %collective-permute-start.12 = (bf16[128,2048]{1,0:T(8,128)(2,1)}, bf16[128,2048]{1,0:T(8,128)(2,1)S(1)}, u32[]{:S(2)}, u32[]{:S(2)}) collective-permute-start(bf16[128,2048]{1,0:T(8,128)(2,1)} %behind.9), channel_id=1, source_target_pairs={{1,2},{3,4},{5,6},{7,8},{9,10},{11,12},{13,14},{2,1},{4,3},{6,5},{... | collective-permute-start | bytes 1572872 | tf_op jit(solution)/shard_map/ppermute | solution.py:444
  55.2 30.7 %collective-permute-start.9 = (bf16[128,2048]{1,0:T(8,128)(2,1)}, bf16[128,2048]{1,0:T(8,128)(2,1)S(1)}, u32[]{:S(2)}, u32[]{:S(2)}) collective-permute-start(bf16[128,2048]{1,0:T(8,128)(2,1)} %behind.6), channel_id=1, source_target_pairs={{1,2},{3,4},{5,6},{7,8},{9,10},{11,12},{13,14},{2,1},{4,3},{6,5},{... | collective-permute-start | bytes 1572872 | tf_op jit(solution)/shard_map/ppermute | solution.py:508
  75.4 0.8 copy-start
  75.4 1.0 copy-start.1
  75.4 1.1 %copy-start.2 = (bf16[128,2048]{1,0:T(8,128)(2,1)}, bf16[128,2048]{1,0:T(8,128)(2,1)S(1)}, u32[]{:S(2)}) copy-start(bf16[128,2048]{1,0:T(8,128)(2,1)S(1)} %collective-permute-done.12.refs_20_.refs_21_.refs_22_.refs_23_) | copy-start | bytes 1572868
  85.9 0.8 copy-start.3
  92.5 10.0 %collective-permute-start.13 = (bf16[160,512]{1,0:T(8,128)(2,1)}, bf16[160,512]{1,0:T(8,128)(2,1)S(1)}, u32[]{:S(2)}, u32[]{:S(2)}) collective-permute-start(bf16[160,512]{1,0:T(8,128)(2,1)} %get-tuple-element.70), channel_id=1, source_target_pairs={{1,2},{3,4},{5,6},{7,8},{9,10},{11,12},{13,14},{2,1},{4,3},{6,5},{... | collective-permute-start | bytes 491528 | tf_op jit(solution)/shard_map/ppermute | solution.py:608
  103.3 1.0 copy-start.6

commit v3 on v2

--- a/solution.py
+++ b/solution.py
@@ -99,7 +99,7 @@
     )
 
 
-def near_kernel(parts, first, info_ref, *refs):
+def near_kernel(parts, info_ref, *refs):
     refs = list(refs)
 
     def take(number):
@@ -108,15 +108,15 @@
         return taken
 
     own, other = take(parts), take(parts)
-    common_ref, table_ref, mean_ref, first_ref, offset_ref, live_ref, before_ref = take(7)
+    common_ref, table_ref, mean_ref, first_ref, offset_ref, live_ref = take(6)
     (acc_ref,) = take(1)
-    white = take(parts) if first else []
+    white = take(parts)
     hot_a, hot_b, *held = refs
     rows = own[0].shape[0]
 
     @pl.when(pl.program_id(0) == 0)
     def _():
-        acc_ref[...] = jnp.zeros_like(acc_ref) if first else before_ref[...]
+        acc_ref[...] = jnp.zeros_like(acc_ref)
         shift = info_ref[0]
         offset = offset_ref[...]
         live = live_ref[...] != 0
@@ -151,7 +151,7 @@
     pl.when(info_ref[1] > total // 2)(lambda: run(total))
 
 
-def plan_kernel(info_ref, first_ref, offset_ref, live_ref, code_ref, _, hot_a, hot_b, spread, back, rest, count_ref):
+def plan_kernel(info_ref, first_ref, offset_ref, live_ref, code_ref, flag_ref, _, hot_a, hot_b, spread, back, rest, count_ref):
     tiles, lanes = first_ref.shape
     rows = hot_a.shape[1] // 2
     shift = info_ref[0]
@@ -205,9 +205,10 @@
         back[target, :] = hot_rows(column, back.shape[1])
         rest[target, :] = hot_rows(column - back.shape[1], rest.shape[1])
     count_ref[0] = jnp.sum(cross).astype(jnp.int32)
-
-
-def far_kernel(parts, pieces, first, info_ref, count_ref, *refs):
+    count_ref[1] = (jnp.max(flag_ref[...]) > 0).astype(jnp.int32)
+
+
+def far_kernel(parts, first, info_ref, count_ref, *refs):
     refs = list(refs)
 
     def take(number):
@@ -215,69 +216,64 @@
         del refs[:number]
         return taken
 
-    white = [take(parts) for _ in range(pieces)]
-    other = [take(parts) for _ in range(pieces)]
-    common = take(pieces)
-    table = take(pieces)
-    mean_ref, hot_a, hot_b = take(3)
-    (before_ref,) = take(1)
-    acc_ref = take(1)[0]
+    white = take(parts)
+    direct = take(parts)
+    across = take(parts) if first else direct
+    common_ref, table_ref, mean_ref, hot_a, hot_b, before_ref, acc_ref = take(7)
     sent_ref, rest_ref = (None, None) if first else take(2)
-    work_ref, load_sem, store_sem = take(3)
     held = refs
-    rows, piece = other[0][0].shape
+    rows = direct[0].shape[0]
+    step = pl.program_id(0)
     blocks = (count_ref[0] + FAR_BLOCK - 1) // FAR_BLOCK
 
-    def span(block):
-        return pl.ds(pl.multiple_of(block * FAR_BLOCK, FAR_BLOCK), FAR_BLOCK)
-
-    def load(block):
-        return pltpu.make_async_copy(
-            before_ref.at[span(block), :], work_ref.at[span(block), :], load_sem.at[block]
-        )
-
-    def store(block):
-        return pltpu.make_async_copy(
-            work_ref.at[span(block), :], acc_ref.at[span(block), :], store_sem.at[block]
-        )
-
-    if not first:
-        lax.fori_loop(0, blocks, lambda block, _: load(block).start(), None)
-    each = piece // GROUP
-    for number, w_ref in enumerate(held):
-        at, start = number // each, number % each * GROUP
+    for group, w_ref in enumerate(held):
+        start = group * GROUP
         for part in range(parts):
-            w_ref[pl.ds(0, rows), pl.ds(part * GROUP, GROUP)] = white[at][part][
+            w_ref[pl.ds(0, rows), pl.ds(part * GROUP, GROUP)] = white[part][
                 :, pl.ds(start, GROUP)
             ]
-        whiten_into(w_ref, rows, other[at], common[at], mean_ref, start)
+        if first:
+            pl.when(info_ref[1] == 0)(
+                lambda: whiten_into(w_ref, rows, direct, common_ref, mean_ref, start)
+            )
+            pl.when(info_ref[1] != 0)(
+                lambda: whiten_into(w_ref, rows, across, common_ref, mean_ref, start)
+            )
+        else:
+            whiten_into(w_ref, rows, direct, common_ref, mean_ref, start)
 
     def one_block(block, _):
-        target = span(block)
+        target = pl.ds(pl.multiple_of(block * FAR_BLOCK, FAR_BLOCK), FAR_BLOCK)
         gained = None
-        for number, w_ref in enumerate(held):
-            at, start = number // each, number % each * GROUP
-            part = correlate_rows(hot_a[target, :], hot_b[target, :], w_ref, table[at], start)
+        for group, w_ref in enumerate(held):
+            part = correlate_rows(
+                hot_a[target, :], hot_b[target, :], w_ref, table_ref, group * GROUP
+            )
             gained = part if gained is None else gained + part
+
+        @pl.when(step == 0)
+        def _():
+            acc_ref[target, :] = gained if first else before_ref[target, :] + gained
+
+        @pl.when(step > 0)
+        def _():
+            acc_ref[target, :] += gained
+
+    lax.fori_loop(0, blocks, one_block, None)
+
+    @pl.when((step == pl.num_programs(0) - 1) & (not first))
+    def _():
         if first:
-            work_ref[target, :] = gained
-        else:
-            load(block).wait()
-            work_ref[target, :] += gained
-        store(block).start()
-
-    lax.fori_loop(0, blocks, one_block, None)
-    if not first:
+            return
         sent = sent_ref.shape[0]
         used = lax.broadcasted_iota(jnp.int32, (sent + rest_ref.shape[0], 1), 0)
         used = used < blocks * FAR_BLOCK
         for ref, at in ((sent_ref, 0), (rest_ref, sent)):
             ours = slice(at, at + ref.shape[0])
-            ref[...] = jnp.where(used[ours], work_ref[ours, :], 0.0).astype(BF16)
-    lax.fori_loop(0, blocks, lambda block, _: store(block).wait(), None)
-
-
-def prepare_kernel(width, counts, info_ref, x_ref, pairs_ref, live_ref, flat_ref, total_ref, *sent):
+            ref[...] = jnp.where(used[ours], acc_ref[ours, :], 0.0).astype(BF16)
+
+
+def prepare_kernel(width, counts, info_ref, x_ref, pairs_ref, live_ref, flat_ref, total_ref, code_ref, *sent):
     bins = x_ref.shape[3]
     parts = flat_ref.shape[1] // bins
     flat_ref[...] = x_ref[...].reshape(flat_ref.shape)
@@ -288,7 +284,14 @@
     @pl.when(pl.program_id(0) == 0)
     def _():
         total_ref[:, :, pl.ds(0, bins)] = total
-        second = pairs_ref[...][:, 1, :] - info_ref[1]
+        pairs = pairs_ref[...]
+        live = live_ref[...]
+        listed = [pairs[:, 0, :] - info_ref[3], pairs[:, 1, :] - pairs[:, 0, :], live]
+        spare = code_ref.shape[0] - 3 * live.shape[0]
+        if spare:
+            listed.append(jnp.zeros((spare, live.shape[1]), jnp.int32))
+        code_ref[...] = jnp.concatenate(listed, axis=0).astype(F32).astype(BF16)
+        second = pairs[:, 1, :] - info_ref[1]
         crossing = (second >= 0) & (second < info_ref[2]) & (live_ref[...] != 0)
         number = jnp.sum(jnp.where(crossing, 1.0, 0.0))
         flag = jnp.where(number > BACK_ROWS, 1.0, 0.0)
@@ -352,6 +355,7 @@
 def prepare(spectra, info, width, counts, pairs, live):
     rows, windows, two, bins = spectra.shape
     parts = windows * two
+    code_rows = -(-3 * live.shape[0] // 16) * 16
     lanes = [parts * bins] + [parts * pieces * width for pieces in counts]
     blocks = [pl.BlockSpec((ROW_BLOCK, n), lambda i, s: (i, 0)) for n in lanes]
     shapes = [jax.ShapeDtypeStruct((rows, n), BF16) for n in lanes]
@@ -365,9 +369,12 @@
                 whole(pairs.shape),
                 whole(live.shape),
             ],
-            out_specs=blocks[:1] + [whole((windows, two, bins + live.shape[1]))] + blocks[1:],
+            out_specs=blocks[:1]
+            + [whole((windows, two, bins + live.shape[1])), whole((code_rows, live.shape[1]))]
+            + blocks[1:],
         ),
         out_shape=shapes[:1] + [jax.ShapeDtypeStruct((windows, two, bins + live.shape[1]), F32)]
+        + [jax.ShapeDtypeStruct((code_rows, live.shape[1]), BF16)]
         + shapes[1:],
         name="prepare",
         **params(),
@@ -396,8 +403,12 @@
     first_row = me * rows
     half = bins // 2
     fast = [(i, i ^ 1) for i in range(count)]
-    slow = [(i, i + 1) for i in range(1, count - 1, 2)]
-    slow = slow + [(b, a) for a, b in slow]
+
+    def slow_of(*places):
+        up = [(i, i + 1) for i in range(1, count - 1, 2) if i % 4 in places]
+        return up + [(b, a) for a, b in up]
+
+    slow = slow_of(1, 3)
     piece = half // 4
     send_start = (1 - odd) * half
 
@@ -405,25 +416,21 @@
     slots = tiles * tile
     first_rows = pair_channels[:, :, 0] - first_row
     offsets = pair_channels[:, :, 1] - first_row
-    code = jnp.concatenate([first_rows, offsets - first_rows, pair_live], axis=0).astype(BF16)
-    code_rows = -(-3 * tiles // 16) * 16
-    code = jnp.pad(code, ((0, code_rows - 3 * tiles), (0, 0)))
-    far_code = lax.ppermute(code, "row", slow)
-
-    counts = (1, 1, 1, 1)
+    counts = (2, 2)
     far_low = first_row + jnp.where(odd == 1, rows, -rows)
-    flat, total, *chunks = prepare(
+    flat, total, code, *chunks = prepare(
         spectra,
-        jnp.stack([send_start, far_low, jnp.int32(rows)]),
+        jnp.stack([send_start, far_low, jnp.int32(rows), first_row]),
         piece,
         counts,
         jnp.swapaxes(pair_channels, 1, 2),
         pair_live,
     )
+    far_code = lax.ppermute(code, "row", slow)
     if count & (count - 1):
+        far_direct = lax.ppermute(chunks[0], "row", slow_of(1))
         reach = lax.psum(total, "row")
         partner_rows = lax.ppermute(flat, "row", fast)
-        far_rows = [lax.ppermute(behind(chunks[0], reach, far_code), "row", slow)]
     else:
         reach = total
         jump = 1
@@ -435,20 +442,21 @@
             ]
             reach = functools.reduce(jnp.add, others, reach)
             if jump == 1:
+                reach = behind(reach, far_code)
+                far_direct = lax.ppermute(behind(chunks[0], reach), "row", slow_of(1))
                 flat = behind(flat, reach)
                 partner_rows = lax.ppermute(flat, "row", fast)
-                far_rows = [lax.ppermute(behind(chunks[0], reach, far_code), "row", slow)]
             jump *= 4
     common = reach / (rows * count)
-    far_rows.append(lax.ppermute(behind(chunks[1], reach), "row", slow))
-    far_rows.append(lax.ppermute(behind(chunks[2], partner_rows), "row", slow))
+    far_across = lax.ppermute(behind(chunks[0], reach), "row", slow_of(3))
+    far_second = lax.ppermute(behind(chunks[1], reach), "row", slow)
 
     wide = NEAR_GROUPS * GROUP
     near_shift = jnp.where(odd == 1, -rows, rows)
     order = jnp.arange(slots, dtype=jnp.int32).reshape(tiles, tile)
     live_end = jnp.max(jnp.where(pair_live != 0, order + 1, 0))
     near_info = jnp.stack(
-        [near_shift, live_end, odd * (half // wide), (1 - odd) * (half // wide)]
+        [near_shift, live_end, odd * (half // wide)]
     )
     lists = (first_rows, offsets, pair_live)
     list_specs = [whole((tiles, tile))] * 3
@@ -456,19 +464,16 @@
     mean = jnp.asarray(band_mean())
 
     steps = bins // wide
-    share = half // wide
-
-    def near_call(first, before):
-        offset = 2 if first else 3
-
+
+    def near_call():
         def bin_block(j, s):
-            return s[offset] + j
+            return lax.rem(s[2] + j, steps)
 
         return pl.pallas_call(
-            functools.partial(near_kernel, parts, first),
+            functools.partial(near_kernel, parts),
             grid_spec=pltpu.PrefetchScalarGridSpec(
                 num_scalar_prefetch=1,
-                grid=(share,),
+                grid=(steps,),
                 in_specs=[
                     pl.BlockSpec(
                         (rows, wide),
@@ -482,15 +487,14 @@
                     pl.BlockSpec((2, wide, LAGS), lambda j, s: (0, bin_block(j, s), 0)),
                     whole((GROUP, GROUP)),
                 ]
-                + list_specs
-                + [pl.BlockSpec(memory_space=pl.ANY) if first else whole((slots, LAGS))],
+                + list_specs,
                 out_specs=[whole((slots, LAGS))]
-                + [pl.BlockSpec((rows, wide), lambda j, s: (0, j))] * (parts * first),
+                + [pl.BlockSpec((rows, wide), lambda j, s: (0, j))] * parts,
                 scratch_shapes=[pltpu.VMEM((slots, 2 * rows), BF16)] * 2
                 + [pltpu.VMEM((2 * rows, parts * GROUP), BF16)] * NEAR_GROUPS,
             ),
             out_shape=[jax.ShapeDtypeStruct((slots, LAGS), F32)]
-            + [jax.ShapeDtypeStruct((rows, half), BF16)] * (parts * first),
+            + [jax.ShapeDtypeStruct((rows, bins), BF16)] * parts,
             name="near_pairs",
             **params(),
         )(
@@ -501,12 +505,9 @@
             table,
             mean,
             *lists,
-            before,
         )
 
-    near_acc, *white = near_call(True, far_code)
-    far_rows.append(lax.ppermute(behind(chunks[3], near_acc), "row", slow))
-    (near_acc,) = near_call(False, near_acc)
+    near_acc, *white = near_call()
 
     hot_a, hot_b, spread, back_spread, rest_spread, cross_count = pl.pallas_call(
         plan_kernel,
@@ -514,7 +515,8 @@
             num_scalar_prefetch=1,
             grid=(1,),
             in_specs=list_specs
-            + [whole((code_rows, tile))]
+            + [whole(code.shape)]
+            + [pl.BlockSpec((windows, 2, tile), lambda j, s: (0, 0, bins // tile))]
             + [pl.BlockSpec(memory_space=pl.ANY)],
             out_specs=[
                 whole((2 * slots, 2 * rows)),
@@ -531,78 +533,70 @@
             jax.ShapeDtypeStruct((slots, 2 * slots), BF16),
             jax.ShapeDtypeStruct((slots, BACK_ROWS), BF16),
             jax.ShapeDtypeStruct((slots, slots - BACK_ROWS), BF16),
-            jax.ShapeDtypeStruct((1,), jnp.int32),
+            jax.ShapeDtypeStruct((2,), jnp.int32),
         ],
         name="plan",
         **params(),
-    )(-near_shift[None], *lists, far_code, near_acc)
-
-    info = (odd * (half // piece))[None]
-
-    owned = [(k, n, i) for k, n in enumerate(counts) for i in range(n)]
-
-    def far_call(at, first, before):
-        pieces = len(at)
-        own_at = [functools.partial(lambda c, j, s, n: s[0] + c, c) for c in at]
-        specs = (
-            [
-                pl.BlockSpec((rows, piece), functools.partial(lambda n, *i: (0, n), c))
-                for c in at
-                for _ in range(parts)
-            ]
-            + [
-                pl.BlockSpec((rows, piece), functools.partial(lambda n, *i: (0, n), p * owned[c][1] + owned[c][2]))
-                for c in at
-                for p in range(parts)
-            ]
-            + [
-                pl.BlockSpec((windows, 2, piece), functools.partial(lambda f, *i: (0, 0, f(*i)), f))
-                for f in own_at
-            ]
-            + [
-                pl.BlockSpec((2, piece, LAGS), functools.partial(lambda f, *i: (0, f(*i), 0), f))
-                for f in own_at
-            ]
-            + [whole((GROUP, GROUP))]
-            + [whole((2 * slots, 2 * rows))] * 2
-        )
-        operands = (
-            list(white) * pieces
-            + [far_rows[owned[c][0]] for c in at for _ in range(parts)]
-            + [common] * pieces
-            + [table] * pieces
-            + [mean, hot_a, hot_b]
-        )
-        out_specs = [pl.BlockSpec(memory_space=pl.ANY)]
-        out_shape = [jax.ShapeDtypeStruct((2 * slots, LAGS), F32)]
-        specs.append(pl.BlockSpec(memory_space=pl.ANY))
-        operands.append(before)
-        if not first:
-            for back_rows in (BACK_ROWS, slots - BACK_ROWS):
-                out_specs.append(whole((back_rows, LAGS)))
-                out_shape.append(jax.ShapeDtypeStruct((back_rows, LAGS), BF16))
-        most = 2 * slots // FAR_BLOCK
+    )(-near_shift[None], *lists, far_code, common, near_acc)
+
+    across = (((me + 1) // 2) % 2 == 0).astype(jnp.int32)
+    info = jnp.stack([odd * (half // piece), across])
+
+    def far_call(first, arrays, before):
+        pieces = half // piece // 2
+        base = 0 if first else pieces
+        choose = (lambda s, k: s[1] == k) if first else (lambda s, k: True)
+        back_rows = () if first else (BACK_ROWS, slots - BACK_ROWS)
         return pl.pallas_call(
-            functools.partial(far_kernel, parts, pieces, first),
+            functools.partial(far_kernel, parts, first),
             grid_spec=pltpu.PrefetchScalarGridSpec(
                 num_scalar_prefetch=2,
-                grid=(1,),
-                in_specs=specs,
-                out_specs=out_specs,
-                scratch_shapes=[
-                    pltpu.VMEM((2 * slots, LAGS), F32),
-                    pltpu.SemaphoreType.DMA((most,)),
-                    pltpu.SemaphoreType.DMA((most,)),
+                grid=(pieces,),
+                in_specs=[
+                    pl.BlockSpec((rows, piece), lambda j, s, n: (0, base + j)) for _ in range(parts)
                 ]
-                + [pltpu.VMEM((2 * rows, parts * GROUP), BF16)] * (pieces * piece // GROUP),
+                + [
+                    pl.BlockSpec(
+                        (rows, piece),
+                        functools.partial(
+                            lambda k, p, j, s, n: (0, jnp.where(choose(s, k), p * pieces + j, 0)),
+                            k,
+                            p,
+                        ),
+                    )
+                    for k in range(len(arrays))
+                    for p in range(parts)
+                ]
+                + [
+                    pl.BlockSpec((windows, 2, piece), lambda j, s, n: (0, 0, s[0] + base + j)),
+                    pl.BlockSpec((2, piece, LAGS), lambda j, s, n: (0, s[0] + base + j, 0)),
+                    whole((GROUP, GROUP)),
+                    whole((2 * slots, 2 * rows)),
+                    whole((2 * slots, 2 * rows)),
+                    pl.BlockSpec(memory_space=pl.ANY) if first else whole((2 * slots, LAGS)),
+                ],
+                out_specs=[whole((2 * slots, LAGS))] + [whole((n, LAGS)) for n in back_rows],
+                scratch_shapes=[pltpu.VMEM((2 * rows, parts * GROUP), BF16)] * (piece // GROUP),
             ),
-            out_shape=out_shape,
+            out_shape=[jax.ShapeDtypeStruct((2 * slots, LAGS), F32)]
+            + [jax.ShapeDtypeStruct((n, LAGS), BF16) for n in back_rows],
             name="far_pairs",
             **params(),
-        )(info, cross_count, *operands)
-
-    (before,) = far_call((0, 1, 2), True, near_acc)
-    far_acc, theirs, their_rest = far_call((3,), False, before)
+        )(
+            info,
+            cross_count,
+            *white,
+            *[a for a in arrays for _ in range(parts)],
+            common,
+            table,
+            mean,
+            hot_a,
+            hot_b,
+            before,
+        )
+
+    (before,) = far_call(True, (far_direct, far_across), near_acc)
+    far_acc, theirs, their_rest = far_call(False, (far_second,), before)
 
     scale = 1.0 / math.sqrt(bins * windows)
     back = lax.ppermute(theirs, "row", slow)
@@ -647,7 +641,7 @@
         )(gathered, *spread_back)
 
     result = lax.cond(
-        common[0, 0, bins] > 0,
+        cross_count[1] > 0,
         lambda: merge(back_spread, back, rest_spread, lax.ppermute(their_rest, "row", slow)),
         lambda: merge(back_spread, back),
     )

time: 105 us -> 95 us (0.905)
  the two profiles are of different devices: /device:TPU:23 before, /device:TPU:1 now
where the time goes in v3:
time: 95 us; the launch traced here: 94.2 us
  Pallas kernels  51.1 us (54%)
  starting transfers between devices  24.3 us (26%)
  waiting for transfers between devices  6 us (6%)
  other arithmetic  5.97 us (6%)
  local copies, waits for them, and re-layouts  5.89 us (6%)
    pallas_call x1, Pallas kernels, near_call(): pl.pallas_call(functools.partial(near_kernel, parts), grid_spec=pltpu.Pre...  17.2 us
    pallas_call x2, Pallas kernels, far_call(): pl.pallas_call(functools.partial(far_kernel, parts, first), grid_spec=plt...  16.4 us
    pallas_call x1, Pallas kernels, prepare(): pl.pallas_call(functools.partial(prepare_kernel, width, counts), grid_spe...  8.41 us
    ppermute x6, starting transfers between devices, body(): lax.ppermute(reach, 'row', [(i, i ^ k) for i in range(count)])  6.45 us
    unnamed x23, local copies, waits for them, and re-layouts  5.3 us
    ppermute x1, starting transfers between devices, body(): far_second = lax.ppermute(behind(chunks[1], reach), 'row', slow)  4.76 us
    pallas_call x1, Pallas kernels, body(): pl.pallas_call(plan_kernel, grid_spec=pltpu.PrefetchScalarGridSpec(num_sc...  4.54 us
    ppermute x1, starting transfers between devices, body(): back = lax.ppermute(theirs, 'row', slow)  4.28 us
  transfers between devices with their start and end apart: 12, of which 3 were waited for; matrix products, arithmetic and copies ran while one was open for 7% of the time, Pallas kernels for 36%

profile of v3, /device:TPU:1, one launch (start us, length us, event | category | flops | bytes accessed | tf_op | source)
XLA Modules:
  0.0 94.2 jit_solution(9299075642527739634)
XLA Ops:
  0.0 0.6 pad_add_fusion.info_ref
  0.6 8.4 %prepare.1 = (bf16[128,16384]{1,0:T(8,128)(2,1)}, f32[2,2,4224]{2,1,0:T(2,128)}, bf16[16,128]{1,0:T(8,128)(2,1)}, bf16[128,4096]{1,0:T(8,128)(2,1)}, bf16[128,4096]{1,0:T(8,128)(2,1)}) custom-call(s32[4]{0:T(128)} %pad_add_fusion.info_ref, bf16[128,2,2,4096]{3,2,1,0:T(2,128)(2,1)} %x_ref.1, s32[4,2,128]{2,1,0:T(2,128)} %bitcast.20, s32[4,128]{1,0:T(4,128)} %live_ref.3), custom_call_target="tpu_custom_call" | custom-call | flops 1000 | bytes 1000 | tf_op jit(solution)/shard_map/prepare/pallas_call | solution.py:362
  9.1 2.7 %collective-permute-start.3 = (f32[2,2,4224]{2,1,0:T(2,128)}, f32[2,2,4224]{2,1,0:T(2,128)S(1)}, u32[]{:S(2)}, u32[]{:S(2)}) collective-permute-start(f32[2,2,4224]{2,1,0:T(2,128)} %get-tuple-element.53), channel_id=1, source_target_pairs={{0,2},{1,3},{2,0},{3,1},{4,6},{5,7},{6,4},{7,5},{8,10},{9,11},{10,... | collective-permute-start | bytes 202760 | tf_op jit(solution)/shard_map/ppermute | solution.py:439
  11.9 3.6 %collective-permute-start.1 = (bf16[16,128]{1,0:T(8,128)(2,1)}, bf16[16,128]{1,0:T(8,128)(2,1)S(1)}, u32[]{:S(2)}, u32[]{:S(2)}) collective-permute-start(bf16[16,128]{1,0:T(8,128)(2,1)} %get-tuple-element.52), channel_id=1, source_target_pairs={{1,2},{3,4},{5,6},{7,8},{9,10},{11,12},{13,14},{2,1},{4,3},{6,5},{... | collective-permute-start | bytes 12296 | tf_op jit(solution)/shard_map/ppermute | solution.py:429
  15.5 0.7 collective-permute-done.4
  16.2 1.6 %add_add_fusion.1.refs_0_ = f32[2,2,4224]{2,1,0:T(2,128)} fusion(f32[2,2,4224]{2,1,0:T(2,128)S(1)} %collective-permute-done.4, f32[2,2,4224]{2,1,0:T(2,128)S(1)} %collective-permute-done.3, f32[2,2,4224]{2,1,0:T(2,128)} %get-tuple-element.53, f32[2,2,4224]{2,1,0:T(2,128)S(1)} %collective-permute-done.2), kind=kLoop, calls=%fused_computation.1 | loop fusion | flops 50688 | bytes 337920 | tf_op jit(solution)/shard_map/add | solution.py:443
  17.8 0.6 copy-done.9
  19.2 1.3 %collective-permute-start.5 = (f32[2,2,4224]{2,1,0:T(2,128)S(1)}, f32[2,2,4224]{2,1,0:T(2,128)S(1)}, u32[]{:S(2)}, u32[]{:S(2)}) collective-permute-start(f32[2,2,4224]{2,1,0:T(2,128)S(1)} %copy-done.4), channel_id=1, source_target_pairs={{0,4},{1,5},{2,6},{3,7},{4,0},{5,1},{6,2},{7,3},{8,12},{9,13},{10,... | collective-permute-start | bytes 202760 | tf_op jit(solution)/shard_map/ppermute | solution.py:439
  20.5 2.3 %collective-permute-start.6 = (f32[2,2,4224]{2,1,0:T(2,128)S(1)}, f32[2,2,4224]{2,1,0:T(2,128)S(1)}, u32[]{:S(2)}, u32[]{:S(2)}) collective-permute-start(f32[2,2,4224]{2,1,0:T(2,128)S(1)} %copy-done.4), channel_id=1, source_target_pairs={{0,8},{1,9},{2,10},{3,11},{4,12},{5,13},{6,14},{7,15},{8,0},{9,1},... | collective-permute-start | bytes 202760 | tf_op jit(solution)/shard_map/ppermute | solution.py:439
  22.9 1.0 %copy.21.refs_0_ = bf16[128,4096]{1,0:T(8,128)(2,1)} copy(bf16[128,4096]{1,0:T(8,128)(2,1)S(1)} %copy-done.3) | data formatting | bytes 2097152
  23.9 4.1 %collective-permute-start.10 = (bf16[128,4096]{1,0:T(8,128)(2,1)}, bf16[128,4096]{1,0:T(8,128)(2,1)S(1)}, u32[]{:S(2)}, u32[]{:S(2)}) collective-permute-start(bf16[128,4096]{1,0:T(8,128)(2,1)} %behind.8), channel_id=1, source_target_pairs={{1,2},{5,6},{9,10},{13,14},{2,1},{6,5},{10,9},{14,13},{17,18},{21,... | collective-permute-start | bytes 3145736 | tf_op jit(solution)/shard_map/ppermute | solution.py:446
  28.0 0.8 broadcast_multiply_fusion
  28.7 0.7 collective-permute-start.11
  29.5 4.8 %collective-permute-start.9 = (bf16[128,4096]{1,0:T(8,128)(2,1)}, bf16[128,4096]{1,0:T(8,128)(2,1)S(1)}, u32[]{:S(2)}, u32[]{:S(2)}) collective-permute-start(bf16[128,4096]{1,0:T(8,128)(2,1)} %behind.7), channel_id=1, source_target_pairs={{1,2},{3,4},{5,6},{7,8},{9,10},{11,12},{13,14},{2,1},{4,3},{6,5},{... | collective-permute-start | bytes 3145736 | tf_op jit(solution)/shard_map/ppermute | solution.py:452
  34.3 0.6 select_reduce_fusion
  34.9 1.1 %pad_add_fusion.1.info_ref = s32[3]{0:T(128)} fusion(s32[1]{0:T(128)} %bitcast.10, s32[1]{0:T(128)} %bitcast.9, s32[1]{0:T(128)} %bitcast.2), kind=kLoop, calls=%fused_computation.7 | loop fusion | flops 6 | bytes 24 | tf_op jit(solution)/shard_map/stack | solution.py:458
  36.1 0.6 pad_add_fusion.2.info_ref
  36.7 0.6 subtract_bitcast_fusion
  37.3 17.2 %near_pairs.1 = (f32[512,512]{1,0:T(8,128)}, bf16[128,4096]{1,0:T(8,128)(2,1)}, bf16[128,4096]{1,0:T(8,128)(2,1)}, bf16[128,4096]{1,0:T(8,128)(2,1)}, bf16[128,4096]{1,0:T(8,128)(2,1)}) custom-call(s32[3]{0:T(128)} %pad_add_fusion.1.info_ref, bf16[128,16384]{1,0:T(8,128)(2,1)} %behind.6.refs_0_.refs_1_.refs_2_.refs_3_, ...), custom_call_target="tpu_custom_call" | custom-call | flops 1000 | bytes 1000 | tf_op jit(solution)/shard_map/near_pairs/pallas_call | solution.py:472
  54.5 4.5 %plan.1 = (bf16[1024,256]{1,0:T(8,128)(2,1)}, bf16[1024,256]{1,0:T(8,128)(2,1)}, bf16[512,1024]{1,0:T(8,128)(2,1)}, bf16[512,160]{1,0:T(8,128)(2,1)S(1)}, bf16[512,352]{1,0:T(8,128)(2,1)S(1)}, /*index=5*/s32[2]{0:T(128)}) custom-call(s32[1]{0:T(128)S(6)} %neg.3.info_ref, s32[4,128]{1,0:T(4,128)} %get-tuple-element.77.refs_11_.first_ref, ...), custom_call_target="tpu_custom_call" | custom-call | flops 1000 | bytes 1000 | tf_op jit(solution)/shard_map/plan/pallas_call | solution.py:512
  59.1 3.4 %collective-permute-done.10.refs_4_.refs_5_.refs_6_.refs_7_ = bf16[128,4096]{1,0:T(8,128)(2,1)S(1)} collective-permute-done((bf16[128,4096]{1,0:T(8,128)(2,1)}, bf16[128,4096]{1,0:T(8,128)(2,1)S(1)}, u32[]{:S(2)}, u32[]{:S(2)}) %collective-permute-start.10) | collective-permute-done | bytes 1048608 | tf_op jit(solution)/shard_map/ppermute | solution.py:446
  62.5 1.0 %copy-done = bf16[128,4096]{1,0:T(8,128)(2,1)} copy-done((bf16[128,4096]{1,0:T(8,128)(2,1)}, bf16[128,4096]{1,0:T(8,128)(2,1)S(1)}, u32[]{:S(2)}) %copy-start) | copy-done | bytes 1048600
  63.8 8.0 %far_pairs.2.refs_13_ = f32[1024,512]{1,0:T(8,128)} custom-call(s32[2]{0:T(128)} %pad_add_fusion.2.info_ref, s32[2]{0:T(128)} %get-tuple-element.56.count_ref, bf16[128,4096]{1,0:T(8,128)(2,1)} %get-tuple-element.58.refs_0_, bf16[128,4096]{1,0:T(8,128)(2,1)} %get-tuple-element.59.refs_1_, bf16[128,4096]{1,0:T(8,128)(2,1)} %get-tuple-element.60.refs_2_, ...), custom_call_target="tpu_custom_call" | custom-call | flops 1000 | bytes 1000 | tf_op jit(solution)/shard_map/far_pairs/pallas_call | solution.py:550
  71.8 1.9 %collective-permute-done.9.refs_4_.refs_5_.refs_6_.refs_7_ = bf16[128,4096]{1,0:T(8,128)(2,1)S(1)} collective-permute-done((bf16[128,4096]{1,0:T(8,128)(2,1)}, bf16[128,4096]{1,0:T(8,128)(2,1)S(1)}, u32[]{:S(2)}, u32[]{:S(2)}) %collective-permute-start.9) | collective-permute-done | bytes 1048608 | tf_op jit(solution)/shard_map/ppermute | solution.py:452
  73.7 1.0 %copy-done.2 = bf16[128,4096]{1,0:T(8,128)(2,1)} copy-done((bf16[128,4096]{1,0:T(8,128)(2,1)}, bf16[128,4096]{1,0:T(8,128)(2,1)S(1)}, u32[]{:S(2)}) %copy-start.2) | copy-done | bytes 1048600
  74.7 8.4 %far_pairs.3 = (f32[1024,512]{1,0:T(8,128)}, bf16[160,512]{1,0:T(8,128)(2,1)}, bf16[352,512]{1,0:T(8,128)(2,1)S(1)}) custom-call(s32[2]{0:T(128)} %pad_add_fusion.2.info_ref, s32[2]{0:T(128)} %get-tuple-element.56.count_ref, bf16[128,4096]{1,0:T(8,128)(2,1)} %get-tuple-element.58.refs_0_, bf16[128,4096]{1,0:T(8,128)(2,1)} %get-tuple-element.59.refs_1_, ...), custom_call_target="tpu_custom_call" | custom-call | flops 1000 | bytes 1000 | tf_op jit(solution)/shard_map/far_pairs/pallas_call | solution.py:550
  83.1 4.3 %collective-permute-start.12 = (bf16[160,512]{1,0:T(8,128)(2,1)}, bf16[160,512]{1,0:T(8,128)(2,1)S(1)}, u32[]{:S(2)}, u32[]{:S(2)}) collective-permute-start(bf16[160,512]{1,0:T(8,128)(2,1)} %get-tuple-element.68), channel_id=1, source_target_pairs={{1,2},{3,4},{5,6},{7,8},{9,10},{11,12},{13,14},{2,1},{4,3},{6,5},{... | collective-permute-start | bytes 491528 | tf_op jit(solution)/shard_map/ppermute | solution.py:602
  87.4 3.8 %gather.1 = f32[512,512]{1,0:T(8,128)S(1)} custom-call(s32[2]{0:T(128)} %get-tuple-element.56.count_ref, f32[512,512]{1,0:T(8,128)} %get-tuple-element.55._.refs_17_.near_ref, bf16[512,1024]{1,0:T(8,128)(2,1)} %get-tuple-element.57.spread_ref, f32[1024,512]{1,0:T(8,128)} %get-tuple-element.66.far_ref), custom_call_target="tpu_custom_call" | custom-call | flops 1000 | bytes 1000 | tf_op jit(solution)/shard_map/gather/pallas_call | solution.py:603
  91.2 0.6 slice.11
  92.4 0.8 conditional.1
  92.4 0.7 merge.2
  93.2 1.0 %copy-done.6 = f32[4,128,512]{2,1,0:T(8,128)} copy-done((f32[4,128,512]{2,1,0:T(8,128)}, f32[4,128,512]{2,1,0:T(8,128)S(1)}, u32[]{:S(2)}) %copy-start.6) | copy-done | bytes 1048600
  (37 shorter events, 1.4 us)
Async XLA Ops:
  9.1 6.5 %collective-permute-start.2 = (f32[2,2,4224]{2,1,0:T(2,128)}, f32[2,2,4224]{2,1,0:T(2,128)S(1)}, u32[]{:S(2)}, u32[]{:S(2)}) collective-permute-start(f32[2,2,4224]{2,1,0:T(2,128)} %get-tuple-element.53), channel_id=1, source_target_pairs={{0,1},{1,0},{2,3},{3,2},{4,5},{5,4},{6,7},{7,6},{8,9},{9,8},{10,11... | collective-permute-start | bytes 202760 | tf_op jit(solution)/shard_map/ppermute | solution.py:439
  9.1 6.4 %collective-permute-start.3 = (f32[2,2,4224]{2,1,0:T(2,128)}, f32[2,2,4224]{2,1,0:T(2,128)S(1)}, u32[]{:S(2)}, u32[]{:S(2)}) collective-permute-start(f32[2,2,4224]{2,1,0:T(2,128)} %get-tuple-element.53), channel_id=1, source_target_pairs={{0,2},{1,3},{2,0},{3,1},{4,6},{5,7},{6,4},{7,5},{8,10},{9,11},{10,... | collective-permute-start | bytes 202760 | tf_op jit(solution)/shard_map/ppermute | solution.py:439
  11.8 4.3 %collective-permute-start.4 = (f32[2,2,4224]{2,1,0:T(2,128)}, f32[2,2,4224]{2,1,0:T(2,128)S(1)}, u32[]{:S(2)}, u32[]{:S(2)}) collective-permute-start(f32[2,2,4224]{2,1,0:T(2,128)} %get-tuple-element.53), channel_id=1, source_target_pairs={{0,3},{1,2},{2,1},{3,0},{4,7},{5,6},{6,5},{7,4},{8,11},{9,10},{10,... | collective-permute-start | bytes 202760 | tf_op jit(solution)/shard_map/ppermute | solution.py:439
  11.9 5.9 %collective-permute-start.1 = (bf16[16,128]{1,0:T(8,128)(2,1)}, bf16[16,128]{1,0:T(8,128)(2,1)S(1)}, u32[]{:S(2)}, u32[]{:S(2)}) collective-permute-start(bf16[16,128]{1,0:T(8,128)(2,1)} %get-tuple-element.52), channel_id=1, source_target_pairs={{1,2},{3,4},{5,6},{7,8},{9,10},{11,12},{13,14},{2,1},{4,3},{6,5},{... | collective-permute-start | bytes 12296 | tf_op jit(solution)/shard_map/ppermute | solution.py:429
  17.8 0.6 copy-start.9
  18.4 0.9 copy-start.4
  18.4 4.5 %copy-start.3 = (bf16[128,4096]{1,0:T(8,128)(2,1)S(1)}, bf16[128,4096]{1,0:T(8,128)(2,1)}, u32[]{:S(2)}) copy-start(bf16[128,4096]{1,0:T(8,128)(2,1)} %get-tuple-element.65.refs_0_) | copy-start | bytes 3145732
  18.4 9.6 %copy-start.5 = (f32[2,2,4224]{2,1,0:T(2,128)S(1)}, f32[2,2,4224]{2,1,0:T(2,128)}, u32[]{:S(2)}) copy-start(f32[2,2,4224]{2,1,0:T(2,128)} %behind.5.refs_1_) | copy-start | bytes 202756
  18.4 18.9 %collective-permute-start.8 = (bf16[128,16384]{1,0:T(8,128)(2,1)}, bf16[128,16384]{1,0:T(8,128)(2,1)}, u32[]{:S(2)}, u32[]{:S(2)}) collective-permute-start(bf16[128,16384]{1,0:T(8,128)(2,1)} %behind.6.refs_0_.refs_1_.refs_2_.refs_3_), channel_id=1, source_target_pairs={{0,1},{1,0},{2,3},{3,2},{4,5},{5,4},{6,7},{7,6},{8,9},{9,8},{10,11... | collective-permute-start | bytes 12582920 | tf_op jit(solution)/shard_map/ppermute | solution.py:448
  19.2 8.7 %collective-permute-start.5 = (f32[2,2,4224]{2,1,0:T(2,128)S(1)}, f32[2,2,4224]{2,1,0:T(2,128)S(1)}, u32[]{:S(2)}, u32[]{:S(2)}) collective-permute-start(f32[2,2,4224]{2,1,0:T(2,128)S(1)} %copy-done.4), channel_id=1, source_target_pairs={{0,4},{1,5},{2,6},{3,7},{4,0},{5,1},{6,2},{7,3},{8,12},{9,13},{10,... | collective-permute-start | bytes 202760 | tf_op jit(solution)/shard_map/ppermute | solution.py:439
  20.5 7.4 %collective-permute-start.6 = (f32[2,2,4224]{2,1,0:T(2,128)S(1)}, f32[2,2,4224]{2,1,0:T(2,128)S(1)}, u32[]{:S(2)}, u32[]{:S(2)}) collective-permute-start(f32[2,2,4224]{2,1,0:T(2,128)S(1)} %copy-done.4), channel_id=1, source_target_pairs={{0,8},{1,9},{2,10},{3,11},{4,12},{5,13},{6,14},{7,15},{8,0},{9,1},... | collective-permute-start | bytes 202760 | tf_op jit(solution)/shard_map/ppermute | solution.py:439
  22.9 5.1 %collective-permute-start.7 = (f32[2,2,4224]{2,1,0:T(2,128)S(1)}, f32[2,2,4224]{2,1,0:T(2,128)S(1)}, u32[]{:S(2)}, u32[]{:S(2)}) collective-permute-start(f32[2,2,4224]{2,1,0:T(2,128)S(1)} %copy-done.4), channel_id=1, source_target_pairs={{0,12},{1,13},{2,14},{3,15},{4,8},{5,9},{6,10},{7,11},{8,4},{9,5},... | collective-permute-start | bytes 202760 | tf_op jit(solution)/shard_map/ppermute | solution.py:439
  22.9 11.4 %copy-start.8 = (s32[4,128]{1,0:T(4,128)S(1)}, s32[4,128]{1,0:T(4,128)}, u32[]{:S(2)}) copy-start(s32[4,128]{1,0:T(4,128)} %live_ref.3) | copy-start | bytes 6148
  22.9 13.8 %copy-start.10 = (s32[4,128,2]{1,2,0:T(2,128)S(1)}, s32[4,128,2]{1,2,0:T(2,128)}, u32[]{:S(2)}) copy-start(s32[4,128,2]{1,2,0:T(2,128)} %param.8) | copy-start | bytes 12292
  23.9 38.6 %collective-permute-start.10 = (bf16[128,4096]{1,0:T(8,128)(2,1)}, bf16[128,4096]{1,0:T(8,128)(2,1)S(1)}, u32[]{:S(2)}, u32[]{:S(2)}) collective-permute-start(bf16[128,4096]{1,0:T(8,128)(2,1)} %behind.8), channel_id=1, source_target_pairs={{1,2},{5,6},{9,10},{13,14},{2,1},{6,5},{10,9},{14,13},{17,18},{21,... | collective-permute-start | bytes 3145736 | tf_op jit(solution)/shard_map/ppermute | solution.py:446
  28.7 33.7 %collective-permute-start.11 = (bf16[128,4096]{1,0:T(8,128)(2,1)}, bf16[128,4096]{1,0:T(8,128)(2,1)S(1)}, u32[]{:S(2)}, u32[]{:S(2)}) collective-permute-start(bf16[128,4096]{1,0:T(8,128)(2,1)} %behind.9), channel_id=1, source_target_pairs={{3,4},{7,8},{11,12},{4,3},{8,7},{12,11},{19,20},{23,24},{27,28},{2... | collective-permute-start | bytes 3145736 | tf_op jit(solution)/shard_map/ppermute | solution.py:451
  29.5 44.2 %collective-permute-start.9 = (bf16[128,4096]{1,0:T(8,128)(2,1)}, bf16[128,4096]{1,0:T(8,128)(2,1)S(1)}, u32[]{:S(2)}, u32[]{:S(2)}) collective-permute-start(bf16[128,4096]{1,0:T(8,128)(2,1)} %behind.7), channel_id=1, source_target_pairs={{1,2},{3,4},{5,6},{7,8},{9,10},{11,12},{13,14},{2,1},{4,3},{6,5},{... | collective-permute-start | bytes 3145736 | tf_op jit(solution)/shard_map/ppermute | solution.py:452
  62.5 1.0 %copy-start = (bf16[128,4096]{1,0:T(8,128)(2,1)}, bf16[128,4096]{1,0:T(8,128)(2,1)S(1)}, u32[]{:S(2)}) copy-start(bf16[128,4096]{1,0:T(8,128)(2,1)S(1)} %collective-permute-done.10.refs_4_.refs_5_.refs_6_.refs_7_) | copy-start | bytes 3145732
  62.5 1.3 %copy-start.1 = (bf16[128,4096]{1,0:T(8,128)(2,1)}, bf16[128,4096]{1,0:T(8,128)(2,1)S(1)}, u32[]{:S(2)}) copy-start(bf16[128,4096]{1,0:T(8,128)(2,1)S(1)} %collective-permute-done.11.refs_8_.refs_9_.refs_10_.refs_11_) | copy-start | bytes 3145732
  73.7 1.0 %copy-start.2 = (bf16[128,4096]{1,0:T(8,128)(2,1)}, bf16[128,4096]{1,0:T(8,128)(2,1)S(1)}, u32[]{:S(2)}) copy-start(bf16[128,4096]{1,0:T(8,128)(2,1)S(1)} %collective-permute-done.9.refs_4_.refs_5_.refs_6_.refs_7_) | copy-start | bytes 3145732
  83.1 8.1 %copy-start.11 = (s32[2]{0:T(128)S(1)}, s32[2]{0:T(128)}, u32[]{:S(2)}) copy-start(s32[2]{0:T(128)} %get-tuple-element.56.count_ref) | copy-start | bytes 28
  83.1 9.3 %collective-permute-start.12 = (bf16[160,512]{1,0:T(8,128)(2,1)}, bf16[160,512]{1,0:T(8,128)(2,1)S(1)}, u32[]{:S(2)}, u32[]{:S(2)}) collective-permute-start(bf16[160,512]{1,0:T(8,128)(2,1)} %get-tuple-element.68), channel_id=1, source_target_pairs={{1,2},{3,4},{5,6},{7,8},{9,10},{11,12},{13,14},{2,1},{4,3},{6,5},{... | collective-permute-start | bytes 491528 | tf_op jit(solution)/shard_map/ppermute | solution.py:602
  93.2 1.0 %copy-start.6 = (f32[4,128,512]{2,1,0:T(8,128)}, f32[4,128,512]{2,1,0:T(8,128)S(1)}, u32[]{:S(2)}) copy-start(f32[4,128,512]{2,1,0:T(8,128)S(1)} %get-tuple-element.90) | copy-start | bytes 3145732

commit v4 on v3

--- a/solution.py
+++ b/solution.py
@@ -17,7 +17,6 @@
 BACK_ROWS = 160
 ROW_BLOCK = 16
 TINY = 1e-37
-VMEM_BYTES = 56 * 1024 * 1024
 F32 = jnp.float32
 BF16 = jnp.bfloat16
 
@@ -108,22 +107,29 @@
         return taken
 
     own, other = take(parts), take(parts)
-    common_ref, table_ref, mean_ref, first_ref, offset_ref, live_ref = take(6)
+    common_ref, table_ref, mean_ref, pairs_ref, live_ref, flag_ref, _ = take(7)
     (acc_ref,) = take(1)
     white = take(parts)
+    (exceeds_ref,) = take(1)
     hot_a, hot_b, *held = refs
     rows = own[0].shape[0]
 
     @pl.when(pl.program_id(0) == 0)
     def _():
         acc_ref[...] = jnp.zeros_like(acc_ref)
-        shift = info_ref[0]
-        offset = offset_ref[...]
+        exceeds_ref[0] = (jnp.max(flag_ref[...]) > 0).astype(jnp.int32)
+        lists = live_ref.shape
+        order = lax.broadcasted_iota(jnp.int32, lists, 0) * lists[1]
+        order = (order + lax.broadcasted_iota(jnp.int32, lists, 1) + 1).astype(F32)
+        exceeds_ref[1] = jnp.max(jnp.where(live_ref[...] != 0, order, 0.0)).astype(jnp.int32)
+        shift = info_ref[4]
+        pairs = pairs_ref[...] - info_ref[3]
+        offset = pairs[:, 1, :]
         live = live_ref[...] != 0
         inside = (offset >= 0) & (offset < rows)
         beside = (offset >= shift) & (offset < shift + rows)
         place = jnp.where(inside, offset, jnp.where(beside, offset - shift + rows, -1))
-        fill_hot(jnp.where(live, first_ref[...], -1), hot_a)
+        fill_hot(jnp.where(live, pairs[:, 0, :], -1), hot_a)
         fill_hot(jnp.where(live, place, -1), hot_b)
 
     def prepare(group):
@@ -147,22 +153,23 @@
             )
 
     total = hot_a.shape[0]
-    pl.when(info_ref[1] <= total // 2)(lambda: run(total // 2))
-    pl.when(info_ref[1] > total // 2)(lambda: run(total))
-
-
-def plan_kernel(info_ref, first_ref, offset_ref, live_ref, code_ref, flag_ref, _, hot_a, hot_b, spread, back, rest, count_ref):
-    tiles, lanes = first_ref.shape
+    pl.when(exceeds_ref[1] <= total // 2)(lambda: run(total // 2))
+    pl.when(exceeds_ref[1] > total // 2)(lambda: run(total))
+
+
+def plan_kernel(info_ref, pairs_ref, live_ref, code_ref, _, hot_a, hot_b, spread, back, rest, count_ref):
+    tiles, lanes = live_ref.shape
     rows = hot_a.shape[1] // 2
-    shift = info_ref[0]
+    shift = -info_ref[4]
+    pairs = pairs_ref[...] - info_ref[3]
     code = code_ref[...].astype(F32).astype(jnp.int32)
     far_a = code[0:tiles]
     far_b = far_a + code[tiles : 2 * tiles] + shift
     theirs = (far_b >= 0) & (far_b < rows) & (code[2 * tiles : 3 * tiles] != 0)
-    offset = offset_ref[...]
+    offset = pairs[:, 1, :]
     owns = (offset >= shift) & (offset < shift + rows) & (live_ref[...] != 0)
     cross = jnp.concatenate([theirs.astype(F32), owns.astype(F32)], axis=0)
-    values_a = jnp.concatenate([far_a + rows, first_ref[...]], axis=0)
+    values_a = jnp.concatenate([far_a + rows, pairs[:, 0, :]], axis=0)
     values_b = jnp.concatenate([far_b, offset - shift + rows], axis=0)
     square = (lanes, lanes)
     row = lax.broadcasted_iota(jnp.int32, square, 0)
@@ -205,7 +212,6 @@
         back[target, :] = hot_rows(column, back.shape[1])
         rest[target, :] = hot_rows(column - back.shape[1], rest.shape[1])
     count_ref[0] = jnp.sum(cross).astype(jnp.int32)
-    count_ref[1] = (jnp.max(flag_ref[...]) > 0).astype(jnp.int32)
 
 
 def far_kernel(parts, first, info_ref, count_ref, *refs):
@@ -221,10 +227,31 @@
     across = take(parts) if first else direct
     common_ref, table_ref, mean_ref, hot_a, hot_b, before_ref, acc_ref = take(7)
     sent_ref, rest_ref = (None, None) if first else take(2)
+    work_ref, load_sem, store_sem = take(3)
     held = refs
     rows = direct[0].shape[0]
     step = pl.program_id(0)
+    last = pl.num_programs(0) - 1
     blocks = (count_ref[0] + FAR_BLOCK - 1) // FAR_BLOCK
+
+    def span(block):
+        return pl.ds(pl.multiple_of(block * FAR_BLOCK, FAR_BLOCK), FAR_BLOCK)
+
+    def load(block):
+        return pltpu.make_async_copy(
+            before_ref.at[span(block), :], work_ref.at[span(block), :], load_sem.at[block]
+        )
+
+    def store(block):
+        return pltpu.make_async_copy(
+            work_ref.at[span(block), :], acc_ref.at[span(block), :], store_sem.at[block]
+        )
+
+    if not first:
+
+        @pl.when(step == 0)
+        def _():
+            lax.fori_loop(0, blocks, lambda block, _: load(block).start(), None)
 
     for group, w_ref in enumerate(held):
         start = group * GROUP
@@ -233,17 +260,17 @@
                 :, pl.ds(start, GROUP)
             ]
         if first:
-            pl.when(info_ref[1] == 0)(
+            pl.when(info_ref[7] == 0)(
                 lambda: whiten_into(w_ref, rows, direct, common_ref, mean_ref, start)
             )
-            pl.when(info_ref[1] != 0)(
+            pl.when(info_ref[7] != 0)(
                 lambda: whiten_into(w_ref, rows, across, common_ref, mean_ref, start)
             )
         else:
             whiten_into(w_ref, rows, direct, common_ref, mean_ref, start)
 
     def one_block(block, _):
-        target = pl.ds(pl.multiple_of(block * FAR_BLOCK, FAR_BLOCK), FAR_BLOCK)
+        target = span(block)
         gained = None
         for group, w_ref in enumerate(held):
             part = correlate_rows(
@@ -253,16 +280,23 @@
 
         @pl.when(step == 0)
         def _():
-            acc_ref[target, :] = gained if first else before_ref[target, :] + gained
+            if first:
+                work_ref[target, :] = gained
+            else:
+                load(block).wait()
+                work_ref[target, :] += gained
 
         @pl.when(step > 0)
         def _():
-            acc_ref[target, :] += gained
+            work_ref[target, :] += gained
+
+        pl.when(step == last)(lambda: store(block).start())
 
     lax.fori_loop(0, blocks, one_block, None)
 
-    @pl.when((step == pl.num_programs(0) - 1) & (not first))
+    @pl.when(step == last)
     def _():
+        lax.fori_loop(0, blocks, lambda block, _: store(block).wait(), None)
         if first:
             return
         sent = sent_ref.shape[0]
@@ -270,7 +304,7 @@
         used = used < blocks * FAR_BLOCK
         for ref, at in ((sent_ref, 0), (rest_ref, sent)):
             ours = slice(at, at + ref.shape[0])
-            ref[...] = jnp.where(used[ours], acc_ref[ours, :], 0.0).astype(BF16)
+            ref[...] = jnp.where(used[ours], work_ref[ours, :], 0.0).astype(BF16)
 
 
 def prepare_kernel(width, counts, info_ref, x_ref, pairs_ref, live_ref, flat_ref, total_ref, code_ref, *sent):
@@ -341,9 +375,9 @@
     refs[-1][...] = total
 
 
-def params():
+def params(mebibytes=56):
     return dict(
-        compiler_params=pltpu.CompilerParams(vmem_limit_bytes=VMEM_BYTES),
+        compiler_params=pltpu.CompilerParams(vmem_limit_bytes=mebibytes * 1024 * 1024),
         cost_estimate=pl.CostEstimate(flops=1000, bytes_accessed=1000, transcendentals=0),
     )
 
@@ -414,21 +448,36 @@
 
     tiles, tile = pair_live.shape
     slots = tiles * tile
-    first_rows = pair_channels[:, :, 0] - first_row
-    offsets = pair_channels[:, :, 1] - first_row
     counts = (2, 2)
+    wide = NEAR_GROUPS * GROUP
+    near_shift = jnp.where(odd == 1, -rows, rows)
+    across = (((me + 1) // 2) % 2 == 0).astype(jnp.int32)
+    pairs = jnp.swapaxes(pair_channels, 1, 2)
     far_low = first_row + jnp.where(odd == 1, rows, -rows)
+    facts = jnp.stack(
+        [
+            send_start,
+            far_low,
+            jnp.int32(rows),
+            first_row,
+            near_shift,
+            odd * (half // wide),
+            odd * (half // piece),
+            across,
+        ]
+    )
     flat, total, code, *chunks = prepare(
         spectra,
-        jnp.stack([send_start, far_low, jnp.int32(rows), first_row]),
+        facts,
         piece,
         counts,
-        jnp.swapaxes(pair_channels, 1, 2),
+        pairs,
         pair_live,
     )
     far_code = lax.ppermute(code, "row", slow)
     if count & (count - 1):
         far_direct = lax.ppermute(chunks[0], "row", slow_of(1))
+        round_one = total
         reach = lax.psum(total, "row")
         partner_rows = lax.ppermute(flat, "row", fast)
     else:
@@ -442,7 +491,7 @@
             ]
             reach = functools.reduce(jnp.add, others, reach)
             if jump == 1:
-                reach = behind(reach, far_code)
+                reach = round_one = behind(reach, far_code)
                 far_direct = lax.ppermute(behind(chunks[0], reach), "row", slow_of(1))
                 flat = behind(flat, reach)
                 partner_rows = lax.ppermute(flat, "row", fast)
@@ -451,15 +500,37 @@
     far_across = lax.ppermute(behind(chunks[0], reach), "row", slow_of(3))
     far_second = lax.ppermute(behind(chunks[1], reach), "row", slow)
 
-    wide = NEAR_GROUPS * GROUP
-    near_shift = jnp.where(odd == 1, -rows, rows)
-    order = jnp.arange(slots, dtype=jnp.int32).reshape(tiles, tile)
-    live_end = jnp.max(jnp.where(pair_live != 0, order + 1, 0))
-    near_info = jnp.stack(
-        [near_shift, live_end, odd * (half // wide)]
-    )
-    lists = (first_rows, offsets, pair_live)
-    list_specs = [whole((tiles, tile))] * 3
+    lists = (pairs, pair_live)
+    list_specs = [whole(pairs.shape), whole(pair_live.shape)]
+    hot_a, hot_b, spread, back_spread, rest_spread, cross_count = pl.pallas_call(
+        plan_kernel,
+        grid_spec=pltpu.PrefetchScalarGridSpec(
+            num_scalar_prefetch=1,
+            grid=(1,),
+            in_specs=list_specs
+            + [whole(code.shape)]
+            + [pl.BlockSpec(memory_space=pl.ANY)],
+            out_specs=[
+                whole((2 * slots, 2 * rows)),
+                whole((2 * slots, 2 * rows)),
+                whole((slots, 2 * slots)),
+                whole((slots, BACK_ROWS)),
+                whole((slots, slots - BACK_ROWS)),
+                pl.BlockSpec(memory_space=pltpu.SMEM),
+            ],
+        ),
+        out_shape=[
+            jax.ShapeDtypeStruct((2 * slots, 2 * rows), BF16),
+            jax.ShapeDtypeStruct((2 * slots, 2 * rows), BF16),
+            jax.ShapeDtypeStruct((slots, 2 * slots), BF16),
+            jax.ShapeDtypeStruct((slots, BACK_ROWS), BF16),
+            jax.ShapeDtypeStruct((slots, slots - BACK_ROWS), BF16),
+            jax.ShapeDtypeStruct((1,), jnp.int32),
+        ],
+        name="plan",
+        **params(),
+    )(facts, *lists, far_code, round_one)
+
     table = jnp.asarray(lag_table(bins, LAGS))
     mean = jnp.asarray(band_mean())
 
@@ -467,7 +538,7 @@
 
     def near_call():
         def bin_block(j, s):
-            return lax.rem(s[2] + j, steps)
+            return lax.rem(s[5] + j, steps)
 
         return pl.pallas_call(
             functools.partial(near_kernel, parts),
@@ -487,65 +558,41 @@
                     pl.BlockSpec((2, wide, LAGS), lambda j, s: (0, bin_block(j, s), 0)),
                     whole((GROUP, GROUP)),
                 ]
-                + list_specs,
+                + list_specs
+                + [
+                    pl.BlockSpec((windows, 2, tile), lambda j, s: (0, 0, bins // tile)),
+                    pl.BlockSpec(memory_space=pl.ANY),
+                ],
                 out_specs=[whole((slots, LAGS))]
-                + [pl.BlockSpec((rows, wide), lambda j, s: (0, j))] * parts,
+                + [pl.BlockSpec((rows, wide), lambda j, s: (0, j))] * parts
+                + [pl.BlockSpec(memory_space=pltpu.SMEM)],
                 scratch_shapes=[pltpu.VMEM((slots, 2 * rows), BF16)] * 2
                 + [pltpu.VMEM((2 * rows, parts * GROUP), BF16)] * NEAR_GROUPS,
             ),
             out_shape=[jax.ShapeDtypeStruct((slots, LAGS), F32)]
-            + [jax.ShapeDtypeStruct((rows, bins), BF16)] * parts,
+            + [jax.ShapeDtypeStruct((rows, bins), BF16)] * parts
+            + [jax.ShapeDtypeStruct((2,), jnp.int32)],
             name="near_pairs",
-            **params(),
+            **params(60),
         )(
-            near_info,
+            facts,
             *[flat] * parts,
             *[partner_rows] * parts,
             common,
             table,
             mean,
             *lists,
+            common,
+            cross_count,
         )
 
-    near_acc, *white = near_call()
-
-    hot_a, hot_b, spread, back_spread, rest_spread, cross_count = pl.pallas_call(
-        plan_kernel,
-        grid_spec=pltpu.PrefetchScalarGridSpec(
-            num_scalar_prefetch=1,
-            grid=(1,),
-            in_specs=list_specs
-            + [whole(code.shape)]
-            + [pl.BlockSpec((windows, 2, tile), lambda j, s: (0, 0, bins // tile))]
-            + [pl.BlockSpec(memory_space=pl.ANY)],
-            out_specs=[
-                whole((2 * slots, 2 * rows)),
-                whole((2 * slots, 2 * rows)),
-                whole((slots, 2 * slots)),
-                whole((slots, BACK_ROWS)),
-                whole((slots, slots - BACK_ROWS)),
-                pl.BlockSpec(memory_space=pltpu.SMEM),
-            ],
-        ),
-        out_shape=[
-            jax.ShapeDtypeStruct((2 * slots, 2 * rows), BF16),
-            jax.ShapeDtypeStruct((2 * slots, 2 * rows), BF16),
-            jax.ShapeDtypeStruct((slots, 2 * slots), BF16),
-            jax.ShapeDtypeStruct((slots, BACK_ROWS), BF16),
-            jax.ShapeDtypeStruct((slots, slots - BACK_ROWS), BF16),
-            jax.ShapeDtypeStruct((2,), jnp.int32),
-        ],
-        name="plan",
-        **params(),
-    )(-near_shift[None], *lists, far_code, common, near_acc)
-
-    across = (((me + 1) // 2) % 2 == 0).astype(jnp.int32)
-    info = jnp.stack([odd * (half // piece), across])
+    near_acc, *white, exceeds = near_call()
+
 
     def far_call(first, arrays, before):
         pieces = half // piece // 2
         base = 0 if first else pieces
-        choose = (lambda s, k: s[1] == k) if first else (lambda s, k: True)
+        choose = (lambda s, k: s[7] == k) if first else (lambda s, k: True)
         back_rows = () if first else (BACK_ROWS, slots - BACK_ROWS)
         return pl.pallas_call(
             functools.partial(far_kernel, parts, first),
@@ -568,22 +615,28 @@
                     for p in range(parts)
                 ]
                 + [
-                    pl.BlockSpec((windows, 2, piece), lambda j, s, n: (0, 0, s[0] + base + j)),
-                    pl.BlockSpec((2, piece, LAGS), lambda j, s, n: (0, s[0] + base + j, 0)),
+                    pl.BlockSpec((windows, 2, piece), lambda j, s, n: (0, 0, s[6] + base + j)),
+                    pl.BlockSpec((2, piece, LAGS), lambda j, s, n: (0, s[6] + base + j, 0)),
                     whole((GROUP, GROUP)),
                     whole((2 * slots, 2 * rows)),
                     whole((2 * slots, 2 * rows)),
-                    pl.BlockSpec(memory_space=pl.ANY) if first else whole((2 * slots, LAGS)),
+                    pl.BlockSpec(memory_space=pl.ANY),
                 ],
-                out_specs=[whole((2 * slots, LAGS))] + [whole((n, LAGS)) for n in back_rows],
-                scratch_shapes=[pltpu.VMEM((2 * rows, parts * GROUP), BF16)] * (piece // GROUP),
+                out_specs=[pl.BlockSpec(memory_space=pl.ANY)]
+                + [whole((n, LAGS)) for n in back_rows],
+                scratch_shapes=[
+                    pltpu.VMEM((2 * slots, LAGS), F32),
+                    pltpu.SemaphoreType.DMA((2 * slots // FAR_BLOCK,)),
+                    pltpu.SemaphoreType.DMA((2 * slots // FAR_BLOCK,)),
+                ]
+                + [pltpu.VMEM((2 * rows, parts * GROUP), BF16)] * (piece // GROUP),
             ),
             out_shape=[jax.ShapeDtypeStruct((2 * slots, LAGS), F32)]
             + [jax.ShapeDtypeStruct((n, LAGS), BF16) for n in back_rows],
             name="far_pairs",
             **params(),
         )(
-            info,
+            facts,
             cross_count,
             *white,
             *[a for a in arrays for _ in range(parts)],
@@ -641,7 +694,7 @@
         )(gathered, *spread_back)
 
     result = lax.cond(
-        cross_count[1] > 0,
+        exceeds[0] > 0,
         lambda: merge(back_spread, back, rest_spread, lax.ppermute(their_rest, "row", slow)),
         lambda: merge(back_spread, back),
     )

time: 95 us -> 94.1 us (level)
  Pallas kernels: 51.1 us -> 57.7 us
  other arithmetic: 5.97 us -> 2.31 us
  waiting for transfers between devices: 6 us -> 3 us
    pallas_call x1, Pallas kernels: 17.2 us -> 23.4 us  [near_call(): pl.pallas_call(functools.partial(near_kernel, parts), grid_spec=pltpu.Pre...]
    ppermute x1, waiting for transfers between devices: 3.4 us -> 0.03 us  [body(): far_direct = lax.ppermute(behind(chunks[0], reach), 'row', slow_of(1))]
    another operation x3 -> x0, other arithmetic: 2.4 us -> none  [the longest x1 1.15 us: body(): near_info = jnp.stack([near_shift, live_end, odd * (half // wide)])]
    unnamed x23 -> x19, local copies, waits for them, and re-layouts: 5.3 us -> 4.97 us
  transfers between devices with their start and end apart: 12 -> 12, of which waited for: 3 -> 4; matrix products, arithmetic and copies ran while one was open for 7% -> 4% of each run, Pallas kernels for 36% -> 43%
where the time goes in v4:
time: 94.1 us; the launch traced here: 93.5 us
  Pallas kernels  57.7 us (61%)
  starting transfers between devices  24.6 us (26%)
  local copies, waits for them, and re-layouts  5.66 us (6%)
  waiting for transfers between devices  3 us (3%)
  other arithmetic  2.31 us (2%)
    pallas_call x1, Pallas kernels, near_call(): pl.pallas_call(functools.partial(near_kernel, parts), grid_spec=pltpu.Pre...  23.4 us
    pallas_call x2, Pallas kernels, far_call(): pl.pallas_call(functools.partial(far_kernel, parts, first), grid_spec=plt...  16.3 us
    pallas_call x1, Pallas kernels, prepare(): pl.pallas_call(functools.partial(prepare_kernel, width, counts), grid_spe...  8.43 us
    ppermute x6, starting transfers between devices, body(): lax.ppermute(reach, 'row', [(i, i ^ k) for i in range(count)])  7.1 us
    pallas_call x1, Pallas kernels, body(): pl.pallas_call(plan_kernel, grid_spec=pltpu.PrefetchScalarGridSpec(num_sc...  5.22 us
    unnamed x19, local copies, waits for them, and re-layouts  4.97 us
    ppermute x1, starting transfers between devices, body(): far_direct = lax.ppermute(behind(chunks[0], reach), 'row', slow_of(1))  4.35 us
    ppermute x1, starting transfers between devices, body(): back = lax.ppermute(theirs, 'row', slow)  4.29 us
  transfers between devices with their start and end apart: 12, of which 4 were waited for; matrix products, arithmetic and copies ran while one was open for 4% of the time, Pallas kernels for 43%

profile of v4, /device:TPU:1, one launch (start us, length us, event | category | flops | bytes accessed | tf_op | source)
XLA Modules:
  0.0 93.5 jit_solution(9847845106900344087)
XLA Ops:
  0.0 0.7 stack.35.info_ref
  0.7 8.4 %prepare.1 = (bf16[128,16384]{1,0:T(8,128)(2,1)}, f32[2,2,4224]{2,1,0:T(2,128)}, bf16[16,128]{1,0:T(8,128)(2,1)}, bf16[128,4096]{1,0:T(8,128)(2,1)}, bf16[128,4096]{1,0:T(8,128)(2,1)}) custom-call(s32[8]{0:T(128)} %stack.35.info_ref, bf16[128,2,2,4096]{3,2,1,0:T(2,128)(2,1)} %x_ref.1, s32[4,2,128]{2,1,0:T(2,128)} %bitcast.14, s32[4,128]{1,0:T(4,128)} %refs_12_.1), custom_call_target="tpu_custom_call" | custom-call | flops 1000 | bytes 1000 | tf_op jit(solution)/shard_map/prepare/pallas_call | solution.py:396
  9.1 2.7 %collective-permute-start.3 = (f32[2,2,4224]{2,1,0:T(2,128)}, f32[2,2,4224]{2,1,0:T(2,128)S(1)}, u32[]{:S(2)}, u32[]{:S(2)}) collective-permute-start(f32[2,2,4224]{2,1,0:T(2,128)} %get-tuple-element.54), channel_id=1, source_target_pairs={{0,3},{1,2},{2,1},{3,0},{4,7},{5,6},{6,5},{7,4},{8,11},{9,10},{10,... | collective-permute-start | bytes 202760 | tf_op jit(solution)/shard_map/ppermute | solution.py:488
  11.8 0.5 collective-permute-start.1
  12.3 3.3 %collective-permute-start.4 = (bf16[16,128]{1,0:T(8,128)(2,1)}, bf16[16,128]{1,0:T(8,128)(2,1)S(1)}, u32[]{:S(2)}, u32[]{:S(2)}) collective-permute-start(bf16[16,128]{1,0:T(8,128)(2,1)} %get-tuple-element.55), channel_id=1, source_target_pairs={{1,2},{3,4},{5,6},{7,8},{9,10},{11,12},{13,14},{2,1},{4,3},{6,5},{... | collective-permute-start | bytes 12296 | tf_op jit(solution)/shard_map/ppermute | solution.py:477
  15.6 0.3 collective-permute-done.2
  15.9 1.6 %add_add_fusion.1.refs_0_ = f32[2,2,4224]{2,1,0:T(2,128)} fusion(f32[2,2,4224]{2,1,0:T(2,128)S(1)} %collective-permute-done.3, f32[2,2,4224]{2,1,0:T(2,128)S(1)} %collective-permute-done.2, f32[2,2,4224]{2,1,0:T(2,128)} %get-tuple-element.54, f32[2,2,4224]{2,1,0:T(2,128)S(1)} %collective-permute-done.1), kind=kLoop, calls=%fused_computation.1 | loop fusion | flops 50688 | bytes 337920 | tf_op jit(solution)/shard_map/add | solution.py:492
  17.4 0.6 copy-done.8
  18.0 0.8 collective-permute-start.5
  18.8 0.1 copy-done.4
  18.9 3.7 %collective-permute-start.8 = (f32[2,2,4224]{2,1,0:T(2,128)S(1)}, f32[2,2,4224]{2,1,0:T(2,128)S(1)}, u32[]{:S(2)}, u32[]{:S(2)}) collective-permute-start(f32[2,2,4224]{2,1,0:T(2,128)S(1)} %copy-done.4), channel_id=1, source_target_pairs={{0,12},{1,13},{2,14},{3,15},{4,8},{5,9},{6,10},{7,11},{8,4},{9,5},... | collective-permute-start | bytes 202760 | tf_op jit(solution)/shard_map/ppermute | solution.py:488
  22.6 0.3 collective-permute-start.6
  22.9 1.0 %copy.17.refs_0_ = bf16[128,4096]{1,0:T(8,128)(2,1)} copy(bf16[128,4096]{1,0:T(8,128)(2,1)S(1)} %copy-done.3) | data formatting | bytes 2097152
  23.9 4.3 %collective-permute-start.10 = (bf16[128,4096]{1,0:T(8,128)(2,1)}, bf16[128,4096]{1,0:T(8,128)(2,1)S(1)}, u32[]{:S(2)}, u32[]{:S(2)}) collective-permute-start(bf16[128,4096]{1,0:T(8,128)(2,1)} %behind.8), channel_id=1, source_target_pairs={{1,2},{5,6},{9,10},{13,14},{2,1},{6,5},{10,9},{14,13},{17,18},{21,... | collective-permute-start | bytes 3145736 | tf_op jit(solution)/shard_map/ppermute | solution.py:495
  28.2 0.2 collective-permute-done.7
  28.4 0.7 broadcast_multiply_fusion
  29.2 0.7 collective-permute-start.11
  29.9 4.1 %collective-permute-start.9 = (bf16[128,4096]{1,0:T(8,128)(2,1)}, bf16[128,4096]{1,0:T(8,128)(2,1)S(1)}, u32[]{:S(2)}, u32[]{:S(2)}) collective-permute-start(bf16[128,4096]{1,0:T(8,128)(2,1)} %behind.7), channel_id=1, source_target_pairs={{1,2},{3,4},{5,6},{7,8},{9,10},{11,12},{13,14},{2,1},{4,3},{6,5},{... | collective-permute-start | bytes 3145736 | tf_op jit(solution)/shard_map/ppermute | solution.py:501
  34.1 5.2 %plan.1 = (bf16[1024,256]{1,0:T(8,128)(2,1)}, bf16[1024,256]{1,0:T(8,128)(2,1)}, bf16[512,1024]{1,0:T(8,128)(2,1)}, bf16[512,160]{1,0:T(8,128)(2,1)S(1)}, bf16[512,352]{1,0:T(8,128)(2,1)S(1)}, /*index=5*/s32[1]{0:T(128)}) custom-call(s32[8]{0:T(128)} %stack.35.info_ref, s32[4,2,128]{2,1,0:T(2,128)} %bitcast.15, s32[4,128]{1,0:T(4,128)} %refs_12_.1, ...), custom_call_target="tpu_custom_call" | custom-call | flops 1000 | bytes 1000 | tf_op jit(solution)/shard_map/plan/pallas_call | solution.py:505
  39.3 23.4 %near_pairs.1 = (f32[512,512]{1,0:T(8,128)}, bf16[128,4096]{1,0:T(8,128)(2,1)}, bf16[128,4096]{1,0:T(8,128)(2,1)}, bf16[128,4096]{1,0:T(8,128)(2,1)}, bf16[128,4096]{1,0:T(8,128)(2,1)}, /*index=5*/s32[2]{0:T(128)}) custom-call(s32[8]{0:T(128)} %stack.35.info_ref, bf16[128,16384]{1,0:T(8,128)(2,1)} %behind.6.refs_0_.refs_1_.refs_2_.refs_3_, ...), custom_call_target="tpu_custom_call" | custom-call | flops 1000 | bytes 1000 | tf_op jit(solution)/shard_map/near_pairs/pallas_call | solution.py:543
  62.7 1.0 %copy-done = bf16[128,4096]{1,0:T(8,128)(2,1)} copy-done((bf16[128,4096]{1,0:T(8,128)(2,1)}, bf16[128,4096]{1,0:T(8,128)(2,1)S(1)}, u32[]{:S(2)}) %copy-start) | copy-done | bytes 1048600
  63.7 0.4 copy-done.1
  64.1 8.1 %far_pairs.2.refs_13_ = f32[1024,512]{1,0:T(8,128)} custom-call(s32[8]{0:T(128)} %stack.35.info_ref, s32[1]{0:T(128)} %get-tuple-element.56.refs_14_.count_ref, bf16[128,4096]{1,0:T(8,128)(2,1)} %get-tuple-element.60.refs_0_, bf16[128,4096]{1,0:T(8,128)(2,1)} %get-tuple-element.61.refs_1_, bf16[128,4096]{1,0:T(8,128)(2,1)} %get-tuple-element.62.refs_2_, ...), custom_call_target="tpu_custom_call" | custom-call | flops 1000 | bytes 1000 | tf_op jit(solution)/shard_map/far_pairs/pallas_call | solution.py:597
  72.1 1.8 %collective-permute-done.9.refs_4_.refs_5_.refs_6_.refs_7_ = bf16[128,4096]{1,0:T(8,128)(2,1)S(1)} collective-permute-done((bf16[128,4096]{1,0:T(8,128)(2,1)}, bf16[128,4096]{1,0:T(8,128)(2,1)S(1)}, u32[]{:S(2)}, u32[]{:S(2)}) %collective-permute-start.9) | collective-permute-done | bytes 1048608 | tf_op jit(solution)/shard_map/ppermute | solution.py:501
  74.0 1.0 %copy-done.2 = bf16[128,4096]{1,0:T(8,128)(2,1)} copy-done((bf16[128,4096]{1,0:T(8,128)(2,1)}, bf16[128,4096]{1,0:T(8,128)(2,1)S(1)}, u32[]{:S(2)}) %copy-start.2) | copy-done | bytes 1048600
  74.9 8.2 %far_pairs.3 = (f32[1024,512]{1,0:T(8,128)}, bf16[160,512]{1,0:T(8,128)(2,1)}, bf16[352,512]{1,0:T(8,128)(2,1)S(1)}) custom-call(s32[8]{0:T(128)} %stack.35.info_ref, s32[1]{0:T(128)} %get-tuple-element.56.refs_14_.count_ref, bf16[128,4096]{1,0:T(8,128)(2,1)} %get-tuple-element.60.refs_0_, bf16[128,4096]{1,0:T(8,128)(2,1)} %get-tuple-element.61.refs_1_, ...), custom_call_target="tpu_custom_call" | custom-call | flops 1000 | bytes 1000 | tf_op jit(solution)/shard_map/far_pairs/pallas_call | solution.py:597
  83.2 4.3 %collective-permute-start.12 = (bf16[160,512]{1,0:T(8,128)(2,1)}, bf16[160,512]{1,0:T(8,128)(2,1)S(1)}, u32[]{:S(2)}, u32[]{:S(2)}) collective-permute-start(bf16[160,512]{1,0:T(8,128)(2,1)} %get-tuple-element.70), channel_id=1, source_target_pairs={{1,2},{3,4},{5,6},{7,8},{9,10},{11,12},{13,14},{2,1},{4,3},{6,5},{... | collective-permute-start | bytes 491528 | tf_op jit(solution)/shard_map/ppermute | solution.py:655
  87.4 3.6 %gather.1 = f32[512,512]{1,0:T(8,128)S(1)} custom-call(s32[1]{0:T(128)} %get-tuple-element.56.refs_14_.count_ref, f32[512,512]{1,0:T(8,128)} %get-tuple-element.58.refs_17_.near_ref, bf16[512,1024]{1,0:T(8,128)(2,1)} %get-tuple-element.59.spread_ref, f32[1024,512]{1,0:T(8,128)} %get-tuple-element.68.far_ref), custom_call_target="tpu_custom_call" | custom-call | flops 1000 | bytes 1000 | tf_op jit(solution)/shard_map/gather/pallas_call | solution.py:656
  91.1 0.6 collective-permute-done.12
  91.8 0.7 conditional.1
  91.8 0.7 merge.2
  92.5 1.0 %copy-done.6 = f32[4,128,512]{2,1,0:T(8,128)} copy-done((f32[4,128,512]{2,1,0:T(8,128)}, f32[4,128,512]{2,1,0:T(8,128)S(1)}, u32[]{:S(2)}) %copy-start.6) | copy-done | bytes 1048600
  (27 shorter events, 0.1 us)
Async XLA Ops:
  9.1 6.4 %collective-permute-start.3 = (f32[2,2,4224]{2,1,0:T(2,128)}, f32[2,2,4224]{2,1,0:T(2,128)S(1)}, u32[]{:S(2)}, u32[]{:S(2)}) collective-permute-start(f32[2,2,4224]{2,1,0:T(2,128)} %get-tuple-element.54), channel_id=1, source_target_pairs={{0,3},{1,2},{2,1},{3,0},{4,7},{5,6},{6,5},{7,4},{8,11},{9,10},{10,... | collective-permute-start | bytes 202760 | tf_op jit(solution)/shard_map/ppermute | solution.py:488
  11.8 4.1 %collective-permute-start.2 = (f32[2,2,4224]{2,1,0:T(2,128)}, f32[2,2,4224]{2,1,0:T(2,128)S(1)}, u32[]{:S(2)}, u32[]{:S(2)}) collective-permute-start(f32[2,2,4224]{2,1,0:T(2,128)} %get-tuple-element.54), channel_id=1, source_target_pairs={{0,2},{1,3},{2,0},{3,1},{4,6},{5,7},{6,4},{7,5},{8,10},{9,11},{10,... | collective-permute-start | bytes 202760 | tf_op jit(solution)/shard_map/ppermute | solution.py:488
  11.8 4.1 %collective-permute-start.1 = (f32[2,2,4224]{2,1,0:T(2,128)}, f32[2,2,4224]{2,1,0:T(2,128)S(1)}, u32[]{:S(2)}, u32[]{:S(2)}) collective-permute-start(f32[2,2,4224]{2,1,0:T(2,128)} %get-tuple-element.54), channel_id=1, source_target_pairs={{0,1},{1,0},{2,3},{3,2},{4,5},{5,4},{6,7},{7,6},{8,9},{9,8},{10,11... | collective-permute-start | bytes 202760 | tf_op jit(solution)/shard_map/ppermute | solution.py:488
  12.3 5.2 %collective-permute-start.4 = (bf16[16,128]{1,0:T(8,128)(2,1)}, bf16[16,128]{1,0:T(8,128)(2,1)S(1)}, u32[]{:S(2)}, u32[]{:S(2)}) collective-permute-start(bf16[16,128]{1,0:T(8,128)(2,1)} %get-tuple-element.55), channel_id=1, source_target_pairs={{1,2},{3,4},{5,6},{7,8},{9,10},{11,12},{13,14},{2,1},{4,3},{6,5},{... | collective-permute-start | bytes 12296 | tf_op jit(solution)/shard_map/ppermute | solution.py:477
  17.4 0.6 copy-start.8
  18.0 0.9 copy-start.4
  18.0 4.8 %copy-start.3 = (bf16[128,4096]{1,0:T(8,128)(2,1)S(1)}, bf16[128,4096]{1,0:T(8,128)(2,1)}, u32[]{:S(2)}) copy-start(bf16[128,4096]{1,0:T(8,128)(2,1)} %get-tuple-element.67.refs_0_) | copy-start | bytes 3145732
  18.0 10.4 %copy-start.5 = (f32[2,2,4224]{2,1,0:T(2,128)S(1)}, f32[2,2,4224]{2,1,0:T(2,128)}, u32[]{:S(2)}) copy-start(f32[2,2,4224]{2,1,0:T(2,128)} %behind.5.refs_1_._) | copy-start | bytes 202756
  18.0 21.3 %collective-permute-start.5 = (bf16[128,16384]{1,0:T(8,128)(2,1)}, bf16[128,16384]{1,0:T(8,128)(2,1)}, u32[]{:S(2)}, u32[]{:S(2)}) collective-permute-start(bf16[128,16384]{1,0:T(8,128)(2,1)} %behind.6.refs_0_.refs_1_.refs_2_.refs_3_), channel_id=1, source_target_pairs={{0,1},{1,0},{2,3},{3,2},{4,5},{5,4},{6,7},{7,6},{8,9},{9,8},{10,11... | collective-permute-start | bytes 12582920 | tf_op jit(solution)/shard_map/ppermute | solution.py:497
  18.9 9.3 %collective-permute-start.8 = (f32[2,2,4224]{2,1,0:T(2,128)S(1)}, f32[2,2,4224]{2,1,0:T(2,128)S(1)}, u32[]{:S(2)}, u32[]{:S(2)}) collective-permute-start(f32[2,2,4224]{2,1,0:T(2,128)S(1)} %copy-done.4), channel_id=1, source_target_pairs={{0,12},{1,13},{2,14},{3,15},{4,8},{5,9},{6,10},{7,11},{8,4},{9,5},... | collective-permute-start | bytes 202760 | tf_op jit(solution)/shard_map/ppermute | solution.py:488
  22.6 5.9 %collective-permute-start.7 = (f32[2,2,4224]{2,1,0:T(2,128)S(1)}, f32[2,2,4224]{2,1,0:T(2,128)S(1)}, u32[]{:S(2)}, u32[]{:S(2)}) collective-permute-start(f32[2,2,4224]{2,1,0:T(2,128)S(1)} %copy-done.4), channel_id=1, source_target_pairs={{0,8},{1,9},{2,10},{3,11},{4,12},{5,13},{6,14},{7,15},{8,0},{9,1},... | collective-permute-start | bytes 202760 | tf_op jit(solution)/shard_map/ppermute | solution.py:488
  22.6 5.9 %collective-permute-start.6 = (f32[2,2,4224]{2,1,0:T(2,128)S(1)}, f32[2,2,4224]{2,1,0:T(2,128)S(1)}, u32[]{:S(2)}, u32[]{:S(2)}) collective-permute-start(f32[2,2,4224]{2,1,0:T(2,128)S(1)} %copy-done.4), channel_id=1, source_target_pairs={{0,4},{1,5},{2,6},{3,7},{4,0},{5,1},{6,2},{7,3},{8,12},{9,13},{10,... | collective-permute-start | bytes 202760 | tf_op jit(solution)/shard_map/ppermute | solution.py:488
  23.9 38.9 %collective-permute-start.10 = (bf16[128,4096]{1,0:T(8,128)(2,1)}, bf16[128,4096]{1,0:T(8,128)(2,1)S(1)}, u32[]{:S(2)}, u32[]{:S(2)}) collective-permute-start(bf16[128,4096]{1,0:T(8,128)(2,1)} %behind.8), channel_id=1, source_target_pairs={{1,2},{5,6},{9,10},{13,14},{2,1},{6,5},{10,9},{14,13},{17,18},{21,... | collective-permute-start | bytes 3145736 | tf_op jit(solution)/shard_map/ppermute | solution.py:495
  29.2 33.5 %collective-permute-start.11 = (bf16[128,4096]{1,0:T(8,128)(2,1)}, bf16[128,4096]{1,0:T(8,128)(2,1)S(1)}, u32[]{:S(2)}, u32[]{:S(2)}) collective-permute-start(bf16[128,4096]{1,0:T(8,128)(2,1)} %behind.9), channel_id=1, source_target_pairs={{3,4},{7,8},{11,12},{4,3},{8,7},{12,11},{19,20},{23,24},{27,28},{2... | collective-permute-start | bytes 3145736 | tf_op jit(solution)/shard_map/ppermute | solution.py:500
  29.9 44.0 %collective-permute-start.9 = (bf16[128,4096]{1,0:T(8,128)(2,1)}, bf16[128,4096]{1,0:T(8,128)(2,1)S(1)}, u32[]{:S(2)}, u32[]{:S(2)}) collective-permute-start(bf16[128,4096]{1,0:T(8,128)(2,1)} %behind.7), channel_id=1, source_target_pairs={{1,2},{3,4},{5,6},{7,8},{9,10},{11,12},{13,14},{2,1},{4,3},{6,5},{... | collective-permute-start | bytes 3145736 | tf_op jit(solution)/shard_map/ppermute | solution.py:501
  62.7 1.0 %copy-start = (bf16[128,4096]{1,0:T(8,128)(2,1)}, bf16[128,4096]{1,0:T(8,128)(2,1)S(1)}, u32[]{:S(2)}) copy-start(bf16[128,4096]{1,0:T(8,128)(2,1)S(1)} %collective-permute-done.10.refs_4_.refs_5_.refs_6_.refs_7_) | copy-start | bytes 3145732
  62.7 1.3 %copy-start.1 = (bf16[128,4096]{1,0:T(8,128)(2,1)}, bf16[128,4096]{1,0:T(8,128)(2,1)S(1)}, u32[]{:S(2)}) copy-start(bf16[128,4096]{1,0:T(8,128)(2,1)S(1)} %collective-permute-done.11.refs_8_.refs_9_.refs_10_.refs_11_) | copy-start | bytes 3145732
  74.0 1.0 %copy-start.2 = (bf16[128,4096]{1,0:T(8,128)(2,1)}, bf16[128,4096]{1,0:T(8,128)(2,1)S(1)}, u32[]{:S(2)}) copy-start(bf16[128,4096]{1,0:T(8,128)(2,1)S(1)} %collective-permute-done.9.refs_4_.refs_5_.refs_6_.refs_7_) | copy-start | bytes 3145732
  83.1 8.0 %copy-start.9 = (s32[2]{0:T(128)S(1)}, s32[2]{0:T(128)}, u32[]{:S(2)}) copy-start(s32[2]{0:T(128)} %get-tuple-element.57) | copy-start | bytes 28
  83.2 8.6 %collective-permute-start.12 = (bf16[160,512]{1,0:T(8,128)(2,1)}, bf16[160,512]{1,0:T(8,128)(2,1)S(1)}, u32[]{:S(2)}, u32[]{:S(2)}) collective-permute-start(bf16[160,512]{1,0:T(8,128)(2,1)} %get-tuple-element.70), channel_id=1, source_target_pairs={{1,2},{3,4},{5,6},{7,8},{9,10},{11,12},{13,14},{2,1},{4,3},{6,5},{... | collective-permute-start | bytes 491528 | tf_op jit(solution)/shard_map/ppermute | solution.py:655
  92.5 1.0 %copy-start.6 = (f32[4,128,512]{2,1,0:T(8,128)}, f32[4,128,512]{2,1,0:T(8,128)S(1)}, u32[]{:S(2)}) copy-start(f32[4,128,512]{2,1,0:T(8,128)S(1)} %get-tuple-element.88) | copy-start | bytes 3145732

commit v5 on v4

--- a/solution.py
+++ b/solution.py
@@ -15,7 +15,7 @@
 NEAR_GROUPS = 4
 FAR_BLOCK = 256
 BACK_ROWS = 160
-ROW_BLOCK = 16
+ROW_BLOCK = 32
 TINY = 1e-37
 F32 = jnp.float32
 BF16 = jnp.bfloat16
@@ -337,13 +337,14 @@
         total_ref[:, :, pl.ds(0, bins)] += total
 
     done = 0
-    for pieces, ref in zip(counts, sent):
+    for pieces, ref in zip(counts, sent[1:]):
         for part in range(parts):
             start = part * bins + done * width + info_ref[0]
             ref[:, pl.ds(part * pieces * width, pieces * width)] = flat_ref[
                 :, pl.ds(pl.multiple_of(start, width), pieces * width)
             ]
         done += pieces
+    sent[0][...] = sent[1][...]
 
 
 def gather_kernel(scale, count_ref, near_ref, spread_ref, far_ref, o_ref, held, sem):
@@ -390,7 +391,7 @@
     rows, windows, two, bins = spectra.shape
     parts = windows * two
     code_rows = -(-3 * live.shape[0] // 16) * 16
-    lanes = [parts * bins] + [parts * pieces * width for pieces in counts]
+    lanes = [parts * bins] + [parts * pieces * width for pieces in counts[:1] + counts]
     blocks = [pl.BlockSpec((ROW_BLOCK, n), lambda i, s: (i, 0)) for n in lanes]
     shapes = [jax.ShapeDtypeStruct((rows, n), BF16) for n in lanes]
     return pl.pallas_call(
@@ -497,8 +498,8 @@
                 partner_rows = lax.ppermute(flat, "row", fast)
             jump *= 4
     common = reach / (rows * count)
-    far_across = lax.ppermute(behind(chunks[0], reach), "row", slow_of(3))
-    far_second = lax.ppermute(behind(chunks[1], reach), "row", slow)
+    far_across = lax.ppermute(behind(chunks[1], reach), "row", slow_of(3))
+    far_second = lax.ppermute(behind(chunks[2], reach), "row", slow)
 
     lists = (pairs, pair_live)
     list_specs = [whole(pairs.shape), whole(pair_live.shape)]

time: 94.1 us -> 91.6 us (0.973)
  local copies, waits for them, and re-layouts: 5.66 us -> 4.64 us
    pallas_call x1, Pallas kernels: 8.43 us -> 7.08 us  [prepare(): pl.pallas_call(functools.partial(prepare_kernel, width, counts), grid_spe...]
    ppermute x2, waiting for transfers between devices: 1.84 us -> 0.5 us  [the longest x1 0.49 us: body(): far_second = lax.ppermute(behind(chunks[2], reach), 'row', slow)]
    ppermute x6, waiting for transfers between devices: 0.51 us -> 1.51 us  [body(): lax.ppermute(reach, 'row', [(i, i ^ k) for i in range(count)])]
    unnamed x19 -> x16, local copies, waits for them, and re-layouts: 4.97 us -> 4.02 us
  transfers between devices with their start and end apart: 12 -> 12, of which waited for: 4 -> 4; matrix products, arithmetic and copies ran while one was open for 4% -> 3% of each run, Pallas kernels for 43% -> 45%
where the time goes in v5:
time: 91.6 us; the launch traced here: 91.1 us
  Pallas kernels  57 us (62%)
  starting transfers between devices  24.5 us (27%)
  local copies, waits for them, and re-layouts  4.64 us (5%)
  waiting for transfers between devices  2.49 us (3%)
  other arithmetic  2.28 us (2%)
    pallas_call x1, Pallas kernels, near_call(): pl.pallas_call(functools.partial(near_kernel, parts), grid_spec=pltpu.Pre...  23.6 us
    pallas_call x2, Pallas kernels, far_call(): pl.pallas_call(functools.partial(far_kernel, parts, first), grid_spec=plt...  16.5 us
    pallas_call x1, Pallas kernels, prepare(): pl.pallas_call(functools.partial(prepare_kernel, width, counts), grid_spe...  7.08 us
    ppermute x6, starting transfers between devices, body(): lax.ppermute(reach, 'row', [(i, i ^ k) for i in range(count)])  7.06 us
    pallas_call x1, Pallas kernels, body(): pl.pallas_call(plan_kernel, grid_spec=pltpu.PrefetchScalarGridSpec(num_sc...  5.22 us
    ppermute x1, starting transfers between devices, body(): far_direct = lax.ppermute(behind(chunks[0], reach), 'row', slow_of(1))  4.35 us
    ppermute x1, starting transfers between devices, body(): back = lax.ppermute(theirs, 'row', slow)  4.27 us
    ppermute x1, starting transfers between devices, body(): far_second = lax.ppermute(behind(chunks[2], reach), 'row', slow)  4.13 us
  transfers between devices with their start and end apart: 12, of which 4 were waited for; matrix products, arithmetic and copies ran while one was open for 3% of the time, Pallas kernels for 45%

profile of v5, /device:TPU:1, one launch (start us, length us, event | category | flops | bytes accessed | tf_op | source)
XLA Modules:
  0.0 91.1 jit_solution(7617439783233794568)
XLA Ops:
  0.0 0.6 stack.35.info_ref
  0.6 7.1 %prepare.1 = (bf16[128,16384]{1,0:T(8,128)(2,1)}, f32[2,2,4224]{2,1,0:T(2,128)}, bf16[16,128]{1,0:T(8,128)(2,1)}, bf16[128,4096]{1,0:T(8,128)(2,1)}, bf16[128,40...) custom-call(s32[8]{0:T(128)} %stack.35.info_ref, bf16[128,2,2,4096]{3,2,1,0:T(2,128)(2,1)} %x_ref.1, s32[4,2,128]{2,1,0:T(2,128)} %bitcast.14, ...), custom_call_target="tpu_custom_call" | custom-call | flops 1000 | bytes 1000 | tf_op jit(solution)/shard_map/prepare/pallas_call | solution.py:397
  7.7 2.6 %collective-permute-start.3 = (f32[2,2,4224]{2,1,0:T(2,128)}, f32[2,2,4224]{2,1,0:T(2,128)S(1)}, u32[]{:S(2)}, u32[]{:S(2)}) collective-permute-start(f32[2,2,4224]{2,1,0:T(2,128)} %get-tuple-element.55), channel_id=1, source_target_pairs={{0,3},{1,2},{2,1},{3,0},{4,7},{5,6},{6,5},{7,4},{8,11},{9,10},{10,... | collective-permute-start | bytes 202760 | tf_op jit(solution)/shard_map/ppermute | solution.py:489
  10.3 0.5 collective-permute-start.1
  10.8 3.3 %collective-permute-start.4 = (bf16[16,128]{1,0:T(8,128)(2,1)}, bf16[16,128]{1,0:T(8,128)(2,1)S(1)}, u32[]{:S(2)}, u32[]{:S(2)}) collective-permute-start(bf16[16,128]{1,0:T(8,128)(2,1)} %get-tuple-element.56), channel_id=1, source_target_pairs={{1,2},{3,4},{5,6},{7,8},{9,10},{11,12},{13,14},{2,1},{4,3},{6,5},{... | collective-permute-start | bytes 12296 | tf_op jit(solution)/shard_map/ppermute | solution.py:478
  14.1 0.3 collective-permute-done.2
  14.4 1.6 %add_add_fusion.1.refs_0_ = f32[2,2,4224]{2,1,0:T(2,128)} fusion(f32[2,2,4224]{2,1,0:T(2,128)S(1)} %collective-permute-done.3, f32[2,2,4224]{2,1,0:T(2,128)S(1)} %collective-permute-done.2, f32[2,2,4224]{2,1,0:T(2,128)} %get-tuple-element.55, f32[2,2,4224]{2,1,0:T(2,128)S(1)} %collective-permute-done.1), kind=kLoop, calls=%fused_computation.1 | loop fusion | flops 50688 | bytes 337920 | tf_op jit(solution)/shard_map/add | solution.py:493
  16.0 0.6 copy-done.7
  16.6 0.7 collective-permute-start.5
  17.3 0.2 copy-done.3
  17.4 3.7 %collective-permute-start.8 = (f32[2,2,4224]{2,1,0:T(2,128)S(1)}, f32[2,2,4224]{2,1,0:T(2,128)S(1)}, u32[]{:S(2)}, u32[]{:S(2)}) collective-permute-start(f32[2,2,4224]{2,1,0:T(2,128)S(1)} %copy-done.3), channel_id=1, source_target_pairs={{0,12},{1,13},{2,14},{3,15},{4,8},{5,9},{6,10},{7,11},{8,4},{9,5},... | collective-permute-start | bytes 202760 | tf_op jit(solution)/shard_map/ppermute | solution.py:489
  21.1 0.3 collective-permute-start.6
  21.4 4.3 %collective-permute-start.10 = (bf16[128,4096]{1,0:T(8,128)(2,1)}, bf16[128,4096]{1,0:T(8,128)(2,1)S(1)}, u32[]{:S(2)}, u32[]{:S(2)}) collective-permute-start(bf16[128,4096]{1,0:T(8,128)(2,1)} %behind.8), channel_id=1, source_target_pairs={{1,2},{5,6},{9,10},{13,14},{2,1},{6,5},{10,9},{14,13},{17,18},{21,... | collective-permute-start | bytes 3145736 | tf_op jit(solution)/shard_map/ppermute | solution.py:496
  25.8 1.2 %collective-permute-done.7 = f32[2,2,4224]{2,1,0:T(2,128)S(1)} collective-permute-done((f32[2,2,4224]{2,1,0:T(2,128)S(1)}, f32[2,2,4224]{2,1,0:T(2,128)S(1)}, u32[]{:S(2)}, u32[]{:S(2)}) %collective-permute-start.7) | collective-permute-done | bytes 67616 | tf_op jit(solution)/shard_map/ppermute | solution.py:489
  27.0 0.7 broadcast_multiply_fusion
  27.7 0.7 collective-permute-start.11
  28.4 4.1 %collective-permute-start.9 = (bf16[128,4096]{1,0:T(8,128)(2,1)}, bf16[128,4096]{1,0:T(8,128)(2,1)S(1)}, u32[]{:S(2)}, u32[]{:S(2)}) collective-permute-start(bf16[128,4096]{1,0:T(8,128)(2,1)} %behind.7), channel_id=1, source_target_pairs={{1,2},{3,4},{5,6},{7,8},{9,10},{11,12},{13,14},{2,1},{4,3},{6,5},{... | collective-permute-start | bytes 3145736 | tf_op jit(solution)/shard_map/ppermute | solution.py:502
  32.6 5.2 %plan.1 = (bf16[1024,256]{1,0:T(8,128)(2,1)}, bf16[1024,256]{1,0:T(8,128)(2,1)}, bf16[512,1024]{1,0:T(8,128)(2,1)}, bf16[512,160]{1,0:T(8,128)(2,1)S(1)}, bf16[512,352]{1,0:T(8,128)(2,1)S(1)}, /*index=5*/s32[1]{0:T(128)}) custom-call(s32[8]{0:T(128)} %stack.35.info_ref, s32[4,2,128]{2,1,0:T(2,128)} %bitcast.15, s32[4,128]{1,0:T(4,128)} %refs_12_.1, ...), custom_call_target="tpu_custom_call" | custom-call | flops 1000 | bytes 1000 | tf_op jit(solution)/shard_map/plan/pallas_call | solution.py:506
  37.8 23.6 %near_pairs.1 = (f32[512,512]{1,0:T(8,128)}, bf16[128,4096]{1,0:T(8,128)(2,1)}, bf16[128,4096]{1,0:T(8,128)(2,1)}, bf16[128,4096]{1,0:T(8,128)(2,1)}, bf16[128,4096]{1,0:T(8,128)(2,1)}, /*index=5*/s32[2]{0:T(128)}) custom-call(s32[8]{0:T(128)} %stack.35.info_ref, bf16[128,16384]{1,0:T(8,128)(2,1)} %behind.6.refs_0_.refs_1_.refs_2_.refs_3_, ...), custom_call_target="tpu_custom_call" | custom-call | flops 1000 | bytes 1000 | tf_op jit(solution)/shard_map/near_pairs/pallas_call | solution.py:544
  61.5 0.9 %copy-done = bf16[128,4096]{1,0:T(8,128)(2,1)} copy-done((bf16[128,4096]{1,0:T(8,128)(2,1)}, bf16[128,4096]{1,0:T(8,128)(2,1)S(1)}, u32[]{:S(2)}) %copy-start) | copy-done | bytes 1048600
  62.4 0.4 copy-done.1
  62.8 8.2 %far_pairs.2.refs_13_ = f32[1024,512]{1,0:T(8,128)} custom-call(s32[8]{0:T(128)} %stack.35.info_ref, s32[1]{0:T(128)} %get-tuple-element.57.refs_14_.count_ref, bf16[128,4096]{1,0:T(8,128)(2,1)} %get-tuple-element.61.refs_0_, bf16[128,4096]{1,0:T(8,128)(2,1)} %get-tuple-element.62.refs_1_, bf16[128,4096]{1,0:T(8,128)(2,1)} %get-tuple-element.63.refs_2_, ...), custom_call_target="tpu_custom_call" | custom-call | flops 1000 | bytes 1000 | tf_op jit(solution)/shard_map/far_pairs/pallas_call | solution.py:598
  71.0 0.5 collective-permute-done.9.refs_4_.refs_5_.refs_6_.refs_7_
  71.5 1.0 %copy-done.2 = bf16[128,4096]{1,0:T(8,128)(2,1)} copy-done((bf16[128,4096]{1,0:T(8,128)(2,1)}, bf16[128,4096]{1,0:T(8,128)(2,1)S(1)}, u32[]{:S(2)}) %copy-start.2) | copy-done | bytes 1048600
  72.5 8.3 %far_pairs.3 = (f32[1024,512]{1,0:T(8,128)}, bf16[160,512]{1,0:T(8,128)(2,1)}, bf16[352,512]{1,0:T(8,128)(2,1)S(1)}) custom-call(s32[8]{0:T(128)} %stack.35.info_ref, s32[1]{0:T(128)} %get-tuple-element.57.refs_14_.count_ref, bf16[128,4096]{1,0:T(8,128)(2,1)} %get-tuple-element.61.refs_0_, bf16[128,4096]{1,0:T(8,128)(2,1)} %get-tuple-element.62.refs_1_, ...), custom_call_target="tpu_custom_call" | custom-call | flops 1000 | bytes 1000 | tf_op jit(solution)/shard_map/far_pairs/pallas_call | solution.py:598
  80.8 4.3 %collective-permute-start.12 = (bf16[160,512]{1,0:T(8,128)(2,1)}, bf16[160,512]{1,0:T(8,128)(2,1)S(1)}, u32[]{:S(2)}, u32[]{:S(2)}) collective-permute-start(bf16[160,512]{1,0:T(8,128)(2,1)} %get-tuple-element.72), channel_id=1, source_target_pairs={{1,2},{3,4},{5,6},{7,8},{9,10},{11,12},{13,14},{2,1},{4,3},{6,5},{... | collective-permute-start | bytes 491528 | tf_op jit(solution)/shard_map/ppermute | solution.py:656
  85.1 3.8 %gather.1 = f32[512,512]{1,0:T(8,128)S(1)} custom-call(s32[1]{0:T(128)} %get-tuple-element.57.refs_14_.count_ref, f32[512,512]{1,0:T(8,128)} %get-tuple-element.59.refs_17_.near_ref, bf16[512,1024]{1,0:T(8,128)(2,1)} %get-tuple-element.60.spread_ref, f32[1024,512]{1,0:T(8,128)} %get-tuple-element.70.far_ref), custom_call_target="tpu_custom_call" | custom-call | flops 1000 | bytes 1000 | tf_op jit(solution)/shard_map/gather/pallas_call | solution.py:657
  88.9 0.5 collective-permute-done.12
  89.4 0.7 conditional.1
  89.4 0.7 merge.2
  90.2 0.0 copy-start.5
  90.2 1.0 %copy-done.5 = f32[4,128,512]{2,1,0:T(8,128)} copy-done((f32[4,128,512]{2,1,0:T(8,128)}, f32[4,128,512]{2,1,0:T(8,128)S(1)}, u32[]{:S(2)}) %copy-start.5) | copy-done | bytes 1048600
  (24 shorter events, 0.0 us)
Async XLA Ops:
  7.7 6.4 %collective-permute-start.3 = (f32[2,2,4224]{2,1,0:T(2,128)}, f32[2,2,4224]{2,1,0:T(2,128)S(1)}, u32[]{:S(2)}, u32[]{:S(2)}) collective-permute-start(f32[2,2,4224]{2,1,0:T(2,128)} %get-tuple-element.55), channel_id=1, source_target_pairs={{0,3},{1,2},{2,1},{3,0},{4,7},{5,6},{6,5},{7,4},{8,11},{9,10},{10,... | collective-permute-start | bytes 202760 | tf_op jit(solution)/shard_map/ppermute | solution.py:489
  10.3 4.1 %collective-permute-start.2 = (f32[2,2,4224]{2,1,0:T(2,128)}, f32[2,2,4224]{2,1,0:T(2,128)S(1)}, u32[]{:S(2)}, u32[]{:S(2)}) collective-permute-start(f32[2,2,4224]{2,1,0:T(2,128)} %get-tuple-element.55), channel_id=1, source_target_pairs={{0,2},{1,3},{2,0},{3,1},{4,6},{5,7},{6,4},{7,5},{8,10},{9,11},{10,... | collective-permute-start | bytes 202760 | tf_op jit(solution)/shard_map/ppermute | solution.py:489
  10.3 4.1 %collective-permute-start.1 = (f32[2,2,4224]{2,1,0:T(2,128)}, f32[2,2,4224]{2,1,0:T(2,128)S(1)}, u32[]{:S(2)}, u32[]{:S(2)}) collective-permute-start(f32[2,2,4224]{2,1,0:T(2,128)} %get-tuple-element.55), channel_id=1, source_target_pairs={{0,1},{1,0},{2,3},{3,2},{4,5},{5,4},{6,7},{7,6},{8,9},{9,8},{10,11... | collective-permute-start | bytes 202760 | tf_op jit(solution)/shard_map/ppermute | solution.py:489
  10.8 5.2 %collective-permute-start.4 = (bf16[16,128]{1,0:T(8,128)(2,1)}, bf16[16,128]{1,0:T(8,128)(2,1)S(1)}, u32[]{:S(2)}, u32[]{:S(2)}) collective-permute-start(bf16[16,128]{1,0:T(8,128)(2,1)} %get-tuple-element.56), channel_id=1, source_target_pairs={{1,2},{3,4},{5,6},{7,8},{9,10},{11,12},{13,14},{2,1},{4,3},{6,5},{... | collective-permute-start | bytes 12296 | tf_op jit(solution)/shard_map/ppermute | solution.py:478
  16.0 0.6 copy-start.7
  16.6 0.9 copy-start.3
  16.6 10.4 %copy-start.4 = (f32[2,2,4224]{2,1,0:T(2,128)S(1)}, f32[2,2,4224]{2,1,0:T(2,128)}, u32[]{:S(2)}) copy-start(f32[2,2,4224]{2,1,0:T(2,128)} %behind.5.refs_1_._) | copy-start | bytes 202756
  16.6 21.2 %collective-permute-start.5 = (bf16[128,16384]{1,0:T(8,128)(2,1)}, bf16[128,16384]{1,0:T(8,128)(2,1)}, u32[]{:S(2)}, u32[]{:S(2)}) collective-permute-start(bf16[128,16384]{1,0:T(8,128)(2,1)} %behind.6.refs_0_.refs_1_.refs_2_.refs_3_), channel_id=1, source_target_pairs={{0,1},{1,0},{2,3},{3,2},{4,5},{5,4},{6,7},{7,6},{8,9},{9,8},{10,11... | collective-permute-start | bytes 12582920 | tf_op jit(solution)/shard_map/ppermute | solution.py:498
  17.4 8.3 %collective-permute-start.8 = (f32[2,2,4224]{2,1,0:T(2,128)S(1)}, f32[2,2,4224]{2,1,0:T(2,128)S(1)}, u32[]{:S(2)}, u32[]{:S(2)}) collective-permute-start(f32[2,2,4224]{2,1,0:T(2,128)S(1)} %copy-done.3), channel_id=1, source_target_pairs={{0,12},{1,13},{2,14},{3,15},{4,8},{5,9},{6,10},{7,11},{8,4},{9,5},... | collective-permute-start | bytes 202760 | tf_op jit(solution)/shard_map/ppermute | solution.py:489
  21.1 5.9 %collective-permute-start.7 = (f32[2,2,4224]{2,1,0:T(2,128)S(1)}, f32[2,2,4224]{2,1,0:T(2,128)S(1)}, u32[]{:S(2)}, u32[]{:S(2)}) collective-permute-start(f32[2,2,4224]{2,1,0:T(2,128)S(1)} %copy-done.3), channel_id=1, source_target_pairs={{0,8},{1,9},{2,10},{3,11},{4,12},{5,13},{6,14},{7,15},{8,0},{9,1},... | collective-permute-start | bytes 202760 | tf_op jit(solution)/shard_map/ppermute | solution.py:489
  21.1 5.9 %collective-permute-start.6 = (f32[2,2,4224]{2,1,0:T(2,128)S(1)}, f32[2,2,4224]{2,1,0:T(2,128)S(1)}, u32[]{:S(2)}, u32[]{:S(2)}) collective-permute-start(f32[2,2,4224]{2,1,0:T(2,128)S(1)} %copy-done.3), channel_id=1, source_target_pairs={{0,4},{1,5},{2,6},{3,7},{4,0},{5,1},{6,2},{7,3},{8,12},{9,13},{10,... | collective-permute-start | bytes 202760 | tf_op jit(solution)/shard_map/ppermute | solution.py:489
  21.4 40.0 %collective-permute-start.10 = (bf16[128,4096]{1,0:T(8,128)(2,1)}, bf16[128,4096]{1,0:T(8,128)(2,1)S(1)}, u32[]{:S(2)}, u32[]{:S(2)}) collective-permute-start(bf16[128,4096]{1,0:T(8,128)(2,1)} %behind.8), channel_id=1, source_target_pairs={{1,2},{5,6},{9,10},{13,14},{2,1},{6,5},{10,9},{14,13},{17,18},{21,... | collective-permute-start | bytes 3145736 | tf_op jit(solution)/shard_map/ppermute | solution.py:496
  27.7 33.8 %collective-permute-start.11 = (bf16[128,4096]{1,0:T(8,128)(2,1)}, bf16[128,4096]{1,0:T(8,128)(2,1)S(1)}, u32[]{:S(2)}, u32[]{:S(2)}) collective-permute-start(bf16[128,4096]{1,0:T(8,128)(2,1)} %behind.9), channel_id=1, source_target_pairs={{3,4},{7,8},{11,12},{4,3},{8,7},{12,11},{19,20},{23,24},{27,28},{2... | collective-permute-start | bytes 3145736 | tf_op jit(solution)/shard_map/ppermute | solution.py:501
  28.4 43.1 %collective-permute-start.9 = (bf16[128,4096]{1,0:T(8,128)(2,1)}, bf16[128,4096]{1,0:T(8,128)(2,1)S(1)}, u32[]{:S(2)}, u32[]{:S(2)}) collective-permute-start(bf16[128,4096]{1,0:T(8,128)(2,1)} %behind.7), channel_id=1, source_target_pairs={{1,2},{3,4},{5,6},{7,8},{9,10},{11,12},{13,14},{2,1},{4,3},{6,5},{... | collective-permute-start | bytes 3145736 | tf_op jit(solution)/shard_map/ppermute | solution.py:502
  61.5 1.0 %copy-start = (bf16[128,4096]{1,0:T(8,128)(2,1)}, bf16[128,4096]{1,0:T(8,128)(2,1)S(1)}, u32[]{:S(2)}) copy-start(bf16[128,4096]{1,0:T(8,128)(2,1)S(1)} %collective-permute-done.10.refs_4_.refs_5_.refs_6_.refs_7_) | copy-start | bytes 3145732
  61.5 1.3 %copy-start.1 = (bf16[128,4096]{1,0:T(8,128)(2,1)}, bf16[128,4096]{1,0:T(8,128)(2,1)S(1)}, u32[]{:S(2)}) copy-start(bf16[128,4096]{1,0:T(8,128)(2,1)S(1)} %collective-permute-done.11.refs_8_.refs_9_.refs_10_.refs_11_) | copy-start | bytes 3145732
  71.5 1.0 %copy-start.2 = (bf16[128,4096]{1,0:T(8,128)(2,1)}, bf16[128,4096]{1,0:T(8,128)(2,1)S(1)}, u32[]{:S(2)}) copy-start(bf16[128,4096]{1,0:T(8,128)(2,1)S(1)} %collective-permute-done.9.refs_4_.refs_5_.refs_6_.refs_7_) | copy-start | bytes 3145732
  80.8 8.1 %copy-start.8 = (s32[2]{0:T(128)S(1)}, s32[2]{0:T(128)}, u32[]{:S(2)}) copy-start(s32[2]{0:T(128)} %get-tuple-element.58) | copy-start | bytes 28
  80.8 8.6 %collective-permute-start.12 = (bf16[160,512]{1,0:T(8,128)(2,1)}, bf16[160,512]{1,0:T(8,128)(2,1)S(1)}, u32[]{:S(2)}, u32[]{:S(2)}) collective-permute-start(bf16[160,512]{1,0:T(8,128)(2,1)} %get-tuple-element.72), channel_id=1, source_target_pairs={{1,2},{3,4},{5,6},{7,8},{9,10},{11,12},{13,14},{2,1},{4,3},{6,5},{... | collective-permute-start | bytes 491528 | tf_op jit(solution)/shard_map/ppermute | solution.py:656
  90.2 1.0 %copy-start.5 = (f32[4,128,512]{2,1,0:T(8,128)}, f32[4,128,512]{2,1,0:T(8,128)S(1)}, u32[]{:S(2)}) copy-start(f32[4,128,512]{2,1,0:T(8,128)S(1)} %get-tuple-element.90) | copy-start | bytes 3145732
